TPU v7x, 32 devices: a whole 2x2x4 slice. The times are simulated.
32 devices in a mesh: dp: 8 (over y, x, core), seq: 4 (over z).
Axes of the slice: x: 2, y: 2, z: 4, core: 2. Of those that a mesh axis runs over, the one named last changes fastest.
Arguments:
- tokens: bfloat16 [16384, 1024], P(('dp', 'seq')), may hold values from -6 to 6
- cotangent: bfloat16 [16384, 1024], P(('dp', 'seq')), may hold values from -6 to 6
- lengths: int32 [8], P('dp'), may hold values from 1537 to 2048, as said below
- proj_z: float32 [1024, 128], P('seq'), may hold values from -0.1875 to 0.1875
- proj_v: float32 [2048, 1024], P('seq'), may hold values from -0.1875 to 0.1875
- proj_gamma: float32 [2048, 1024], P('seq'), may hold values from -0.1875 to 0.1875
- proj_phi: float32 [1024, 1024], P('seq'), may hold values from -0.1875 to 0.1875
- proj_h: float32 [1024, 1024], P('seq'), may hold values from -0.1875 to 0.1875
- proj_u: float32 [2048, 1024], P('seq'), may hold values from -0.25 to 0.25
- proj_up: float32 [4096, 1024], P('seq'), may hold values from -0.1875 to 0.1875
- proj_down: float32 [4096, 1024], P('seq'), may hold values from -0.09375 to 0.09375
- moment_z: float32 [1024, 128], P('seq'), may hold values from -224 to 224
- moment_v: float32 [2048, 1024], P('seq'), may hold values from -224 to 224
- moment_gamma: float32 [2048, 1024], P('seq'), may hold values from -224 to 224
- moment_phi: float32 [1024, 1024], P('seq'), may hold values from -224 to 224
- moment_h: float32 [1024, 1024], P('seq'), may hold values from -224 to 224
- moment_u: float32 [2048, 1024], P('seq'), may hold values from -224 to 224
- moment_up: float32 [4096, 1024], P('seq'), may hold values from -224 to 224
- moment_down: float32 [4096, 1024], P('seq'), may hold values from -224 to 224
- channel_params: float32 [1024, 67], P('seq'), may hold values from -8 to 8
- channel_moment: float32 [1024, 67], P('seq'), may hold values from -768 to 768
- query_params: float32 [128, 3], P('seq'), may hold values from -4 to 4
- query_moment: float32 [128, 3], P('seq'), may hold values from -768 to 768
Outputs:
- block_output: bfloat16 [16384, 1024], P(('dp', 'seq'))
- tokens_grad: float32 [16384, 1024], P(('dp', 'seq'))
- updated_z: float32 [1024, 128], P('seq')
- updated_v: float32 [2048, 1024], P('seq')
- updated_gamma: float32 [2048, 1024], P('seq')
- updated_phi: float32 [1024, 1024], P('seq')
- updated_h: float32 [1024, 1024], P('seq')
- updated_u: float32 [2048, 1024], P('seq')
- updated_up: float32 [4096, 1024], P('seq')
- updated_down: float32 [4096, 1024], P('seq')
- momentum_z: float32 [1024, 128], P('seq')
- momentum_v: float32 [2048, 1024], P('seq')
- momentum_gamma: float32 [2048, 1024], P('seq')
- momentum_phi: float32 [1024, 1024], P('seq')
- momentum_h: float32 [1024, 1024], P('seq')
- momentum_u: float32 [2048, 1024], P('seq')
- momentum_up: float32 [4096, 1024], P('seq')
- momentum_down: float32 [4096, 1024], P('seq')
- updated_channel: float32 [1024, 67], P('seq')
- momentum_channel: float32 [1024, 67], P('seq')
- updated_query: float32 [128, 3], P('seq')
- momentum_query: float32 [128, 3], P('seq')
Inputs may be any that keep to these rules, and one draw needn't show every extreme that they name: `lengths`: one slot is full in every draw; the others end in the last 512 positions of their slot.
All inputs are finite; a program needn't handle non-finite values.
Results may differ from a plain program's by a relative error of at most 0.011.
The roundings to bfloat16 on the way count: a program that leaves them out, or rounds other values in their place, can miss the bound.
Values may be sent and summed in bfloat16 or wider, within the bound.
No kernel may reach another device: no remote copies, remote signals or barrier semaphores. Data moves between devices by JAX's collectives and lax.ppermute only.
A program may use at most 384 MiB of HBM per device.

v0:
```python
import math

import jax
import jax.numpy as jnp
from jax import lax
from jax.sharding import PartitionSpec as P

D = 1024
Z = 128
V = 2048
NE = 16
FF = 4096
EBLK = 64
NS_STEPS = 5


HIGHEST = lax.Precision.HIGHEST
POLY_A = 3.4445
POLY_B = -4.775
POLY_C = 2.0315
MOMENTUM = 0.5
MATRIX_RATE = 0.5
VECTOR_RATE = 0.2


def carried_in(value, axis, join, neutral, backward):
    count, mine = (lax.axis_size(axis), lax.axis_index(axis))
    pieces = jax.tree.map(lambda part: lax.all_gather(part, axis), value)
    if backward:
        pieces = jax.tree.map(lambda part: part[::-1], pieces)
        mine = count - 1 - mine
    running = jax.tree.map(
        lambda part, zero: jnp.full_like(part, 0) + jnp.asarray(zero, part.dtype), value, neutral
    )

    def hop(position, running):
        longer = join(running, jax.tree.map(lambda part: part[position], pieces))
        return jax.tree.map(lambda new, old: jnp.where(position < mine, new, old), longer, running)

    return lax.fori_loop(0, count - 1, hop, running)


def passed_along(block, axis, distance):
    devices = range(lax.axis_size(axis))
    route = [(i - distance, i) for i in devices if i - distance in devices]
    return lax.ppermute(block, axis, route)


def spread_2(x, axis, root):
    mine = lax.axis_index(axis) == root
    return lax.psum(jnp.where(mine, x, jnp.zeros_like(x)), axis)


def as_half(value):
    return value.astype(jnp.bfloat16)


def times_plain(left, right):
    return jnp.dot(left, right, preferred_element_type=jnp.float32)


def times_right(left, right):
    return lax.dot_general(
        left, right, (((1,), (1,)), ((), ())), preferred_element_type=jnp.float32
    )


def times_left(left, right):
    return lax.dot_general(
        left, right, (((0,), (0,)), ((), ())), preferred_element_type=jnp.float32
    )


def exact_plain(left, right):
    return jnp.dot(left, right, precision=HIGHEST, preferred_element_type=jnp.float32)


def exact_left(left, right):
    return lax.dot_general(
        left, right, (((0,), (0,)), ((), ())), precision=HIGHEST, preferred_element_type=jnp.float32
    )


def silu_grad(value):
    sig = jax.nn.sigmoid(value)
    return sig * (1.0 + value * (1.0 - sig))


def norm_rows(rows, gain):
    center = rows - jnp.mean(rows, axis=-1, keepdims=True)
    spread = jnp.mean(center * center, axis=-1, keepdims=True)
    return center * lax.rsqrt(spread + 1e-05) * gain


def ema_tables(alpha, delta, beta, eta, block):
    inject_rate = jax.nn.sigmoid(alpha)
    keep_rate = 1.0 - inject_rate * jax.nn.sigmoid(delta)
    steps = jnp.arange(block + 1).astype(jnp.float32)
    powers = jnp.exp(steps[:, None, None] * jnp.log(keep_rate)[None])
    inject = inject_rate * beta
    kernel = jnp.sum(powers[:block] * (eta * inject)[None], axis=1)
    places = jnp.arange(block)
    distance = places[:, None] - places[None, :]
    toeplitz = jnp.where((distance >= 0)[:, :, None], kernel[jnp.clip(distance, 0, block - 1)], 0.0)
    return (powers, inject, toeplitz)


def ema_run(normed, omega, alpha, delta, beta, eta, start):
    block = EBLK
    powers, inject, toeplitz = ema_tables(alpha, delta, beta, eta, block)
    later = powers[1:] * eta[None]
    tail = powers[block - 1 :: -1] * inject[None]
    last = powers[block]
    pieces = normed.reshape(normed.shape[0] // block, block, normed.shape[1])

    def one_block(state, piece):
        inner = jnp.einsum("tsc,sc->tc", toeplitz, piece, precision=HIGHEST)
        carried = jnp.einsum("tjc,jc->tc", later, state, precision=HIGHEST)
        fresh = last * state + jnp.einsum("sjc,sc->jc", tail, piece, precision=HIGHEST)
        return (fresh, inner + carried)

    final, mixed = lax.scan(jax.checkpoint(one_block), start, pieces)
    return (jax.nn.silu(mixed.reshape(normed.shape) + omega * normed), final)


def chain(earlier, later):
    return (earlier[0] * later[0], later[0] * earlier[1] + later[1])


def padded_to(item, pad_rows, pad_cols):
    return jnp.pad(item, ((0, pad_rows - item.shape[0]), (0, pad_cols - item.shape[1])))


def body(
    tokens,
    cotangent,
    lengths,
    proj_z,
    proj_v,
    proj_gamma,
    proj_phi,
    proj_h,
    proj_u,
    proj_up,
    proj_down,
    moment_z,
    moment_v,
    moment_gamma,
    moment_phi,
    moment_h,
    moment_u,
    moment_up,
    moment_down,
    channel_params,
    channel_moment,
    query_params,
    query_moment,
):
    seq_count = lax.axis_size("seq")
    seq_index = lax.axis_index("seq")
    rows = tokens.shape[0]
    (
        half_z,
        half_v,
        half_gamma,
        half_phi,
        half_h,
        half_u,
        half_up,
        half_down,
        half_channel,
        half_query,
    ) = (
        lax.all_gather(as_half(proj_z), "seq", axis=0, tiled=True),
        lax.all_gather(as_half(proj_v), "seq", axis=0, tiled=True),
        lax.all_gather(as_half(proj_gamma), "seq", axis=0, tiled=True),
        lax.all_gather(as_half(proj_phi), "seq", axis=0, tiled=True),
        lax.all_gather(as_half(proj_h), "seq", axis=0, tiled=True),
        lax.all_gather(as_half(proj_u), "seq", axis=0, tiled=True),
        lax.all_gather(as_half(proj_up), "seq", axis=0, tiled=True),
        lax.all_gather(as_half(proj_down), "seq", axis=0, tiled=True),
        lax.all_gather(as_half(channel_params), "seq", axis=0, tiled=True),
        lax.all_gather(as_half(query_params), "seq", axis=0, tiled=True),
    )
    channel = half_channel.astype(jnp.float32)
    query_set = half_query.astype(jnp.float32)
    gain_one = channel[:, 0]
    gain_two = channel[:, 1]
    omega = channel[:, 2]
    alpha = channel[:, 3 : 3 + NE].T
    delta = channel[:, 3 + NE : 3 + 2 * NE].T
    beta = channel[:, 3 + 2 * NE : 3 + 3 * NE].T
    eta = channel[:, 3 + 3 * NE : 3 + 4 * NE].T
    scale_q = query_set[:, 0]
    shift_q = query_set[:, 1]
    scale_k = query_set[:, 2]
    score_scale = Z ** (-0.5)
    place = seq_index * rows + jnp.arange(rows, dtype=jnp.int32)
    keep = (place < lengths[0]).astype(jnp.float32)[:, None]
    inputs = tokens.astype(jnp.float32)
    weighted = cotangent.astype(jnp.float32) * keep
    normed, norm_back_one = jax.vjp(norm_rows, inputs, gain_one)
    normed_low = as_half(normed)
    v_pre = times_right(normed_low, half_v)
    values_low = as_half(jax.nn.silu(v_pre))
    blank = jnp.zeros_like(alpha)
    ones_state = jnp.ones_like(alpha)
    decay_all = jnp.exp(rows * jnp.log(1.0 - jax.nn.sigmoid(alpha) * jax.nn.sigmoid(delta)))
    local_end = ema_run(normed, omega, alpha, delta, beta, eta, blank)[1]
    carried = carried_in((decay_all, local_end), "seq", chain, (ones_state, blank), False)
    (mixed, unused_end), mixer_back = jax.vjp(
        ema_run, normed, omega, alpha, delta, beta, eta, carried[1]
    )
    mixed_low = as_half(mixed)
    z_pre = times_plain(mixed_low, half_z)
    zed = jax.nn.silu(z_pre)
    queries_low = as_half(zed * scale_q + shift_q)
    keys_low = as_half(zed * scale_k)
    lower = passed_along((keys_low, values_low), "seq", 1)
    keys_all = jnp.concatenate([lower[0], keys_low], axis=0)
    values_all = jnp.concatenate([lower[1], values_low], axis=0)
    odd_device = seq_index % 2 == 1
    query_place = jnp.arange(rows)[:, None]
    key_place = jnp.arange(2 * rows)[None, :]
    allowed = jnp.where(key_place < rows, odd_device, key_place - rows <= query_place)
    scores = jnp.where(allowed, times_right(queries_low, keys_all) * score_scale, -1e30)
    top = jnp.max(scores, axis=-1, keepdims=True)
    expo = jnp.exp(scores - top)
    total = jnp.sum(expo, axis=-1, keepdims=True)
    attended = times_plain(as_half(expo / total), values_all)
    gam_pre = times_right(mixed_low, half_gamma)
    gamma = jax.nn.silu(gam_pre)
    gated_low = as_half(gamma * attended)
    phi = jax.nn.sigmoid(times_plain(mixed_low, half_phi))
    h_pre = times_plain(mixed_low, half_h) + times_plain(gated_low, half_u)
    cand = jax.nn.silu(h_pre)
    middle = phi * cand + (1.0 - phi) * inputs
    wide, norm_back_two = jax.vjp(norm_rows, middle, gain_two)
    wide_low = as_half(wide)
    a_pre = times_right(wide_low, half_up)
    active_low = as_half(jax.nn.silu(a_pre))
    result = middle + times_plain(active_low, half_down)
    block_output = as_half(result * keep)
    back_ffn = as_half(weighted)
    grad_down = times_left(active_low, back_ffn)
    d_apre = as_half(times_right(back_ffn, half_down) * silu_grad(a_pre))
    grad_up = times_left(d_apre, wide_low)
    d_mid_norm, d_gain_two = norm_back_two(times_plain(d_apre, half_up))
    d_middle = weighted + d_mid_norm
    d_phipre = as_half(d_middle * (cand - inputs) * phi * (1.0 - phi))
    d_hpre = as_half(d_middle * phi * silu_grad(h_pre))
    tokens_grad = d_middle * (1.0 - phi)
    grad_phi = times_left(mixed_low, d_phipre)
    grad_h = times_left(mixed_low, d_hpre)
    grad_u = times_left(gated_low, d_hpre)
    d_gated = times_right(d_hpre, half_u)
    d_attended = as_half(d_gated * gamma)
    d_gampre = as_half(d_gated * attended * silu_grad(gam_pre))
    grad_gamma = times_left(d_gampre, mixed_low)
    d_mixed = (
        times_right(d_phipre, half_phi)
        + times_right(d_hpre, half_h)
        + times_plain(d_gampre, half_gamma)
    )
    scores = jnp.where(allowed, times_right(queries_low, keys_all) * score_scale, -1e30)
    probs = jnp.exp(scores - top) / total
    d_probs = times_right(d_attended, values_all)
    d_scores = as_half(probs * (d_probs - jnp.sum(probs * d_probs, axis=-1, keepdims=True)))
    d_values_all = times_left(as_half(probs), d_attended)
    d_queries = times_plain(d_scores, keys_all) * score_scale
    d_keys_all = times_left(d_scores, queries_low) * score_scale
    upper = passed_along((d_keys_all[:rows], d_values_all[:rows]), "seq", -1)
    d_keys = d_keys_all[rows:] + upper[0]
    d_values = d_values_all[rows:] + upper[1]
    d_scale_q = jnp.sum(d_queries * zed, axis=0)
    d_shift_q = jnp.sum(d_queries, axis=0)
    d_scale_k = jnp.sum(d_keys * zed, axis=0)
    d_zpre = as_half((d_queries * scale_q + d_keys * scale_k) * silu_grad(z_pre))
    grad_z = times_left(mixed_low, d_zpre)
    d_mixed = d_mixed + times_right(d_zpre, half_z)
    d_vpre = as_half(d_values * silu_grad(v_pre))
    grad_v = times_left(d_vpre, normed_low)
    d_normed = times_plain(d_vpre, half_v)
    partial_back = mixer_back((d_mixed, blank))
    behind = carried_in((decay_all, partial_back[6]), "seq", chain, (ones_state, blank), True)
    mixer_grads = mixer_back((d_mixed, behind[1]))
    d_input_norm, d_gain_one = norm_back_one(d_normed + mixer_grads[0])
    tokens_grad = tokens_grad + d_input_norm
    grad_channel = jnp.concatenate(
        [
            d_gain_one[:, None],
            d_gain_two[:, None],
            mixer_grads[1][:, None],
            mixer_grads[2].T,
            mixer_grads[3].T,
            mixer_grads[4].T,
            mixer_grads[5].T,
        ],
        axis=1,
    )
    grad_query = jnp.stack([d_scale_q, d_shift_q, d_scale_k], axis=1)
    masters = [proj_z, proj_v, proj_gamma, proj_phi, proj_h, proj_u, proj_up, proj_down]
    olds = [
        moment_z,
        moment_v,
        moment_gamma,
        moment_phi,
        moment_h,
        moment_u,
        moment_up,
        moment_down,
    ]
    matrix_count = len(olds)
    pad_rows = max([item.shape[0] for item in olds])
    pad_cols = max([item.shape[1] for item in olds])
    slot = jnp.minimum(lax.axis_index("dp"), matrix_count - 1)
    (
        part_z,
        part_v,
        part_gamma,
        part_phi,
        part_h,
        part_u,
        part_up,
        part_down,
        part_channel,
        part_query,
    ) = (
        lax.psum_scatter(grad_z, "seq", scatter_dimension=0, tiled=True),
        lax.psum_scatter(grad_v, "seq", scatter_dimension=0, tiled=True),
        lax.psum_scatter(grad_gamma, "seq", scatter_dimension=0, tiled=True),
        lax.psum_scatter(grad_phi, "seq", scatter_dimension=0, tiled=True),
        lax.psum_scatter(grad_h, "seq", scatter_dimension=0, tiled=True),
        lax.psum_scatter(grad_u, "seq", scatter_dimension=0, tiled=True),
        lax.psum_scatter(grad_up, "seq", scatter_dimension=0, tiled=True),
        lax.psum_scatter(grad_down, "seq", scatter_dimension=0, tiled=True),
        lax.psum_scatter(grad_channel, "seq", scatter_dimension=0, tiled=True),
        lax.psum_scatter(grad_query, "seq", scatter_dimension=0, tiled=True),
    )
    sum_z, sum_v, sum_gamma, sum_phi, sum_h, sum_u, sum_up, sum_down, sum_channel, sum_query = (
        lax.psum(
            (
                part_z,
                part_v,
                part_gamma,
                part_phi,
                part_h,
                part_u,
                part_up,
                part_down,
                part_channel,
                part_query,
            ),
            "dp",
        )
    )
    sums = [sum_z, sum_v, sum_gamma, sum_phi, sum_h, sum_u, sum_up, sum_down]
    renewed = [MOMENTUM * old + grad for old, grad in zip(olds, sums)]
    stacked = jnp.stack([padded_to(item, pad_rows, pad_cols) for item in renewed])
    owned = lax.dynamic_index_in_dim(stacked, slot, 0, keepdims=False)
    channel_renewed = MOMENTUM * channel_moment + sum_channel
    query_renewed = MOMENTUM * query_moment + sum_query
    gram_raw, channel_total, query_total = lax.psum(
        (
            exact_left(owned, owned),
            jnp.sum(channel_renewed * channel_renewed, axis=0),
            jnp.sum(query_renewed * query_renewed, axis=0),
        ),
        "seq",
    )
    scale = 1.0 / (jnp.sqrt(jnp.trace(gram_raw)) + 1e-07)
    iterate = owned * scale
    gram = gram_raw * (scale * scale)
    for step in range(NS_STEPS):
        if step > 0:
            gram = lax.psum(exact_left(iterate, iterate), "seq")
        poly = POLY_B * gram + POLY_C * exact_plain(gram, gram)
        iterate = POLY_A * iterate + exact_plain(iterate, poly)
    directions = []
    for index in range(matrix_count):
        piece = iterate[: renewed[index].shape[0], : renewed[index].shape[1]]
        directions.append(spread_2(piece, "dp", index))
    fans = [D, D, D, D, D, V, D, FF]
    updated = []
    for master, direction, fan in zip(masters, directions, fans):
        full_rows = master.shape[0] * seq_count
        updated.append(master - MATRIX_RATE * math.sqrt(full_rows / fan) * direction)
    channel_rms = jnp.sqrt(channel_total / D + 1e-06)
    channel_new = channel_params - VECTOR_RATE * channel_renewed / channel_rms
    query_rms = jnp.sqrt(query_total / Z + 1e-06)
    query_new = query_params - VECTOR_RATE * query_renewed / query_rms
    return (
        block_output,
        tokens_grad,
        updated[0],
        updated[1],
        updated[2],
        updated[3],
        updated[4],
        updated[5],
        updated[6],
        updated[7],
        renewed[0],
        renewed[1],
        renewed[2],
        renewed[3],
        renewed[4],
        renewed[5],
        renewed[6],
        renewed[7],
        channel_new,
        channel_renewed,
        query_new,
        query_renewed,
    )


def solution(mesh):
    placed = (
        P(("dp", "seq"), None),
        P(("dp", "seq"), None),
        P("dp"),
        P("seq", None),
        P("seq", None),
        P("seq", None),
        P("seq", None),
        P("seq", None),
        P("seq", None),
        P("seq", None),
        P("seq", None),
        P("seq", None),
        P("seq", None),
        P("seq", None),
        P("seq", None),
        P("seq", None),
        P("seq", None),
        P("seq", None),
        P("seq", None),
        P("seq", None),
        P("seq", None),
        P("seq", None),
        P("seq", None),
    )
    return jax.shard_map(
        body,
        mesh=mesh,
        in_specs=placed,
        out_specs=(
            P(("dp", "seq"), None),
            P(("dp", "seq"), None),
            P("seq", None),
            P("seq", None),
            P("seq", None),
            P("seq", None),
            P("seq", None),
            P("seq", None),
            P("seq", None),
            P("seq", None),
            P("seq", None),
            P("seq", None),
            P("seq", None),
            P("seq", None),
            P("seq", None),
            P("seq", None),
            P("seq", None),
            P("seq", None),
            P("seq", None),
            P("seq", None),
            P("seq", None),
            P("seq", None),
        ),
        check_vma=False,
    )
```

profile of v0, /device:TPU:0, one launch (start us, length us, event | category | flops | bytes accessed | tf_op | source)
XLA Modules:
  0.0 3736.3 jit_solution(7624590568461541445)
XLA Ops:
  24.5 17.1 all_gather.50
  43.7 17.6 all-gather
  70.7 29.6 while.94
  114.9 18.5 gather_fusion
  146.6 134.4 %while.93 = (s32[]{:T(128)}, f32[16,1024]{1,0:T(8,128)S(1)}, f32[8,64,1024]{2,1,0:T(8,128)}, f32[8,16,1024]{2,1,0:T(8,128)}, f32[16,1024]{1,0:T(8,128)S(1)}, /*i...) while((s32[]{:T(128)}, f32[16,1024]{1,0:T(8,128)S(1)}, ...), condition=%wide.region_8.9_spmd, body=%wide.region_7.8_spmd.sunk | while | flops 12533762 | bytes 28049528 | solution.py:122
  306.7 89.8 %all_gather.58 = bf16[1024,128]{1,0:T(8,128)(2,1)S(1)} all-gather(bf16[256,128]{1,0:T(8,128)(2,1)S(1)} %convert_element_type.134), channel_id=1, replica_groups=mesh['dp'=8,'seq'=4] {'seq'}, dimensions={0}, use_global_device_ids=true | all-gather | bytes 327680 | tf_op jit(solution)/shard_map/all_gather | solution.py:174
  441.3 98.8 %all-gather.22.cloned.1.call-done = bf16[4096,1024]{1,0:T(8,128)(2,1)} async-done(((bf16[1024,1024]{1,0:T(8,128)(2,1)}), bf16[4096,1024]{1,0:T(8,128)(2,1)}) %all-gather.22.cloned.1.call-update) | async-done | bytes 8388624 | tf_op jit(solution)/shard_map/all_gather | solution.py:180
  552.9 137.9 %all-gather.24.cloned.1.call-done = bf16[4096,1024]{1,0:T(8,128)(2,1)} async-done(((bf16[1024,1024]{1,0:T(8,128)(2,1)}), bf16[4096,1024]{1,0:T(8,128)(2,1)}) %all-gather.24.cloned.1.call-update) | async-done | bytes 8388624 | tf_op jit(solution)/shard_map/all_gather | solution.py:181
  769.7 180.0 %collective-permute-done.2 = f32[512,2048]{1,0:T(8,128)S(1)} collective-permute-done((f32[512,2048]{1,0:T(8,128)S(1)}, f32[512,2048]{1,0:T(8,128)S(1)}, u32[]{:S(2)}, u32[]{:S(2)}) %collective-permute-start.2) | collective-permute-done | bytes 4194336 | tf_op jit(solution)/shard_map/ppermute | solution.py:46
  994.5 147.3 %reduce-scatter.23.cloned.1.call-done = f32[512,1024]{1,0:T(8,128)} async-done(((f32[2048,1024]{1,0:T(8,128)}), f32[512,1024]{1,0:T(8,128)}) %reduce-scatter.23.cloned.1.call-update) | async-done | bytes 2097168 | tf_op jit(solution)/shard_map/reduce_scatter | solution.py:334
  1141.8 147.4 %reduce-scatter.17.cloned.1.call-done = f32[512,1024]{1,0:T(8,128)} async-done(((f32[2048,1024]{1,0:T(8,128)}), f32[512,1024]{1,0:T(8,128)}) %reduce-scatter.17.cloned.1.call-update) | async-done | bytes 2097168 | tf_op jit(solution)/shard_map/reduce_scatter | solution.py:331
  1289.3 147.6 %reduce-scatter.15.cloned.1.call-done = f32[512,1024]{1,0:T(8,128)} async-done(((f32[2048,1024]{1,0:T(8,128)}), f32[512,1024]{1,0:T(8,128)}) %reduce-scatter.15.cloned.1.call-update) | async-done | bytes 2097168 | tf_op jit(solution)/shard_map/reduce_scatter | solution.py:330
  1436.8 283.3 %reduce-scatter.27.cloned.1.call-done = f32[1024,1024]{1,0:T(8,128)} async-done(((f32[4096,1024]{1,0:T(8,128)}), f32[1024,1024]{1,0:T(8,128)}) %reduce-scatter.27.cloned.1.call-update) | async-done | bytes 4194320 | tf_op jit(solution)/shard_map/reduce_scatter | solution.py:336
  1720.1 283.4 %reduce-scatter.25.cloned.1.call-done = f32[1024,1024]{1,0:T(8,128)} async-done(((f32[4096,1024]{1,0:T(8,128)}), f32[1024,1024]{1,0:T(8,128)}) %reduce-scatter.25.cloned.1.call-update) | async-done | bytes 4194320 | tf_op jit(solution)/shard_map/reduce_scatter | solution.py:335
  2003.6 227.9 %all-reduce.33.cloned.1.call-done = (f32[256,128]{1,0:T(8,128)}, f32[512,1024]{1,0:T(8,128)}, f32[512,1024]{1,0:T(8,128)}, f32[256,1024]{1,0:T(8,128)}, f32[256,...) async-done(((f32[256,128]{1,0:T(8,128)}, f32[512,1024]{1,0:T(8,128)}, f32[512,1024]{1,0:T(8,128)}, f32[256,1024]{1,0:T(8,128)}, ...) | async-done | bytes 16908304 | tf_op jit(solution)/shard_map/psum | solution.py:341
  2268.5 17.8 fusion.4
  2286.3 155.2 %all-reduce.21.cloned.1.call-done = f32[1024,1024]{1,0:T(8,128)} async-done(((f32[1024,1024]{1,0:T(8,128)}), f32[1024,1024]{1,0:T(8,128)}) %all-reduce.21.cloned.1.call-update) | async-done | bytes 4194320 | tf_op jit(solution)/shard_map/psum | solution.py:363
  2445.0 17.8 fusion.27
  2462.9 17.7 multiply_add_fusion.4
  2509.2 142.8 %all-reduce.23.cloned.1.call-done = f32[1024,1024]{1,0:T(8,128)} async-done(((f32[1024,1024]{1,0:T(8,128)}), f32[1024,1024]{1,0:T(8,128)}) %all-reduce.23.cloned.1.call-update) | async-done | bytes 4194320 | tf_op jit(solution)/shard_map/psum | solution.py:376
  2652.0 17.0 fusion.151
  2700.7 22.9 while.96
  2723.6 18.0 all-gather.2
  2741.7 116.5 %all-reduce.25.cloned.1.call-done = f32[1024,1024]{1,0:T(8,128)} async-done(((f32[1024,1024]{1,0:T(8,128)}), f32[1024,1024]{1,0:T(8,128)}) %all-reduce.25.cloned.1.call-update) | async-done | bytes 4194320 | tf_op jit(solution)/shard_map/psum | solution.py:376
  2858.2 17.6 fusion.153
  2908.2 297.1 %while.98 = (s32[]{:T(128)}, f32[64,64,1024]{2,1,0:T(8,128)}, f32[64,16,1024]{2,1,0:T(8,128)}, f32[16,1024]{1,0:T(8,128)S(1)}, f32[64,16,1024]{2,1,0:T(8,128)}, ...) while((s32[]{:T(128)}, f32[64,64,1024]{2,1,0:T(8,128)}, ...), condition=%wide.region_21.22_spmd.clone, body=%wide.region_20.21_spmd.clone.sunk | while | flops 31457284 | bytes 113836288 | solution.py:122
  3216.9 17.6 fusion.155
  3277.6 36.4 scatter_custom_fusion
  3335.4 84.0 %all-reduce.29.cloned.1.call-done = f32[1024,1024]{1,0:T(8,128)} async-done(((f32[1024,1024]{1,0:T(8,128)}), f32[1024,1024]{1,0:T(8,128)}) %all-reduce.29.cloned.1.call-update) | async-done | bytes 4194320 | tf_op jit(solution)/shard_map/psum | solution.py:376
  3419.5 17.2 fusion.157
  3436.7 16.3 broadcast_select_fusion.3
  3490.4 201.7 %all-reduce.31.cloned.1.call-done = (f32[256,128]{1,0:T(8,128)}, f32[512,1024]{1,0:T(8,128)}, f32[512,1024]{1,0:T(8,128)}, f32[256,1024]{1,0:T(8,128)}, f32[256,...) async-done(((f32[256,128]{1,0:T(8,128)}, f32[512,1024]{1,0:T(8,128)}, f32[512,1024]{1,0:T(8,128)}, ...) | async-done | bytes 16976912 | tf_op jit(solution)/shard_map/psum | solution.py:51
  (731 shorter events, 1027.6 us)
Async XLA Ops:
  7.2 289.2 %all-gather.18.cloned.1.call-start = ((), (), s32[]{:S(2)}) async-start(), calls=%async_computation.13 | async-start | bytes 5242880 | tf_op jit(solution)/shard_map/all_gather | solution.py:175
  10.2 398.3 %all-gather.14.cloned.1.call-start = ((), (), s32[]{:S(2)}) async-start(), calls=%async_computation.11 | async-start | bytes 2621440 | tf_op jit(solution)/shard_map/all_gather | solution.py:178
  11.1 401.5 %all-gather.16.cloned.1.call-start = ((), (), s32[]{:S(2)}) async-start(), calls=%async_computation.12 | async-start | bytes 5242880 | tf_op jit(solution)/shard_map/all_gather | solution.py:176
  12.3 414.7 %all-gather.20.cloned.1.call-start = ((), (), s32[]{:S(2)}) async-start(), calls=%async_computation.14 | async-start | bytes 5242880 | tf_op jit(solution)/shard_map/all_gather | solution.py:179
  15.1 419.1 %all-gather.12.cloned.1.call-start = ((), (), s32[]{:S(2)}) async-start(), calls=%async_computation.10 | async-start | bytes 2621440 | tf_op jit(solution)/shard_map/all_gather | solution.py:177
  16.1 523.9 %all-gather.22.cloned.1.call-start = ((), (), s32[]{:S(2)}) async-start(), calls=%async_computation.15 | async-start | bytes 10485760 | tf_op jit(solution)/shard_map/all_gather | solution.py:180
  20.0 670.7 %all-gather.24.cloned.1.call-start = ((), (), s32[]{:S(2)}) async-start(), calls=%async_computation.16 | async-start | bytes 10485760 | tf_op jit(solution)/shard_map/all_gather | solution.py:181
  24.4 960.5 %reduce-scatter.13.cloned.1.call-start = ((), (), s32[]{:S(2)}) async-start(), calls=%async_computation.17 | async-start | bytes 655360 | tf_op jit(solution)/shard_map/reduce_scatter | solution.py:329
  42.2 909.7 %copy-start.94 = (f32[1024,1]{0,1:T(1,128)}, f32[1024,1]{0,1:T(1,128)S(1)}, u32[]{:S(2)}) copy-start(f32[1024,1]{0,1:T(1,128)S(1)} %get-tuple-element.982) | copy-start | bytes 12292
  42.6 909.3 %copy-start.96 = (f32[512]{0:T(512)}, f32[512]{0:T(512)S(1)}, u32[]{:S(2)}) copy-start(f32[512]{0:T(512)S(1)} %broadcast_multiply_fusion.4) | copy-start | bytes 6148
  43.7 908.3 %copy-start.102 = (f32[512]{0:T(512)}, f32[512]{0:T(512)S(1)}, u32[]{:S(2)}) copy-start(f32[512]{0:T(512)S(1)} %fusion.105) | copy-start | bytes 6148
  304.1 113.2 %collective-permute-start.1 = (bf16[512,2048]{1,0:T(8,128)(2,1)}, bf16[512,2048]{1,0:T(8,128)(2,1)}, u32[]{:S(2)}, u32[]{:S(2)}) collective-permute-start(bf16[512,2048]{1,0:T(8,128)(2,1)} %get-tuple-element.986), channel_id=1, source_target_pairs={{0,1},{1,2},{2,3},{4,5},{5,6},{6,7},{8,9},{9,10},{10,11},{12,13},{... | collective-permute-start | bytes 6291464 | tf_op jit(solution)/shard_map/ppermute | solution.py:46
  397.7 8.1 collective-permute-start
  401.3 557.9 %copy-start.104 = (f32[512]{0:T(512)}, f32[512]{0:T(512)S(1)}, u32[]{:S(2)}) copy-start(f32[512]{0:T(512)S(1)} %fusion.104) | copy-start | bytes 6148
  726.1 10.2 collective-permute-start.3
  739.3 245.6 %reduce-scatter.19.cloned.1.call-start = ((), (), s32[]{:S(2)}) async-start(), calls=%async_computation.20 | async-start | bytes 5242880 | tf_op jit(solution)/shard_map/reduce_scatter | solution.py:332
  744.0 250.5 %reduce-scatter.21.cloned.1.call-start = ((), (), s32[]{:S(2)}) async-start(), calls=%async_computation.21 | async-start | bytes 5242880 | tf_op jit(solution)/shard_map/reduce_scatter | solution.py:333
  747.3 394.5 %reduce-scatter.23.cloned.1.call-start = ((), (), s32[]{:S(2)}) async-start(), calls=%async_computation.22 | async-start | bytes 10485760 | tf_op jit(solution)/shard_map/reduce_scatter | solution.py:334
  754.7 534.6 %reduce-scatter.17.cloned.1.call-start = ((), (), s32[]{:S(2)}) async-start(), calls=%async_computation.19 | async-start | bytes 10485760 | tf_op jit(solution)/shard_map/reduce_scatter | solution.py:331
  762.1 674.7 %reduce-scatter.15.cloned.1.call-start = ((), (), s32[]{:S(2)}) async-start(), calls=%async_computation.18 | async-start | bytes 10485760 | tf_op jit(solution)/shard_map/reduce_scatter | solution.py:330
  768.3 181.4 %collective-permute-start.2 = (f32[512,2048]{1,0:T(8,128)S(1)}, f32[512,2048]{1,0:T(8,128)S(1)}, u32[]{:S(2)}, u32[]{:S(2)}) collective-permute-start(f32[512,2048]{1,0:T(8,128)S(1)} %slice.99), channel_id=1, source_target_pairs={{1,0},{2,1},{3,2},{5,4},{6,5},{7,6},{9,8},{10,9},{11,10},{13,12},{... | collective-permute-start | bytes 12582920 | tf_op jit(solution)/shard_map/ppermute | solution.py:46
  959.2 760.9 %reduce-scatter.27.cloned.1.call-start = ((), (), s32[]{:S(2)}) async-start(), calls=%async_computation.24 | async-start | bytes 20971520 | tf_op jit(solution)/shard_map/reduce_scatter | solution.py:336
  972.7 1030.8 %reduce-scatter.25.cloned.1.call-start = ((), (), s32[]{:S(2)}) async-start(), calls=%async_computation.23 | async-start | bytes 20971520 | tf_op jit(solution)/shard_map/reduce_scatter | solution.py:335
  984.8 1246.7 %all-reduce.33.cloned.1.call-start = ((), (), s32[]{:S(2)}) async-start(), calls=%async_computation.33 | async-start | bytes 33816576 | tf_op jit(solution)/shard_map/psum | solution.py:341
  2003.5 437.9 %all-reduce.21.cloned.1.call-start = ((), (), s32[]{:S(2)}) async-start(), calls=%async_computation.25 | async-start | bytes 8388608 | tf_op jit(solution)/shard_map/psum | solution.py:363
  2286.3 365.8 %all-reduce.23.cloned.1.call-start = ((), (), s32[]{:S(2)}) async-start(), calls=%async_computation.26 | async-start | bytes 8388608 | tf_op jit(solution)/shard_map/psum | solution.py:376
  2497.8 360.4 %all-reduce.25.cloned.1.call-start = ((), (), s32[]{:S(2)}) async-start(), calls=%async_computation.27 | async-start | bytes 8388608 | tf_op jit(solution)/shard_map/psum | solution.py:376
  2699.9 516.9 %all-reduce.27.cloned.1.call-start = ((), (), s32[]{:S(2)}) async-start(), calls=%async_computation.28 | async-start | bytes 8388608 | tf_op jit(solution)/shard_map/psum | solution.py:376
  2906.5 512.9 %all-reduce.29.cloned.1.call-start = ((), (), s32[]{:S(2)}) async-start(), calls=%async_computation.29 | async-start | bytes 8388608 | tf_op jit(solution)/shard_map/psum | solution.py:376
  3265.3 192.9 %reduce-scatter.29.cloned.1.call-start = ((), (), s32[]{:S(2)}) async-start(), calls=%async_computation.30 | async-start | bytes 368640 | tf_op jit(solution)/shard_map/reduce_scatter | solution.py:337
  3334.5 136.4 %reduce-scatter.31.cloned.1.call-start = ((), (), s32[]{:S(2)}) async-start(), calls=%async_computation.31 | async-start | bytes 81920
  3335.4 356.7 %all-reduce.31.cloned.1.call-start = ((), (), s32[]{:S(2)}) async-start(), calls=%async_computation.32 | async-start | bytes 33964032 | tf_op jit(solution)/shard_map/psum | solution.py:51
  (155 other events, 4052.9 us)
Sparse Core Ops, SparseCore 0:
  10.3 89.8 all-gather.17
  102.3 45.1 all-gather.13
  149.7 79.7 all-gather.15
  231.5 81.8 all-gather.19
  315.4 72.9 all-gather.11
  389.8 150.1 all-gather.21
  541.6 149.0 all-gather.23
  739.4 19.7 reduce-scatter.12
  762.1 137.1 reduce-scatter.18
  901.5 92.9 reduce-scatter.20
  996.9 144.9 reduce-scatter.22
  1144.0 145.1 reduce-scatter.16
  1291.6 145.1 reduce-scatter.14
  1439.1 280.9 reduce-scatter.26
  1722.4 281.0 reduce-scatter.24
  2008.5 222.9 all-reduce.32
  2286.4 155.0 all-reduce.20
  2497.9 154.0 all-reduce.22
  2700.1 158.1 all-reduce.24
  2906.7 153.9 all-reduce.26
  3265.5 153.9 all-reduce.28
  3422.3 18.8 reduce-scatter.28
  3444.0 17.2 reduce-scatter.30
  3468.9 223.1 all-reduce.30
where the time goes:
time: 3750 us; the launch traced here: 3740 us
  waiting for transfers between devices  2380 us (63%)
  other arithmetic  606 us (16%)
  matrix products  399 us (11%)
  blocking collectives  194 us (5%)
  local copies, waits for them, and re-layouts  132 us (4%)
    psum x4, waiting for transfers between devices, body(): gram = lax.psum(exact_left(iterate, iterate), 'seq')  343 us
    reduce_scatter x1, waiting for transfers between devices, body(): lax.psum_scatter(grad_up, 'seq', scatter_dimension=0, tiled=True)  283 us
    reduce_scatter x1, waiting for transfers between devices, body(): lax.psum_scatter(grad_down, 'seq', scatter_dimension=0, tiled=True)  283 us
    psum x1, waiting for transfers between devices, body(): lax.psum((part_z, part_v, part_gamma, part_phi, part_h, part_u, part_up,...  228 us
    psum x1, waiting for transfers between devices, spread_2(): return lax.psum(jnp.where(mine, x, jnp.zeros_like(x)), axis)  202 us
    ppermute x4, waiting for transfers between devices, passed_along(): return lax.ppermute(block, axis, route)  193 us
    dot_general x10, matrix products, exact_plain(): jnp.dot(left, right, precision=HIGHEST, preferred_element_type=jnp.float32)  162 us
    add_any x16, other arithmetic, ema_run(): final, mixed = lax.scan(jax.checkpoint(one_block), start, pieces)  159 us
  transfers between devices with their start and end apart: 28, of which 17 were waited for; matrix products, arithmetic and copies ran while one was open for 21% of the time, Pallas kernels for 0%

commit v1 on v0

v1 whole, which is shorter than its diff:
```python
import math

import jax
import jax.numpy as jnp
from jax import lax
from jax.experimental import pallas as pl
from jax.experimental.pallas import tpu as pltpu
from jax.sharding import PartitionSpec as P

D = 1024
Z = 128
V = 2048
NE = 16
FF = 4096
NS_STEPS = 5
LANES = 128
SUBS = D // LANES

HIGH = lax.Precision.HIGH
POLY_A = 3.4445
POLY_B = -4.775
POLY_C = 2.0315
MOMENTUM = 0.5
MATRIX_RATE = 0.5
VECTOR_RATE = 0.2

SLOT = {"up": 0, "z": 1, "down": 2, "phi": 3, "g": 4, "h": 5, "u": 6, "v": 7}
NAMES = ("z", "v", "g", "phi", "h", "u", "up", "down")
FAN = {"z": D, "v": D, "g": D, "phi": D, "h": D, "u": V, "up": D, "down": FF}


def as_half(value):
    return value.astype(jnp.bfloat16)


def times_plain(left, right):
    return jnp.dot(left, right, preferred_element_type=jnp.float32)


def times_right(left, right):
    return lax.dot_general(
        left, right, (((1,), (1,)), ((), ())), preferred_element_type=jnp.float32
    )


def times_left(left, right):
    return lax.dot_general(
        left, right, (((0,), (0,)), ((), ())), preferred_element_type=jnp.float32
    )


def times_high(left, right):
    return jnp.dot(left, right, precision=HIGH, preferred_element_type=jnp.float32)


def silu_grad(value):
    sig = jax.nn.sigmoid(value)
    return sig * (1.0 + value * (1.0 - sig))


def norm_rows(rows, gain):
    center = rows - jnp.mean(rows, axis=-1, keepdims=True)
    spread = jnp.mean(center * center, axis=-1, keepdims=True)
    return center * lax.rsqrt(spread + 1e-05) * gain


def turned(x, distance):
    count = lax.axis_size("seq")
    return lax.ppermute(x, "seq", [(i, (i + distance) % count) for i in range(count)])


def others_blocks(x):
    return [turned(x, k) for k in range(1, lax.axis_size("seq"))]


def in_order(own, others):
    count, mine = lax.axis_size("seq"), lax.axis_index("seq")
    held = jnp.stack([own] + others)
    rows = [
        lax.dynamic_index_in_dim(held, lax.rem(mine - i + count, count), 0, keepdims=False)
        for i in range(count)
    ]
    return jnp.concatenate(rows, axis=0)


def own_slice(block):
    share = block.shape[0] // lax.axis_size("dp")
    return lax.dynamic_slice_in_dim(block, lax.axis_index("dp") * share, share, 0)


def gathered_weight(block):
    dp = lax.axis_size("dp")
    share = block.shape[0] // dp
    far = jnp.stack(others_blocks(own_slice(block)))
    far = lax.all_gather(far, "dp", axis=0, tiled=False)
    near = block.reshape(dp, 1, share, block.shape[1])
    return jnp.concatenate([near, far], axis=1).reshape(-1, block.shape[1])


def summed_share(grad):
    count = lax.axis_size("seq")
    dp = lax.axis_size("dp")
    share = grad.shape[0] // (dp * count)
    part = lax.psum_scatter(grad, "dp", scatter_dimension=0, tiled=True)
    part = part.reshape(count, share, grad.shape[1])
    total = part[0].astype(jnp.float32)
    for k in range(1, count):
        total = total + turned(part[k], -k).astype(jnp.float32)
    return total


def in_columns(block, slots):
    count = lax.axis_size("seq")
    return [
        lax.ppermute(
            block,
            ("dp", "seq"),
            [(s * count + i, s * count + (i + k) % count) for s in slots for i in range(count)],
        )
        for k in range(1, count)
    ]


def summed_small(x):
    count, mine, dp = lax.axis_size("seq"), lax.axis_index("seq"), lax.axis_size("dp")
    share = x.shape[0] // count
    held = x.reshape(count, share, x.shape[1])
    total = lax.dynamic_index_in_dim(held, mine, 0, keepdims=False)
    for k in range(1, count):
        piece = lax.dynamic_index_in_dim(held, lax.rem(mine + k, count), 0, keepdims=False)
        total = total + turned(piece, k)
    step = 1
    while step < dp:
        total = total + lax.ppermute(total, "dp", [(i, i ^ step) for i in range(dp)])
        step *= 2
    return total


def ema_end_kernel(u_ref, q_ref, end_ref):
    q = [q_ref[j] for j in range(NE)]

    def step(t, state):
        u = u_ref[t]
        return tuple(q[j] * state[j] + u for j in range(NE))

    zero = jnp.zeros((SUBS, LANES), jnp.float32)
    state = lax.fori_loop(0, u_ref.shape[0], step, (zero,) * NE, unroll=8)
    for j in range(NE):
        end_ref[j] = state[j]


def ema_run_kernel(u_ref, q_ref, w_ref, start_ref, e_ref):
    q = [q_ref[j] for j in range(NE)]
    w = [w_ref[j] for j in range(NE)]

    def step(t, state):
        u = u_ref[t]
        state = tuple(q[j] * state[j] + u for j in range(NE))
        terms = [w[j] * state[j] for j in range(NE)]
        while len(terms) > 1:
            terms = [terms[i] + terms[i + 1] for i in range(0, len(terms), 2)]
        e_ref[t] = terms[0]
        return state

    lax.fori_loop(0, u_ref.shape[0], step, tuple(start_ref[j] for j in range(NE)), unroll=4)


def ema_sums_kernel(u_ref, de_ref, q_ref, start_ref, first_ref, dw_ref, dh_ref, tail_ref):
    rows = u_ref.shape[0]
    zero = jnp.zeros((SUBS, LANES), jnp.float32)
    half = NE // 2
    for base in (0, half):
        q = [q_ref[base + j] for j in range(half)]

        def step(t, carry, q=q):
            h, g, dw, dh, r = carry
            u, de, late = u_ref[t], de_ref[t], de_ref[rows - 1 - t]
            g = tuple(q[j] * g[j] + h[j] for j in range(half))
            h = tuple(q[j] * h[j] + u for j in range(half))
            dw = tuple(dw[j] + de * h[j] for j in range(half))
            dh = tuple(dh[j] + de * g[j] for j in range(half))
            r = tuple(q[j] * r[j] + late for j in range(half))
            return (h, g, dw, dh, r)

        blank = (zero,) * half
        start = tuple(start_ref[base + j] for j in range(half))
        _, g, dw, dh, r = lax.fori_loop(0, rows, step, (start, blank, blank, blank, blank), unroll=2)
        for j in range(half):
            dw_ref[base + j] = dw[j]
            dh_ref[base + j] = dh[j]
            tail_ref[base + j] = g[j]
            first_ref[base + j] = r[j]


def ema_back_kernel(de_ref, q_ref, w_ref, start_ref, du_ref):
    rows = de_ref.shape[0]
    q = [q_ref[j] for j in range(NE)]
    w = [w_ref[j] for j in range(NE)]

    def step(s, state):
        t = rows - 1 - s
        de = de_ref[t]
        state = tuple(q[j] * state[j] + de for j in range(NE))
        terms = [w[j] * state[j] for j in range(NE)]
        while len(terms) > 1:
            terms = [terms[i] + terms[i + 1] for i in range(0, len(terms), 2)]
        du_ref[t] = terms[0]
        return state

    lax.fori_loop(0, rows, step, tuple(start_ref[j] for j in range(NE)), unroll=4)


def f32_shape(*dims):
    return jax.ShapeDtypeStruct(dims, jnp.float32)


def local_call(kernel, out_shape, flops, moved, *args):
    return pl.pallas_call(
        kernel,
        out_shape=out_shape,
        compiler_params=pltpu.CompilerParams(vmem_limit_bytes=24 * 1024 * 1024),
        cost_estimate=pl.CostEstimate(flops=flops, bytes_accessed=moved, transcendentals=0),
    )(*args)


def tiled(x):
    return x.reshape(x.shape[:-1] + (SUBS, LANES))


def flat(x):
    return x.reshape(x.shape[:-2] + (D,))


def carried(ends, decay, forward):
    count, mine = lax.axis_size("seq"), lax.axis_index("seq")
    total = jnp.zeros_like(ends)
    factor = jnp.ones_like(decay)
    for k in range(1, count):
        if forward:
            pairs = [(i, i + k) for i in range(count - k)]
        else:
            pairs = [(i + k, i) for i in range(count - k)]
        total = total + factor * lax.ppermute(ends, "seq", pairs)
        factor = factor * decay
    return total


def orthogonal_factor(gram_raw):
    scale = 1.0 / (jnp.sqrt(jnp.trace(gram_raw)) + 1e-07)
    gram = gram_raw * (scale * scale)
    eye = jnp.eye(gram.shape[0], dtype=jnp.float32)
    factor = None
    for step in range(NS_STEPS):
        square = times_high(gram, gram)
        poly = POLY_A * eye + POLY_B * gram + POLY_C * square
        factor = poly * scale if factor is None else times_high(factor, poly)
        if step + 1 < NS_STEPS:
            gram = times_high(times_high(gram, poly), poly)
    return factor


def body(tokens, cotangent, lengths, *rest):
    order = ("z", "v", "g", "phi", "h", "u", "up", "down")
    masters = dict(zip(order, rest[:8]))
    moments = dict(zip(order, rest[8:16]))
    channel_params, channel_moment, query_params, query_moment = rest[16:]
    seq_count = lax.axis_size("seq")
    seq_index = lax.axis_index("seq")
    dp_count = lax.axis_size("dp")
    dp_index = lax.axis_index("dp")
    rows = tokens.shape[0]

    half = {name: as_half(masters[name]) for name in order}
    small = jnp.concatenate(
        [
            channel_params,
            jnp.pad(query_params, ((0, channel_params.shape[0] - query_params.shape[0]), (0, 0))),
        ],
        axis=1,
    )
    small = as_half(small)
    small_all = in_order(small, others_blocks(small)).astype(jnp.float32)
    channel = small_all[:, : channel_params.shape[1]]
    query_set = small_all.reshape(seq_count, -1, small_all.shape[1])[
        :, : query_params.shape[0], channel_params.shape[1] :
    ].reshape(Z, 3)
    full = {"v": gathered_weight(half["v"])}
    wide_block = jnp.concatenate([half["z"], half["phi"], half["h"]], axis=1)
    wide_full = lax.all_gather(own_slice(wide_block), ("seq", "dp"), axis=0, tiled=True)
    full["z"] = wide_full[:, :Z]
    full["phi"] = wide_full[:, Z : Z + D]
    full["h"] = wide_full[:, Z + D :]
    for name in ("g", "u", "up", "down"):
        full[name] = gathered_weight(half[name])

    gain_one = channel[:, 0]
    gain_two = channel[:, 1]
    omega = channel[:, 2]
    alpha, delta, beta, eta = (
        channel[:, 3 + k * NE : 3 + (k + 1) * NE].T for k in range(4)
    )
    scale_q = query_set[:, 0]
    shift_q = query_set[:, 1]
    scale_k = query_set[:, 2]
    score_scale = Z ** (-0.5)

    place = seq_index * rows + jnp.arange(rows, dtype=jnp.int32)
    keep = (place < lengths[0]).astype(jnp.float32)[:, None]
    inputs = tokens.astype(jnp.float32)
    weighted = cotangent.astype(jnp.float32) * keep
    back_ffn = as_half(weighted)
    normed, norm_back_one = jax.vjp(norm_rows, inputs, gain_one)
    normed_low = as_half(normed)
    evens = [(i, i + 1) for i in range(0, seq_count - 1, 2)]
    odds = [(i + 1, i) for i in range(0, seq_count - 1, 2)]
    normed_both = jnp.concatenate([lax.ppermute(normed_low, "seq", evens), normed_low], axis=0)

    inject_rate = jax.nn.sigmoid(alpha)
    damp = jax.nn.sigmoid(delta)
    decay = 1.0 - inject_rate * damp
    mix = eta * inject_rate * beta
    decay_tiled, mix_tiled = tiled(decay), tiled(mix)
    decay_all = decay_tiled**rows
    normed_tiled = tiled(normed)
    ends = local_call(
        ema_end_kernel, f32_shape(NE, SUBS, LANES), 2 * rows * NE * D, 4 * rows * D, normed_tiled, decay_tiled
    )
    start = carried(ends, decay_all, True)
    v_pre = times_right(normed_both, full["v"])
    values_all = as_half(jax.nn.silu(v_pre))
    ema = flat(
        local_call(
            ema_run_kernel,
            f32_shape(rows, SUBS, LANES),
            4 * rows * NE * D,
            8 * rows * D,
            normed_tiled,
            decay_tiled,
            mix_tiled,
            start,
        )
    )
    mix_pre = ema + omega * normed
    mixed_low = as_half(jax.nn.silu(mix_pre))
    z_pre = times_plain(mixed_low, full["z"])
    zed = jax.nn.silu(z_pre)
    queries_low = as_half(zed * scale_q + shift_q)
    keys_low = as_half(zed * scale_k)
    keys_all = jnp.concatenate([lax.ppermute(keys_low, "seq", evens), keys_low], axis=0)
    odd_device = seq_index % 2 == 1
    query_place = jnp.arange(rows)[:, None]
    key_place = jnp.arange(2 * rows)[None, :]
    allowed = jnp.where(key_place < rows, odd_device, key_place - rows <= query_place)
    scores = jnp.where(allowed, times_right(queries_low, keys_all) * score_scale, -1e30)
    top = jnp.max(scores, axis=-1, keepdims=True)
    expo = jnp.exp(scores - top)
    probs = expo / jnp.sum(expo, axis=-1, keepdims=True)
    probs_low = as_half(probs)
    attended = times_plain(probs_low, values_all)
    gam_pre = times_right(mixed_low, full["g"])
    gamma = jax.nn.silu(gam_pre)
    gated_low = as_half(gamma * attended)
    phi = jax.nn.sigmoid(times_plain(mixed_low, full["phi"]))
    h_pre = times_plain(mixed_low, full["h"]) + times_plain(gated_low, full["u"])
    cand = jax.nn.silu(h_pre)
    middle = phi * cand + (1.0 - phi) * inputs
    wide, norm_back_two = jax.vjp(norm_rows, middle, gain_two)
    wide_low = as_half(wide)
    a_pre = times_right(wide_low, full["up"])
    active_low = as_half(jax.nn.silu(a_pre))
    result = middle + times_plain(active_low, full["down"])
    block_output = as_half(result * keep)

    share = {}
    share["down"] = summed_share(as_half(times_left(active_low, back_ffn)))
    d_apre = as_half(times_right(back_ffn, full["down"]) * silu_grad(a_pre))
    share["up"] = summed_share(as_half(times_left(d_apre, wide_low)))
    d_mid_norm, d_gain_two = norm_back_two(times_plain(d_apre, full["up"]))
    d_middle = weighted + d_mid_norm
    d_phipre = as_half(d_middle * (cand - inputs) * phi * (1.0 - phi))
    d_hpre = as_half(d_middle * phi * silu_grad(h_pre))
    tokens_grad = d_middle * (1.0 - phi)
    d_gated = times_right(d_hpre, full["u"])
    d_attended = as_half(d_gated * gamma)
    d_gampre = as_half(d_gated * attended * silu_grad(gam_pre))
    share["u"] = summed_share(as_half(times_left(gated_low, d_hpre)))
    share["g"] = summed_share(as_half(times_left(d_gampre, mixed_low)))

    d_probs = times_right(d_attended, values_all)
    d_scores = as_half(probs * (d_probs - jnp.sum(probs * d_probs, axis=-1, keepdims=True)))
    d_vpre = as_half(times_left(probs_low, d_attended) * silu_grad(v_pre))
    share["v"] = summed_share(as_half(times_left(d_vpre, normed_both)))
    d_queries = times_plain(d_scores, keys_all) * score_scale
    d_keys_all = times_left(d_scores, queries_low) * score_scale
    d_keys = d_keys_all[rows:] + lax.ppermute(d_keys_all[:rows], "seq", odds)
    d_normed_all = times_plain(d_vpre, full["v"])
    d_normed = d_normed_all[rows:] + lax.ppermute(
        as_half(d_normed_all[:rows]), "seq", odds
    ).astype(jnp.float32)
    d_scale_q = jnp.sum(d_queries * zed, axis=0)
    d_shift_q = jnp.sum(d_queries, axis=0)
    d_scale_k = jnp.sum(d_keys * zed, axis=0)
    d_zpre = as_half((d_queries * scale_q + d_keys * scale_k) * silu_grad(z_pre))
    d_wide = jnp.concatenate([d_zpre, d_phipre, d_hpre], axis=1)
    grad_wide = as_half(times_left(mixed_low, d_wide))
    ordered = grad_wide.reshape(seq_count, dp_count, -1, grad_wide.shape[1])
    ordered = jnp.stack(
        [
            lax.dynamic_index_in_dim(
                ordered, lax.rem(seq_index - k + seq_count, seq_count), 0, keepdims=False
            )
            for k in range(seq_count)
        ],
        axis=1,
    )
    share_wide = summed_share(ordered.reshape(grad_wide.shape))
    share["z"] = share_wide[:, :Z]
    share["phi"] = share_wide[:, Z : Z + D]
    share["h"] = share_wide[:, Z + D :]
    d_mixed = times_right(d_wide, wide_full) + times_plain(d_gampre, full["g"])

    d_ema = d_mixed * silu_grad(mix_pre)
    d_ema_tiled = tiled(d_ema)
    state_shape = f32_shape(NE, SUBS, LANES)
    first, d_mix, d_state, state_tail = local_call(
        ema_sums_kernel,
        (state_shape,) * 4,
        10 * rows * NE * D,
        8 * rows * D,
        normed_tiled,
        d_ema_tiled,
        decay_tiled,
        start,
    )
    behind = carried(first, decay_all, False)
    d_normed_ema = flat(
        local_call(
            ema_back_kernel,
            f32_shape(rows, SUBS, LANES),
            4 * rows * NE * D,
            8 * rows * D,
            d_ema_tiled,
            decay_tiled,
            mix_tiled,
            behind,
        )
    )
    d_mix = flat(d_mix)
    d_decay = mix * flat(d_state + decay_tiled * behind * state_tail)
    d_eta = d_mix * inject_rate * beta
    d_beta = d_mix * eta * inject_rate
    d_inject = d_mix * eta * beta - d_decay * damp
    d_alpha = d_inject * inject_rate * (1.0 - inject_rate)
    d_delta = -d_decay * inject_rate * damp * (1.0 - damp)
    d_omega = jnp.sum(d_ema * normed, axis=0)
    d_input_norm, d_gain_one = norm_back_one(d_normed + d_normed_ema + omega * d_ema)
    tokens_grad = tokens_grad + d_input_norm

    share_low = {}
    momentum = {}
    for name in order:
        share_low[name] = as_half(MOMENTUM * own_slice(moments[name]) + share[name])
    block = {}
    for name in ("down", "up", "u", "g", "phi", "h"):
        block[name] = lax.all_gather(share_low[name], "dp", axis=0, tiled=True)
        momentum[name] = block[name].astype(jnp.float32)

    def chosen(names, height):
        out = jnp.zeros((height, D), jnp.bfloat16)
        for name in names:
            item = block[name]
            item = jnp.pad(item, ((0, height - item.shape[0]), (0, D - item.shape[1])))
            out = jnp.where(dp_index == SLOT[name], item, out)
        return out

    def gram_of(names):
        height = max(block[name].shape[0] for name in names)
        own = chosen(names, height)
        pieces = [own] + in_columns(own, [SLOT[name] for name in names])
        return times_left(jnp.concatenate(pieces, axis=0), jnp.concatenate(pieces, axis=0))

    gram = gram_of(("down", "up")) + gram_of(("u", "g", "phi", "h"))
    late = jnp.concatenate([share_low["v"], share_low["z"].reshape(-1, D)], axis=0)
    late = lax.all_gather(late, ("seq", "dp"), axis=0, tiled=False)
    late = late.reshape(seq_count, dp_count, -1, D)
    cut = share_low["v"].shape[0]
    all_v = late[:, :, :cut].reshape(seq_count, -1, D)
    all_z = late[:, :, cut:].reshape(seq_count, -1, Z)
    block["v"] = lax.dynamic_index_in_dim(all_v, seq_index, 0, keepdims=False)
    block["z"] = lax.dynamic_index_in_dim(all_z, seq_index, 0, keepdims=False)
    for name in ("v", "z"):
        momentum[name] = block[name].astype(jnp.float32)
    all_v = all_v.reshape(-1, D)
    all_z = all_z.reshape(-1, Z)
    gram_v = times_left(all_v, all_v)
    gram_z = jnp.pad(times_left(all_z, all_z), ((0, D - Z), (0, D - Z)))
    gram = gram + jnp.where(dp_index == SLOT["v"], gram_v, 0.0)
    gram = gram + jnp.where(dp_index == SLOT["z"], gram_z, 0.0)
    factor = as_half(orthogonal_factor(gram))
    height = max(block[name].shape[0] for name in order)
    direction = as_half(times_plain(chosen(order, height), factor))
    directions = lax.all_gather(direction, "dp", axis=0, tiled=False)
    updated = {}
    for name in order:
        master = masters[name]
        piece = directions[SLOT[name], : master.shape[0], : master.shape[1]].astype(jnp.float32)
        rate = MATRIX_RATE * math.sqrt(master.shape[0] * seq_count / FAN[name])
        updated[name] = master - rate * piece

    grad_channel = jnp.concatenate(
        [
            d_gain_one[:, None],
            d_gain_two[:, None],
            d_omega[:, None],
            d_alpha.T,
            d_delta.T,
            d_beta.T,
            d_eta.T,
        ],
        axis=1,
    )
    grad_query = jnp.stack([d_scale_q, d_shift_q, d_scale_k], axis=1)
    query_rows = Z // seq_count
    channel_rows = D // seq_count
    grad_query = jnp.pad(
        grad_query.reshape(seq_count, query_rows, 3),
        ((0, 0), (0, channel_rows - query_rows), (0, 0)),
    ).reshape(D, 3)
    small_sum = summed_small(jnp.concatenate([grad_channel, grad_query], axis=1))
    columns = channel_params.shape[1]
    channel_renewed = MOMENTUM * channel_moment + small_sum[:, :columns]
    query_renewed = MOMENTUM * query_moment + small_sum[:query_rows, columns:]
    squares = jnp.concatenate(
        [
            jnp.sum(channel_renewed * channel_renewed, axis=0),
            jnp.sum(query_renewed * query_renewed, axis=0),
        ]
    )[None]
    squares = sum(others_blocks(squares), squares)[0]
    channel_rms = jnp.sqrt(squares[:columns] / D + 1e-06)
    channel_new = channel_params - VECTOR_RATE * channel_renewed / channel_rms
    query_rms = jnp.sqrt(squares[columns:] / Z + 1e-06)
    query_new = query_params - VECTOR_RATE * query_renewed / query_rms
    return (
        block_output,
        tokens_grad,
        *[updated[name] for name in order],
        *[momentum[name] for name in order],
        channel_new,
        channel_renewed,
        query_new,
        query_renewed,
    )


def solution(mesh):
    token_spec = P(("dp", "seq"), None)
    row_spec = P("seq", None)
    return jax.shard_map(
        body,
        mesh=mesh,
        in_specs=(token_spec, token_spec, P("dp")) + (row_spec,) * 20,
        out_specs=(token_spec, token_spec) + (row_spec,) * 20,
        check_vma=False,
    )
```

time: 3750 us -> 1350 us (0.36)
  waiting for transfers between devices: 2380 us -> 655 us
  other arithmetic: 606 us -> 118 us
  blocking collectives: 194 us -> 19.2 us
  starting transfers between devices: 9.95 us -> 101 us
  local copies, waits for them, and re-layouts: 132 us -> 42 us
  matrix products: 399 us -> 349 us
    psum x7 -> x0, waiting for transfers between devices: 928 us -> none  [the longest x4 343 us: body(): gram = lax.psum(exact_left(iterate, iterate), 'seq')]
    reduce_scatter x9 -> x6, waiting for transfers between devices: 1020 us -> 209 us  [summed_share(): part = lax.psum_scatter(grad, 'dp', scatter_dimension=0, tiled=True)]
    dot_general x64 -> x0, other arithmetic: 274 us -> none  [the longest x16 137 us: one_block(): inner = jnp.einsum('tsc,sc->tc', toeplitz, piece, precision=HIGHEST)]
    add_any x32 -> x0, other arithmetic: 160 us -> none  [the longest x16 159 us: ema_run(): final, mixed = lax.scan(jax.checkpoint(one_block), start, pieces)]
    all_gather x6 -> x2, blocking collectives: 168 us -> 19.2 us  [body(): block[name] = lax.all_gather(share_low[name], 'dp', axis=0, tiled=True)]
    dot_general x15 -> x17, matrix products: 241 us -> 126 us  [times_high(): jnp.dot(left, right, precision=HIGH, preferred_element_type=jnp.float32)]
    ppermute x4 -> x61, starting transfers between devices: 8.34 us -> 99.6 us  [the longest x42 61.1 us: turned(): lax.ppermute(x, 'seq', [(i, (i + distance) % count) for i in range(count)])]
    dot_general x10 -> x12, matrix products: 57.1 us -> 105 us  [times_left(): lax.dot_general(left, right, (((0,), (0,)), ((), ())), preferred_element_...]
  transfers between devices with their start and end apart: 28 -> 79, of which waited for: 17 -> 46; matrix products, arithmetic and copies ran while one was open for 21% -> 19% of each run, Pallas kernels for 0% -> 3%
where the time goes in v1:
time: 1350 us; the launch traced here: 1340 us
  waiting for transfers between devices  655 us (49%)
  matrix products  349 us (26%)
  other arithmetic  118 us (9%)
  starting transfers between devices  101 us (7%)
  local copies, waits for them, and re-layouts  42 us (3%)
  Pallas kernels  35.2 us (3%)
  blocking collectives  19.2 us (1%)
  between operations  18 us (1%)
    reduce_scatter x6, waiting for transfers between devices, summed_share(): part = lax.psum_scatter(grad, 'dp', scatter_dimension=0, tiled=True)  209 us
    ppermute x42, waiting for transfers between devices, turned(): lax.ppermute(x, 'seq', [(i, (i + distance) % count) for i in range(count)])  127 us
    dot_general x17, matrix products, times_high(): jnp.dot(left, right, precision=HIGH, preferred_element_type=jnp.float32)  126 us
    dot_general x12, matrix products, times_left(): lax.dot_general(left, right, (((0,), (0,)), ((), ())), preferred_element_...  105 us
    all_gather x1, waiting for transfers between devices, body(): late = lax.all_gather(late, ('seq', 'dp'), axis=0, tiled=False)  97.7 us
    ppermute x6, waiting for transfers between devices, in_columns(): lax.ppermute(block, ('dp', 'seq'), [(s * count + i, s * count + (i + k) %...  73.5 us
    dot_general x8, matrix products, times_right(): lax.dot_general(left, right, (((1,), (1,)), ((), ())), preferred_element_...  64 us
    all_gather x4, waiting for transfers between devices, body(): block[name] = lax.all_gather(share_low[name], 'dp', axis=0, tiled=True)  63.7 us
  transfers between devices with their start and end apart: 79, of which 46 were waited for; matrix products, arithmetic and copies ran while one was open for 19% of the time, Pallas kernels for 3%

profile of v1, /device:TPU:0, one launch (start us, length us, event | category | flops | bytes accessed | tf_op | source)
XLA Modules:
  0.0 1337.4 jit_solution(13694013166328295970)
XLA Ops:
  72.1 15.6 %collective-permute-done.21 = bf16[128,1024]{1,0:T(8,128)(2,1)S(1)} collective-permute-done((bf16[128,1024]{1,0:T(8,128)(2,1)S(1)}, bf16[128,1024]{1,0:T(8,128)(2,1)S(1)}, u32[]{:S(2)}, u32[]{:S(2)}) %collective-permute-start.21) | collective-permute-done | bytes 262176 | tf_op jit(solution)/shard_map/ppermute | solution.py:69
  100.5 17.4 %collective-permute-done.18 = bf16[128,1024]{1,0:T(8,128)(2,1)S(1)} collective-permute-done((bf16[128,1024]{1,0:T(8,128)(2,1)S(1)}, bf16[128,1024]{1,0:T(8,128)(2,1)S(1)}, u32[]{:S(2)}, u32[]{:S(2)}) %collective-permute-start.18) | collective-permute-done | bytes 262176 | tf_op jit(solution)/shard_map/ppermute | solution.py:69
  166.2 13.8 %collective-permute-done.10 = bf16[512,1024]{1,0:T(8,128)(2,1)} collective-permute-done((bf16[512,1024]{1,0:T(8,128)(2,1)}, bf16[512,1024]{1,0:T(8,128)(2,1)}, u32[]{:S(2)}, u32[]{:S(2)}) %collective-permute-start.10) | collective-permute-done | bytes 1048608 | tf_op jit(solution)/shard_map/ppermute | solution.py:316
  179.9 10.3 fusion.8
  207.7 8.8 online-softmax
  216.5 8.7 multiply_convert_fusion.5
  248.8 39.8 %all-gather.37.cloned.1.call-done = bf16[24,128,1024]{2,1,0:T(8,128)(2,1)} async-done(((bf16[3,128,1024]{2,1,0:T(8,128)(2,1)}), bf16[24,128,1024]{2,1,0:T(8,128)(2,1)}) %all-gather.37.cloned.1.call-update) | async-done | bytes 6291472 | tf_op jit(solution)/shard_map/all_gather | solution.py:95
  296.2 12.0 fusion.249
  308.3 9.7 multiply_convert_fusion.1
  318.0 9.2 multiply_reduce_fusion
  339.4 8.4 multiply_convert_fusion.3
  355.7 9.2 multiply_convert_fusion
  402.4 11.9 convolution_convert_fusion.1
  414.6 11.7 convolution_convert_fusion
  452.5 48.2 %reduce-scatter.17.cloned.1.call-done = bf16[256,1024]{1,0:T(8,128)(2,1)} async-done(((bf16[2048,1024]{1,0:T(8,128)(2,1)}), bf16[256,1024]{1,0:T(8,128)(2,1)}) %reduce-scatter.17.cloned.1.call-update) | async-done | bytes 524304 | tf_op jit(solution)/shard_map/reduce_scatter | solution.py:104
  508.9 48.2 %reduce-scatter.13.cloned.1.call-done = bf16[128,2176]{1,0:T(8,128)(2,1)} async-done(((bf16[1024,2176]{1,0:T(8,128)(2,1)}), bf16[128,2176]{1,0:T(8,128)(2,1)}) %reduce-scatter.13.cloned.1.call-update) | async-done | bytes 557072 | tf_op jit(solution)/shard_map/reduce_scatter | solution.py:104
  574.0 57.8 %reduce-scatter.7.cloned.1.call-done = bf16[512,1024]{1,0:T(8,128)(2,1)} async-done(((bf16[4096,1024]{1,0:T(8,128)(2,1)}), bf16[512,1024]{1,0:T(8,128)(2,1)}) %reduce-scatter.7.cloned.1.call-update) | async-done | bytes 1048592 | tf_op jit(solution)/shard_map/reduce_scatter | solution.py:104
  644.2 10.1 collective-permute-done.29
  656.4 50.5 %reduce-scatter.9.cloned.1.call-done = bf16[512,1024]{1,0:T(8,128)(2,1)} async-done(((bf16[4096,1024]{1,0:T(8,128)(2,1)}), bf16[512,1024]{1,0:T(8,128)(2,1)}) %reduce-scatter.9.cloned.1.call-update) | async-done | bytes 1048592 | tf_op jit(solution)/shard_map/reduce_scatter | solution.py:104
  719.2 10.1 collective-permute-done.32
  732.4 9.7 all_gather.78
  742.1 9.5 all_gather.77
  768.8 9.5 fusion.16
  778.3 97.7 %all-gather.43.cloned.1.call-done = bf16[32,68,1024]{2,1,0:T(8,128)(2,1)} async-done(((bf16[1,68,1024]{2,1,0:T(8,128)(2,1)}), bf16[32,68,1024]{2,1,0:T(8,128)(2,1)}) %all-gather.43.cloned.1.call-update) | async-done | bytes 4456464 | tf_op jit(solution)/shard_map/all_gather | solution.py:484
  882.4 26.4 %all-gather.23.cloned.1.call-done = bf16[1024,1024]{1,0:T(8,128)(2,1)} async-done(((bf16[128,1024]{1,0:T(8,128)(2,1)}), bf16[1024,1024]{1,0:T(8,128)(2,1)}) %all-gather.23.cloned.1.call-update) | async-done | bytes 2097168 | tf_op jit(solution)/shard_map/all_gather | solution.py:465
  908.7 30.2 %all-gather.25.cloned.1.call-done = bf16[1024,1024]{1,0:T(8,128)(2,1)} async-done(((bf16[128,1024]{1,0:T(8,128)(2,1)}), bf16[1024,1024]{1,0:T(8,128)(2,1)}) %all-gather.25.cloned.1.call-update) | async-done | bytes 2097168 | tf_op jit(solution)/shard_map/all_gather | solution.py:465
  959.3 10.2 fusion.244
  975.6 67.4 %collective-permute-done.47 = bf16[1024,1024]{1,0:T(8,128)(2,1)S(1)} collective-permute-done((bf16[1024,1024]{1,0:T(8,128)(2,1)S(1)}, bf16[1024,1024]{1,0:T(8,128)(2,1)S(1)}, u32[]{:S(2)}, u32[]{:S(2)}) %collective-permute-start.47) | collective-permute-done | bytes 2097184 | tf_op jit(solution)/shard_map/ppermute | solution.py:115
  1044.3 31.2 %select_reduce_fusion = (f32[]{:T(128)}, f32[1024,1024]{1,0:T(8,128)}) fusion(f32[128,128]{1,0:T(8,128)S(1)} %copy-done.71, pred[]{:T(512)S(6)} %eq.60, f32[1024,1024,1,1]{1,0,3,2:T(8,128)} %fusion.244, pred[]{:T(512)S(6)} %eq.59, f32[1024,1024]{1,0:T(8,128)} %fusion.16, bf16[1024,1024]{1,0:T(8,128)(2,1)} %copy-done.95, bf16[1024,1024]{1,0:T(8,128)(2,1)} %copy-done.96, ...), kind=kOutput, calls=%fused_computation.51 | convolution fusion | flops 8631877632 | bytes 21037062 | tf_op jit(solution)/shard_map/dot_general | solution.py:47
  1076.3 12.4 fusion.9
  1231.1 14.6 %shard_map.392 = (f32[16,8,128]{2,1,0:T(8,128)S(1)}, f32[16,8,128]{2,1,0:T(8,128)S(1)}, f32[16,8,128]{2,1,0:T(8,128)S(1)}, f32[16,8,128]{2,1,0:T(8,128)S(1)}) custom-call(f32[512,8,128]{2,1,0:T(8,128)S(1)} %bitcast.303, f32[512,8,128]{2,1,0:T(8,128)S(1)} %bitcast.304, f32[16,8,128]{2,1,0:T(8,128)S(1)} %bitcast.311, f32[16,8,128]{2,1,0:T(8,128)S(1)} %copy-done.5), custom_call_target="tpu_custom_call" | custom-call | flops 83886080 | bytes 4194304 | tf_op jit(solution)/shard_map/pallas_call | solution.py:218
  1284.5 12.8 multiply_convert_fusion.8
  (546 shorter events, 576.5 us)
Async XLA Ops:
  7.2 145.2 %all-gather.33.cloned.1.call-start = ((), (), s32[]{:S(2)}) async-start(), calls=%async_computation.18 | async-start | bytes 3538944 | tf_op jit(solution)/shard_map/all_gather | solution.py:95
  26.3 130.6 %all-gather.31.cloned.1.call-start = ((), (), s32[]{:S(2)}) async-start(), calls=%async_computation.17 | async-start | bytes 3538944 | tf_op jit(solution)/shard_map/all_gather | solution.py:95
  42.3 119.1 %all-gather.35.cloned.1.call-start = ((), (), s32[]{:S(2)}) async-start(), calls=%async_computation.19 | async-start | bytes 3538944 | tf_op jit(solution)/shard_map/all_gather | solution.py:95
  58.6 137.1 %all-gather.21.cloned.1.call-start = ((), (), s32[]{:S(2)}) async-start(), calls=%async_computation.6 | async-start | bytes 4595712 | tf_op jit(solution)/shard_map/all_gather | solution.py:289
  60.8 180.5 %all-gather.39.cloned.1.call-start = ((), (), s32[]{:S(2)}) async-start(), calls=%async_computation.21 | async-start | bytes 7077888 | tf_op jit(solution)/shard_map/all_gather | solution.py:95
  63.5 24.2 %collective-permute-start.21 = (bf16[128,1024]{1,0:T(8,128)(2,1)S(1)}, bf16[128,1024]{1,0:T(8,128)(2,1)S(1)}, u32[]{:S(2)}, u32[]{:S(2)}) collective-permute-start(bf16[128,1024]{1,0:T(8,128)(2,1)S(1)} %constant_dynamic-slice_fusion), channel_id=1, source_target_pairs={{0,2},{1,3},{2,0},{3,1},{4,6},{5,7},{6,4},{7,5},{8,10},{9,11},{10,... | collective-permute-start | bytes 786440 | tf_op jit(solution)/shard_map/ppermute | solution.py:69
  88.7 199.9 %all-gather.37.cloned.1.call-start = ((), (), s32[]{:S(2)}) async-start(), calls=%async_computation.20 | async-start | bytes 7077888 | tf_op jit(solution)/shard_map/all_gather | solution.py:95
  92.7 25.2 %collective-permute-start.18 = (bf16[128,1024]{1,0:T(8,128)(2,1)S(1)}, bf16[128,1024]{1,0:T(8,128)(2,1)S(1)}, u32[]{:S(2)}, u32[]{:S(2)}) collective-permute-start(bf16[128,1024]{1,0:T(8,128)(2,1)S(1)} %constant_dynamic-slice_fusion.1), channel_id=1, source_target_pairs={{0,2},{1,3},{2,0},{3,1},{4,6},{5,7},{6,4},{7,5},{8,10},{9,11},{10,... | collective-permute-start | bytes 786440 | tf_op jit(solution)/shard_map/ppermute | solution.py:69
  94.4 23.5 %collective-permute-start.17 = (bf16[128,1024]{1,0:T(8,128)(2,1)S(1)}, bf16[128,1024]{1,0:T(8,128)(2,1)S(1)}, u32[]{:S(2)}, u32[]{:S(2)}) collective-permute-start(bf16[128,1024]{1,0:T(8,128)(2,1)S(1)} %constant_dynamic-slice_fusion.1), channel_id=1, source_target_pairs={{0,1},{1,2},{2,3},{3,0},{4,5},{5,6},{6,7},{7,4},{8,9},{9,10},{10,1... | collective-permute-start | bytes 786440 | tf_op jit(solution)/shard_map/ppermute | solution.py:69
  118.9 307.5 %reduce-scatter.11.cloned.1.call-start = ((), (), s32[]{:S(2)}) async-start(), calls=%async_computation.11 | async-start | bytes 4718592 | tf_op jit(solution)/shard_map/reduce_scatter | solution.py:104
  147.7 32.2 %collective-permute-start.10 = (bf16[512,1024]{1,0:T(8,128)(2,1)}, bf16[512,1024]{1,0:T(8,128)(2,1)}, u32[]{:S(2)}, u32[]{:S(2)}) collective-permute-start(bf16[512,1024]{1,0:T(8,128)(2,1)} %get-tuple-element.73), channel_id=1, source_target_pairs={{0,1},{2,3},{4,5},{6,7},{8,9},{10,11},{12,13},{14,15},{16,17},{18,... | collective-permute-start | bytes 3145736 | tf_op jit(solution)/shard_map/ppermute | solution.py:316
  338.2 107.2 %reduce-scatter.15.cloned.1.call-start = ((), (), s32[]{:S(2)}) async-start(), calls=%async_computation.14 | async-start | bytes 4718592 | tf_op jit(solution)/shard_map/reduce_scatter | solution.py:104
  353.6 147.1 %reduce-scatter.17.cloned.1.call-start = ((), (), s32[]{:S(2)}) async-start(), calls=%async_computation.16 | async-start | bytes 4718592 | tf_op jit(solution)/shard_map/reduce_scatter | solution.py:104
  374.8 182.3 %reduce-scatter.13.cloned.1.call-start = ((), (), s32[]{:S(2)}) async-start(), calls=%async_computation.13 | async-start | bytes 5013504 | tf_op jit(solution)/shard_map/reduce_scatter | solution.py:104
  401.1 230.8 %reduce-scatter.7.cloned.1.call-start = ((), (), s32[]{:S(2)}) async-start(), calls=%async_computation.7 | async-start | bytes 9437184 | tf_op jit(solution)/shard_map/reduce_scatter | solution.py:104
  414.3 292.5 %reduce-scatter.9.cloned.1.call-start = ((), (), s32[]{:S(2)}) async-start(), calls=%async_computation.9 | async-start | bytes 9437184 | tf_op jit(solution)/shard_map/reduce_scatter | solution.py:104
  426.3 325.3 %all-gather.27.cloned.1.call-start = ((), (), s32[]{:S(2)}) async-start(), calls=%async_computation.12 | async-start | bytes 1179648 | tf_op jit(solution)/shard_map/all_gather | solution.py:465
  441.0 317.7 %all-gather.29.cloned.1.call-start = ((), (), s32[]{:S(2)}) async-start(), calls=%async_computation.15 | async-start | bytes 1179648 | tf_op jit(solution)/shard_map/all_gather | solution.py:465
  447.1 58.6 %collective-permute-start.42 = (bf16[64,1024]{1,0:T(8,128)(2,1)S(1)}, bf16[64,1024]{1,0:T(8,128)(2,1)S(1)}, u32[]{:S(2)}, u32[]{:S(2)}) collective-permute-start(bf16[64,1024]{1,0:T(8,128)(2,1)S(1)} %get-tuple-element.91), channel_id=1, source_target_pairs={{0,1},{1,2},{2,3},{3,0},{4,5},{5,6},{6,7},{7,4},{8,9},{9,10},{10,1... | collective-permute-start | bytes 393224 | tf_op jit(solution)/shard_map/ppermute | solution.py:69
  448.6 58.5 %collective-permute-start.41 = (bf16[64,1024]{1,0:T(8,128)(2,1)}, bf16[64,1024]{1,0:T(8,128)(2,1)S(1)}, u32[]{:S(2)}, u32[]{:S(2)}) collective-permute-start(bf16[64,1024]{1,0:T(8,128)(2,1)} %get-tuple-element.92), channel_id=1, source_target_pairs={{0,2},{1,3},{2,0},{3,1},{4,6},{5,7},{6,4},{7,5},{8,10},{9,11},{10,... | collective-permute-start | bytes 393224 | tf_op jit(solution)/shard_map/ppermute | solution.py:69
  451.0 56.1 %collective-permute-start.40 = (bf16[64,1024]{1,0:T(8,128)(2,1)S(1)}, bf16[64,1024]{1,0:T(8,128)(2,1)S(1)}, u32[]{:S(2)}, u32[]{:S(2)}) collective-permute-start(bf16[64,1024]{1,0:T(8,128)(2,1)S(1)} %get-tuple-element.90), channel_id=1, source_target_pairs={{0,3},{1,0},{2,1},{3,2},{4,7},{5,4},{6,5},{7,6},{8,11},{9,8},{10,9... | collective-permute-start | bytes 393224 | tf_op jit(solution)/shard_map/ppermute | solution.py:69
  501.8 60.4 %collective-permute-start.45 = (bf16[64,1024]{1,0:T(8,128)(2,1)S(1)}, bf16[64,1024]{1,0:T(8,128)(2,1)S(1)}, u32[]{:S(2)}, u32[]{:S(2)}) collective-permute-start(bf16[64,1024]{1,0:T(8,128)(2,1)S(1)} %get-tuple-element.94), channel_id=1, source_target_pairs={{0,1},{1,2},{2,3},{3,0},{4,5},{5,6},{6,7},{7,4},{8,9},{9,10},{10,1... | collective-permute-start | bytes 393224 | tf_op jit(solution)/shard_map/ppermute | solution.py:69
  503.3 60.3 %collective-permute-start.44 = (bf16[64,1024]{1,0:T(8,128)(2,1)S(1)}, bf16[64,1024]{1,0:T(8,128)(2,1)S(1)}, u32[]{:S(2)}, u32[]{:S(2)}) collective-permute-start(bf16[64,1024]{1,0:T(8,128)(2,1)S(1)} %get-tuple-element.95), channel_id=1, source_target_pairs={{0,2},{1,3},{2,0},{3,1},{4,6},{5,7},{6,4},{7,5},{8,10},{9,11},{10,... | collective-permute-start | bytes 393224 | tf_op jit(solution)/shard_map/ppermute | solution.py:69
  505.7 57.9 %collective-permute-start.43 = (bf16[64,1024]{1,0:T(8,128)(2,1)S(1)}, bf16[64,1024]{1,0:T(8,128)(2,1)S(1)}, u32[]{:S(2)}, u32[]{:S(2)}) collective-permute-start(bf16[64,1024]{1,0:T(8,128)(2,1)S(1)} %get-tuple-element.93), channel_id=1, source_target_pairs={{0,3},{1,0},{2,1},{3,2},{4,7},{5,4},{6,5},{7,6},{8,11},{9,8},{10,9... | collective-permute-start | bytes 393224 | tf_op jit(solution)/shard_map/ppermute | solution.py:69
  508.9 367.1 %all-gather.43.cloned.1.call-start = ((), (), s32[]{:S(2)}) async-start(), calls=%async_computation.23 | async-start | bytes 4866048 | tf_op jit(solution)/shard_map/all_gather | solution.py:484
  574.0 334.8 %all-gather.23.cloned.1.call-start = ((), (), s32[]{:S(2)}) async-start(), calls=%async_computation.8 | async-start | bytes 2359296 | tf_op jit(solution)/shard_map/all_gather | solution.py:465
  656.3 282.6 %all-gather.25.cloned.1.call-start = ((), (), s32[]{:S(2)}) async-start(), calls=%async_computation.10 | async-start | bytes 2359296 | tf_op jit(solution)/shard_map/all_gather | solution.py:465
  731.3 580.4 %all-gather.41.cloned.1.call-start = ((), (), s32[]{:S(2)}) async-start(), calls=%async_computation.22 | async-start | bytes 18874368 | tf_op jit(solution)/shard_map/all_gather | solution.py:502
  946.7 28.9 %collective-permute-start.48 = (bf16[1024,1024]{1,0:T(8,128)(2,1)S(1)}, bf16[1024,1024]{1,0:T(8,128)(2,1)S(1)}, u32[]{:S(2)}, u32[]{:S(2)}) collective-permute-start(bf16[1024,1024]{1,0:T(8,128)(2,1)S(1)} %get-tuple-element.70), channel_id=1, source_target_pairs={{8,11},{9,8},{10,9},{11,10},{0,3},{1,0},{2,1},{3,2}} | collective-permute-start | bytes 6291464 | tf_op jit(solution)/shard_map/ppermute | solution.py:115
  952.0 91.0 %collective-permute-start.47 = (bf16[1024,1024]{1,0:T(8,128)(2,1)S(1)}, bf16[1024,1024]{1,0:T(8,128)(2,1)S(1)}, u32[]{:S(2)}, u32[]{:S(2)}) collective-permute-start(bf16[1024,1024]{1,0:T(8,128)(2,1)S(1)} %get-tuple-element.70), channel_id=1, source_target_pairs={{8,10},{9,11},{10,8},{11,9},{0,2},{1,3},{2,0},{3,1}} | collective-permute-start | bytes 6291464 | tf_op jit(solution)/shard_map/ppermute | solution.py:115
  953.9 90.4 %collective-permute-start.46 = (bf16[1024,1024]{1,0:T(8,128)(2,1)S(1)}, bf16[1024,1024]{1,0:T(8,128)(2,1)}, u32[]{:S(2)}, u32[]{:S(2)}) collective-permute-start(bf16[1024,1024]{1,0:T(8,128)(2,1)S(1)} %get-tuple-element.70), channel_id=1, source_target_pairs={{8,9},{9,10},{10,11},{11,8},{0,1},{1,2},{2,3},{3,0}} | collective-permute-start | bytes 6291464 | tf_op jit(solution)/shard_map/ppermute | solution.py:115
  1219.8 44.0 %collective-permute-start.23 = (bf16[512,1024]{1,0:T(8,128)(2,1)}, bf16[512,1024]{1,0:T(8,128)(2,1)}, u32[]{:S(2)}, u32[]{:S(2)}) collective-permute-start(bf16[512,1024]{1,0:T(8,128)(2,1)} %slice.444), channel_id=1, source_target_pairs={{1,0},{3,2},{5,4},{7,6},{9,8},{11,10},{13,12},{15,14},{17,16},{19,... | collective-permute-start | bytes 3145736 | tf_op jit(solution)/shard_map/ppermute | solution.py:397
  (159 other events, 2057.9 us)
Sparse Core Ops, SparseCore 0:
  26.4 32.5 all-gather.32
  61.5 32.3 all-gather.30
  96.3 32.3 all-gather.34
  132.0 63.6 all-gather.20
  197.4 43.8 all-gather.38
  243.0 45.5 all-gather.36
  338.3 51.3 reduce-scatter.10
  394.1 51.3 reduce-scatter.14
  449.4 51.3 reduce-scatter.16
  504.4 52.6 reduce-scatter.12
  560.6 71.2 reduce-scatter.6
  635.6 71.2 reduce-scatter.8
  709.4 23.4 all-gather.26
  735.2 23.4 all-gather.28
  762.0 113.9 all-gather.42
  878.3 30.3 all-gather.22
  911.0 27.8 all-gather.24
  1209.0 89.4 all-gather.40

commit v2 on v1

--- a/solution.py
+++ b/solution.py
@@ -16,7 +16,6 @@
 LANES = 128
 SUBS = D // LANES
 
-HIGH = lax.Precision.HIGH
 POLY_A = 3.4445
 POLY_B = -4.775
 POLY_C = 2.0315
@@ -47,10 +46,6 @@
     return lax.dot_general(
         left, right, (((0,), (0,)), ((), ())), preferred_element_type=jnp.float32
     )
-
-
-def times_high(left, right):
-    return jnp.dot(left, right, precision=HIGH, preferred_element_type=jnp.float32)
 
 
 def silu_grad(value):
@@ -88,37 +83,194 @@
     return lax.dynamic_slice_in_dim(block, lax.axis_index("dp") * share, share, 0)
 
 
-def gathered_weight(block):
-    dp = lax.axis_size("dp")
-    share = block.shape[0] // dp
-    far = jnp.stack(others_blocks(own_slice(block)))
-    far = lax.all_gather(far, "dp", axis=0, tiled=False)
-    near = block.reshape(dp, 1, share, block.shape[1])
-    return jnp.concatenate([near, far], axis=1).reshape(-1, block.shape[1])
-
-
-def summed_share(grad):
+def across(x, bit):
+    return lax.ppermute(x, "dp", [(i, i ^ bit) for i in range(lax.axis_size("dp"))])
+
+
+def chip_bits():
+    bits = []
+    bit = 2
+    while bit < lax.axis_size("dp"):
+        bits.append(bit)
+        bit *= 2
+    return bits, bits[::-1]
+
+
+def own_bit(bit):
+    return lax.rem(lax.axis_index("dp") // bit, 2)
+
+
+def pick(x, axis, index):
+    return lax.dynamic_index_in_dim(x, index, axis, keepdims=False)
+
+
+def add_half(left, right):
+    return as_half(left.astype(jnp.float32) + right.astype(jnp.float32))
+
+
+class Flight:
+    def __init__(self, make, given, beside):
+        given, beside = lax.optimization_barrier((given, beside))
+        self.steps = make(given)
+        self.result = None
+        sent, self.moving = next(self.steps)
+        self.beside, _ = lax.optimization_barrier((beside, sent))
+
+    def advance(self, beside):
+        moving, beside = lax.optimization_barrier((self.moving, beside))
+        try:
+            sent, self.moving = self.steps.send(moving)
+        except StopIteration as end:
+            self.result = end.value
+            return beside
+        beside, _ = lax.optimization_barrier((beside, sent))
+        return beside
+
+    def finish(self):
+        while self.result is None:
+            try:
+                _, self.moving = self.steps.send(self.moving)
+            except StopIteration as end:
+                self.result = end.value
+        return self.result
+
+
+def tied(value, beside):
+    return lax.optimization_barrier((value, beside))
+
+
+def near_gather(blocks):
+    count = len(blocks)
+    slices = blocks
+    share = slices[0].shape[0] // 2
+    own = jnp.concatenate([item[:share] for item in slices] + [item[share:] for item in slices], axis=0)
+    others = yield [own], others_blocks(own)
+    held = jnp.stack([own] + others)
+    held = held.reshape(held.shape[0], 2, count, share, -1)
+    orders = chip_bits()
+    parts = [held[:, index][None] for index in range(2)]
+    for step in reversed(range(len(orders[0]))):
+        there = yield parts, [across(part, order[step]) for part, order in zip(parts, orders)]
+        parts = [jnp.concatenate(pair, axis=0) for pair in zip(parts, there)]
+    both = jnp.stack(parts)
+    (there,) = yield [both], [across(both, 1)]
+    both = jnp.stack([both, there])
+    return [both[:, :, :, :, i].reshape(-1, both.shape[-1]) for i in range(count)]
+
+
+def along_pieces(pieces):
+    count = pieces.shape[0]
+    moving = yield [pieces], [turned(pieces[k], -k) for k in range(1, count)]
+    total = pieces[0].astype(jnp.float32)
+    for item in moving:
+        total = total + item.astype(jnp.float32)
+    return total
+
+
+def near_sum(grad):
     count = lax.axis_size("seq")
-    dp = lax.axis_size("dp")
-    share = grad.shape[0] // (dp * count)
-    part = lax.psum_scatter(grad, "dp", scatter_dimension=0, tiled=True)
-    part = part.reshape(count, share, grad.shape[1])
-    total = part[0].astype(jnp.float32)
-    for k in range(1, count):
-        total = total + turned(part[k], -k).astype(jnp.float32)
-    return total
+    middle = grad.shape[0] // 2
+    (there,) = yield [grad], [across(grad[middle:], 1)]
+    cut = middle // 2
+    orders = chip_bits()
+    parts = [
+        (grad[:cut], there[:cut]),
+        (grad[cut:middle], there[cut:]),
+    ]
+    for step in range(len(orders[0])):
+        keep, send = [], []
+        for mine, theirs in parts:
+            rows = mine.shape[0] // 2
+            send.append(add_half(mine[rows:], theirs[rows:]))
+            keep.append(add_half(mine[:rows], theirs[:rows]))
+        there = yield send, [across(item, order[step]) for item, order in zip(send, orders)]
+        parts = list(zip(keep, there))
+    pieces = jnp.concatenate(
+        [add_half(mine, theirs).reshape(count, -1, mine.shape[1]) for mine, theirs in parts], axis=1
+    )
+    return (yield from along_pieces(pieces))
+
+
+def far_gather(held):
+    return lax.all_gather(held, "dp", axis=0, tiled=False).reshape(-1, held.shape[-1])
+
+
+def far_sum(grad):
+    count = lax.axis_size("seq")
+    (part,) = yield [grad], [lax.psum_scatter(grad, "dp", scatter_dimension=0, tiled=True)]
+    return (yield from along_pieces(part.reshape(count, -1, grad.shape[1])))
+
+
+def whole_gather(slices):
+    count, dp = lax.axis_size("seq"), lax.axis_size("dp")
+    orders = chip_bits()
+    others = yield slices, [others_blocks(item) for item in slices]
+    parts = [in_order(own[None], [item[None] for item in rest]) for own, rest in zip(slices, others)]
+    axes = [[], []]
+    for step in list(reversed(range(len(orders[0])))) + [None]:
+        bits = [1 if step is None else order[step] for order in orders]
+        there = yield parts, [across(part, bit) for part, bit in zip(parts, bits)]
+        for index, bit in enumerate(bits):
+            mine = own_bit(bit) == 0
+            ours, theirs = parts[index], there[index]
+            parts[index] = jnp.stack([jnp.where(mine, ours, theirs), jnp.where(mine, theirs, ours)])
+            axes[index].insert(0, bit)
+    full = []
+    for part, names in zip(parts, axes):
+        bits = len(names)
+        wanted = sorted(names, reverse=True)
+        part = jnp.transpose(part, [bits] + [names.index(bit) for bit in wanted] + [bits + 1, bits + 2])
+        full.append(part.reshape(-1, part.shape[-1]))
+    return full
+
+
+def whole_sum(grads):
+    count, dp = lax.axis_size("seq"), lax.axis_size("dp")
+    orders = chip_bits()
+    mine = own_bit(1)
+    parts = [jnp.swapaxes(g.reshape(count, dp // 2, 2, -1, g.shape[1]), 0, 1) for g in grads]
+    send = [pick(part, 2, 1 - mine) for part in parts]
+    there = yield send, [across(item, 1) for item in send]
+    high = sorted(orders[0], reverse=True)
+    split = (2,) * len(high)
+    parts = [
+        (pick(part, 2, mine).reshape(split + item.shape[1:]), item.reshape(split + item.shape[1:]))
+        for part, item in zip(parts, there)
+    ]
+    axes = [list(high), list(high)]
+    for step in range(len(high)):
+        keep, send, moving = [], [], []
+        for (ours, theirs), order, names in zip(parts, orders, axes):
+            bit = order[step]
+            axis = names.index(bit)
+            names.remove(bit)
+            here = own_bit(bit)
+            send.append(add_half(pick(ours, axis, 1 - here), pick(theirs, axis, 1 - here)))
+            keep.append(add_half(pick(ours, axis, here), pick(theirs, axis, here)))
+            moving.append(across(send[-1], bit))
+        there = yield send, moving
+        parts = list(zip(keep, there))
+    both = jnp.concatenate([add_half(ours, theirs) for ours, theirs in parts], axis=2)
+    seq_index = lax.axis_index("seq")
+    pieces = jnp.stack(
+        [pick(both, 0, lax.rem(seq_index - k + count, count)) for k in range(count)]
+    )
+    return (yield from along_pieces(pieces))
 
 
 def in_columns(block, slots):
     count = lax.axis_size("seq")
-    return [
-        lax.ppermute(
-            block,
-            ("dp", "seq"),
-            [(s * count + i, s * count + (i + k) % count) for s in slots for i in range(count)],
-        )
-        for k in range(1, count)
-    ]
+    up = [(s * count + i, s * count + i + 1) for s in slots for i in range(count - 1)]
+    down = [(j, i) for i, j in up]
+    held = [block]
+    above = below = block
+    for _ in range(count - 1):
+        below, above = yield [below, above], [
+            lax.ppermute(below, ("dp", "seq"), up),
+            lax.ppermute(above, ("dp", "seq"), down),
+        ]
+        held += [below, above]
+    return held
 
 
 def summed_small(x):
@@ -245,18 +397,105 @@
     return total
 
 
-def orthogonal_factor(gram_raw):
-    scale = 1.0 / (jnp.sqrt(jnp.trace(gram_raw)) + 1e-07)
-    gram = gram_raw * (scale * scale)
-    eye = jnp.eye(gram.shape[0], dtype=jnp.float32)
-    factor = None
-    for step in range(NS_STEPS):
-        square = times_high(gram, gram)
-        poly = POLY_A * eye + POLY_B * gram + POLY_C * square
-        factor = poly * scale if factor is None else times_high(factor, poly)
-        if step + 1 < NS_STEPS:
-            gram = times_high(times_high(gram, poly), poly)
-    return factor
+SIDE = 256
+
+
+def split_half(value):
+    high = value.astype(jnp.bfloat16)
+    return high, (value - high.astype(jnp.float32)).astype(jnp.bfloat16)
+
+
+def factor_kernel(gram_ref, high_ref, low_ref, a_ref, p_ref, t_ref, q_ref):
+    side = gram_ref.shape[0]
+    count = side // SIDE
+
+    def rows_of(i):
+        return slice(i * SIDE, (i + 1) * SIDE)
+
+    def put(ref, i, strip, lead=()):
+        for part, value in enumerate(split_half(strip)):
+            ref[lead + (part, rows_of(i), slice(i * SIDE, side))] = value
+        for j in range(i + 1, count):
+            block = strip[:, (j - i) * SIDE : (j - i + 1) * SIDE].T
+            for part, value in enumerate(split_half(block)):
+                ref[lead + (part, rows_of(j), rows_of(i))] = value
+
+    def strip_of(left, right, i):
+        lh, ll = left[0, rows_of(i), :], left[1, rows_of(i), :]
+        rh, rl = right[0, :, i * SIDE :], right[1, :, i * SIDE :]
+        total = jnp.dot(lh, rl, preferred_element_type=jnp.float32)
+        total = total + jnp.dot(ll, rh, preferred_element_type=jnp.float32)
+        return total + jnp.dot(lh, rh, preferred_element_type=jnp.float32)
+
+    def diagonal(i, width):
+        shape = (SIDE, width)
+        return lax.broadcasted_iota(jnp.int32, shape, 0) == lax.broadcasted_iota(
+            jnp.int32, shape, 1
+        )
+
+    trace = jnp.zeros((1, 1), jnp.float32)
+    for i in range(count):
+        block = gram_ref[rows_of(i), rows_of(i)]
+        block = jnp.where(diagonal(i, SIDE), block, 0.0)
+        trace = trace + jnp.sum(jnp.sum(block, axis=0, keepdims=True), axis=1, keepdims=True)
+    scale = 1.0 / (jnp.sqrt(trace) + 1e-07)
+    for i in range(count):
+        for part, value in enumerate(split_half(gram_ref[rows_of(i), :] * (scale * scale))):
+            a_ref[part, rows_of(i), :] = value
+
+    def step(k, carry):
+        for i in range(count):
+            width = side - i * SIDE
+            now = a_ref[0, rows_of(i), i * SIDE :].astype(jnp.float32)
+            now = now + a_ref[1, rows_of(i), i * SIDE :].astype(jnp.float32)
+            strip = POLY_B * now + POLY_C * strip_of(a_ref, a_ref, i)
+            put(p_ref, i, jnp.where(diagonal(i, width), strip + POLY_A, strip))
+
+        @pl.when(k < NS_STEPS - 1)
+        def _():
+            for i in range(count):
+                put(t_ref, i, strip_of(a_ref, p_ref, i))
+            for i in range(count):
+                put(a_ref, i, strip_of(t_ref, p_ref, i))
+
+        there = lax.rem(k, 2)
+
+        @pl.when(k == 0)
+        def _():
+            q_ref[0] = p_ref[...]
+
+        @pl.when(k > 0)
+        def _():
+            for i in range(count):
+                put(q_ref, i, strip_of(q_ref.at[1 - there], p_ref, i), (there,))
+
+        return carry
+
+    lax.fori_loop(0, NS_STEPS, step, 0)
+    last = (NS_STEPS - 1) % 2
+    for i in range(count):
+        value = q_ref[last, 0, rows_of(i), :].astype(jnp.float32)
+        value = (value + q_ref[last, 1, rows_of(i), :].astype(jnp.float32)) * scale
+        high_ref[rows_of(i), :], low_ref[rows_of(i), :] = split_half(value)
+
+
+def orthogonal_factor(gram):
+    side = gram.shape[0]
+    pair = (2, side, side)
+    return pl.pallas_call(
+        factor_kernel,
+        out_shape=(jax.ShapeDtypeStruct(gram.shape, jnp.bfloat16),) * 2,
+        scratch_shapes=[
+            pltpu.VMEM(pair, jnp.bfloat16),
+            pltpu.VMEM(pair, jnp.bfloat16),
+            pltpu.VMEM(pair, jnp.bfloat16),
+            pltpu.VMEM((2,) + pair, jnp.bfloat16),
+        ],
+        compiler_params=pltpu.CompilerParams(vmem_limit_bytes=56 * 1024 * 1024),
+        cost_estimate=pl.CostEstimate(
+            flops=17 * 4 * side**3, bytes_accessed=8 * side * side, transcendentals=0
+        ),
+    )(gram)
 
 
 def body(tokens, cotangent, lengths, *rest):
@@ -270,7 +509,11 @@
     dp_index = lax.axis_index("dp")
     rows = tokens.shape[0]
 
-    half = {name: as_half(masters[name]) for name in order}
+    half = {name: as_half(own_slice(masters[name])) for name in order}
+    far_own = jnp.concatenate([half["up"], half["down"]], axis=0)
+    far_held = jnp.stack([far_own] + others_blocks(far_own))
+    cut = half["up"].shape[0]
+    full = {"up": far_gather(far_held[:, :cut]), "down": far_gather(far_held[:, cut:])}
     small = jnp.concatenate(
         [
             channel_params,
@@ -284,14 +527,7 @@
     query_set = small_all.reshape(seq_count, -1, small_all.shape[1])[
         :, : query_params.shape[0], channel_params.shape[1] :
     ].reshape(Z, 3)
-    full = {"v": gathered_weight(half["v"])}
-    wide_block = jnp.concatenate([half["z"], half["phi"], half["h"]], axis=1)
-    wide_full = lax.all_gather(own_slice(wide_block), ("seq", "dp"), axis=0, tiled=True)
-    full["z"] = wide_full[:, :Z]
-    full["phi"] = wide_full[:, Z : Z + D]
-    full["h"] = wide_full[:, Z + D :]
-    for name in ("g", "u", "up", "down"):
-        full[name] = gathered_weight(half[name])
+    get_v = Flight(near_gather, [half["v"]], small)
 
     gain_one = channel[:, 0]
     gain_two = channel[:, 1]
@@ -309,12 +545,11 @@
     inputs = tokens.astype(jnp.float32)
     weighted = cotangent.astype(jnp.float32) * keep
     back_ffn = as_half(weighted)
+    evens = [(i, i + 1) for i in range(0, seq_count - 1, 2)]
+    odds = [(i + 1, i) for i in range(0, seq_count - 1, 2)]
+
     normed, norm_back_one = jax.vjp(norm_rows, inputs, gain_one)
     normed_low = as_half(normed)
-    evens = [(i, i + 1) for i in range(0, seq_count - 1, 2)]
-    odds = [(i + 1, i) for i in range(0, seq_count - 1, 2)]
-    normed_both = jnp.concatenate([lax.ppermute(normed_low, "seq", evens), normed_low], axis=0)
-
     inject_rate = jax.nn.sigmoid(alpha)
     damp = jax.nn.sigmoid(delta)
     decay = 1.0 - inject_rate * damp
@@ -325,43 +560,74 @@
     ends = local_call(
         ema_end_kernel, f32_shape(NE, SUBS, LANES), 2 * rows * NE * D, 4 * rows * D, normed_tiled, decay_tiled
     )
+    normed_there = lax.ppermute(normed_low, "seq", evens)
+    clock = get_v.advance(ends)
+    ends = clock
+    zphi_slice = jnp.concatenate([half["z"], half["phi"]], axis=1)
+    get_wide = Flight(whole_gather, [zphi_slice, half["h"]], clock)
+    clock = get_v.advance(get_wide.beside)
     start = carried(ends, decay_all, True)
+    clock = get_wide.advance(clock)
+    clock = get_v.advance(clock)
+    start, clock = tied(start, clock)
+    ema_out = local_call(
+        ema_run_kernel,
+        f32_shape(rows, SUBS, LANES),
+        4 * rows * NE * D,
+        8 * rows * D,
+        normed_tiled,
+        decay_tiled,
+        mix_tiled,
+        start,
+    )
+    ema_out, clock = tied(ema_out, clock)
+    clock = get_wide.advance(clock)
+    clock = get_v.advance(clock)
+    (full["v"],) = get_v.finish()
+    normed_both = jnp.concatenate([normed_there, normed_low], axis=0)
+    normed_both, clock = tied(normed_both, clock)
     v_pre = times_right(normed_both, full["v"])
     values_all = as_half(jax.nn.silu(v_pre))
-    ema = flat(
-        local_call(
-            ema_run_kernel,
-            f32_shape(rows, SUBS, LANES),
-            4 * rows * NE * D,
-            8 * rows * D,
-            normed_tiled,
-            decay_tiled,
-            mix_tiled,
-            start,
-        )
-    )
-    mix_pre = ema + omega * normed
+    values_all, clock = tied(values_all, clock)
+    clock = get_wide.advance(clock)
+    get_near = Flight(near_gather, [half["g"], half["u"]], clock)
+    clock = get_wide.advance(get_near.beside)
+    zphi_full, full["h"] = get_wide.finish()
+    full["z"], full["phi"] = zphi_full[:, :Z], zphi_full[:, Z:]
+    ema_out, clock = tied(ema_out, clock)
+    mix_pre = flat(ema_out) + omega * normed
     mixed_low = as_half(jax.nn.silu(mix_pre))
     z_pre = times_plain(mixed_low, full["z"])
     zed = jax.nn.silu(z_pre)
     queries_low = as_half(zed * scale_q + shift_q)
     keys_low = as_half(zed * scale_k)
-    keys_all = jnp.concatenate([lax.ppermute(keys_low, "seq", evens), keys_low], axis=0)
+    keys_there = lax.ppermute(keys_low, "seq", evens)
+    phi = jax.nn.sigmoid(times_plain(mixed_low, full["phi"]))
+    h_part = times_plain(mixed_low, full["h"])
+    keys_there, h_part, clock = lax.optimization_barrier((keys_there, h_part, clock))
+    clock = get_near.advance(clock)
+    keys_all = jnp.concatenate([keys_there, keys_low], axis=0)
     odd_device = seq_index % 2 == 1
     query_place = jnp.arange(rows)[:, None]
     key_place = jnp.arange(2 * rows)[None, :]
     allowed = jnp.where(key_place < rows, odd_device, key_place - rows <= query_place)
+    queries_low, clock = tied(queries_low, clock)
     scores = jnp.where(allowed, times_right(queries_low, keys_all) * score_scale, -1e30)
     top = jnp.max(scores, axis=-1, keepdims=True)
     expo = jnp.exp(scores - top)
     probs = expo / jnp.sum(expo, axis=-1, keepdims=True)
     probs_low = as_half(probs)
     attended = times_plain(probs_low, values_all)
+    attended, clock = tied(attended, clock)
+    clock = get_near.advance(clock)
+    clock = get_near.advance(clock)
+    clock = get_near.advance(clock)
+    full["g"], full["u"] = get_near.finish()
+    mixed_low, clock = tied(mixed_low, clock)
     gam_pre = times_right(mixed_low, full["g"])
     gamma = jax.nn.silu(gam_pre)
     gated_low = as_half(gamma * attended)
-    phi = jax.nn.sigmoid(times_plain(mixed_low, full["phi"]))
-    h_pre = times_plain(mixed_low, full["h"]) + times_plain(gated_low, full["u"])
+    h_pre = h_part + times_plain(gated_low, full["u"])
     cand = jax.nn.silu(h_pre)
     middle = phi * cand + (1.0 - phi) * inputs
     wide, norm_back_two = jax.vjp(norm_rows, middle, gain_two)
@@ -371,54 +637,128 @@
     result = middle + times_plain(active_low, full["down"])
     block_output = as_half(result * keep)
 
-    share = {}
-    share["down"] = summed_share(as_half(times_left(active_low, back_ffn)))
+    def share_of(name, total):
+        return as_half(MOMENTUM * own_slice(moments[name]) + total)
+
+    def kept_rows(shares):
+        packed = jnp.concatenate([item.reshape(-1, D) for item in shares], axis=0)
+        (packed,) = yield [packed], [lax.all_gather(packed, "dp", axis=0, tiled=False)]
+        out, at = [], 0
+        for item in shares:
+            size = item.size // D
+            out.append(packed[:, at : at + size].reshape(-1, item.shape[1]))
+            at += size
+        return out
+
+    def column_rows(names, blocks):
+        height = max(item.shape[0] for item in blocks)
+        own = chosen(names, blocks, height)
+        held = yield from in_columns(own, [SLOT[name] for name in names])
+        mine = held[0]
+        rest = []
+        for k in range(1, seq_count):
+            rest.append(held[2 * k - 1] + held[2 * (seq_count - k)])
+        return jnp.concatenate([mine] + rest, axis=0)
+
+    def chosen(names, blocks, height):
+        out = jnp.zeros((height, D), jnp.bfloat16)
+        for name, item in zip(names, blocks):
+            item = jnp.pad(item, ((0, height - item.shape[0]), (0, D - item.shape[1])))
+            out = jnp.where(dp_index == SLOT[name], item, out)
+        return out
+
+    block = {}
+    orders = chip_bits()
+
+    clock = result
+    grad = as_half(times_left(active_low, back_ffn))
+    sum_down = Flight(far_sum, grad, clock)
+    back_ffn, clock = tied(back_ffn, sum_down.beside)
     d_apre = as_half(times_right(back_ffn, full["down"]) * silu_grad(a_pre))
-    share["up"] = summed_share(as_half(times_left(d_apre, wide_low)))
+    d_apre, clock = tied(d_apre, clock)
+    grad = as_half(times_left(d_apre, wide_low))
+    sum_up = Flight(far_sum, grad, clock)
+    clock = sum_up.beside
+    d_apre, clock = tied(d_apre, clock)
     d_mid_norm, d_gain_two = norm_back_two(times_plain(d_apre, full["up"]))
     d_middle = weighted + d_mid_norm
     d_phipre = as_half(d_middle * (cand - inputs) * phi * (1.0 - phi))
     d_hpre = as_half(d_middle * phi * silu_grad(h_pre))
     tokens_grad = d_middle * (1.0 - phi)
+    d_hpre, clock = tied(d_hpre, clock)
+    grad = as_half(times_left(gated_low, d_hpre))
+    sum_u = Flight(near_sum, grad, clock)
+    d_hpre, clock = tied(d_hpre, sum_u.beside)
     d_gated = times_right(d_hpre, full["u"])
     d_attended = as_half(d_gated * gamma)
     d_gampre = as_half(d_gated * attended * silu_grad(gam_pre))
-    share["u"] = summed_share(as_half(times_left(gated_low, d_hpre)))
-    share["g"] = summed_share(as_half(times_left(d_gampre, mixed_low)))
-
+    d_gampre, clock = tied(d_gampre, clock)
+    clock = sum_u.advance(clock)
+    d_gampre, clock = tied(d_gampre, clock)
+    grad = as_half(times_left(d_gampre, mixed_low))
+    sum_g = Flight(near_sum, grad, clock)
+    d_attended, clock = tied(d_attended, sum_g.beside)
     d_probs = times_right(d_attended, values_all)
     d_scores = as_half(probs * (d_probs - jnp.sum(probs * d_probs, axis=-1, keepdims=True)))
+    d_scores, clock = tied(d_scores, clock)
+    clock = sum_g.advance(clock)
+    d_attended, clock = tied(d_attended, clock)
     d_vpre = as_half(times_left(probs_low, d_attended) * silu_grad(v_pre))
-    share["v"] = summed_share(as_half(times_left(d_vpre, normed_both)))
+    d_vpre, clock = tied(d_vpre, clock)
+    clock = sum_down.advance(clock)
+    clock = sum_u.advance(clock)
+    d_vpre, clock = tied(d_vpre, clock)
+    grad = as_half(times_left(d_vpre, normed_both))
+    sum_v = Flight(near_sum, grad, clock)
+    d_vpre, clock = tied(d_vpre, sum_v.beside)
     d_queries = times_plain(d_scores, keys_all) * score_scale
     d_keys_all = times_left(d_scores, queries_low) * score_scale
-    d_keys = d_keys_all[rows:] + lax.ppermute(d_keys_all[:rows], "seq", odds)
+    d_keys_there = lax.ppermute(d_keys_all[:rows], "seq", odds)
     d_normed_all = times_plain(d_vpre, full["v"])
-    d_normed = d_normed_all[rows:] + lax.ppermute(
-        as_half(d_normed_all[:rows]), "seq", odds
-    ).astype(jnp.float32)
+    d_normed_there = lax.ppermute(as_half(d_normed_all[:rows]), "seq", odds)
+    d_normed_all, clock = tied(d_normed_all, clock)
+    clock = sum_v.advance(clock)
+    clock = sum_g.advance(clock)
+    clock = sum_down.advance(clock)
+    keep_down = Flight(kept_rows, [share_of("down", sum_down.finish())], clock)
+    clock = sum_up.advance(keep_down.beside)
+    d_keys_there, clock = tied(d_keys_there, clock)
+    d_keys = d_keys_all[rows:] + d_keys_there
     d_scale_q = jnp.sum(d_queries * zed, axis=0)
     d_shift_q = jnp.sum(d_queries, axis=0)
     d_scale_k = jnp.sum(d_keys * zed, axis=0)
     d_zpre = as_half((d_queries * scale_q + d_keys * scale_k) * silu_grad(z_pre))
-    d_wide = jnp.concatenate([d_zpre, d_phipre, d_hpre], axis=1)
-    grad_wide = as_half(times_left(mixed_low, d_wide))
-    ordered = grad_wide.reshape(seq_count, dp_count, -1, grad_wide.shape[1])
-    ordered = jnp.stack(
-        [
-            lax.dynamic_index_in_dim(
-                ordered, lax.rem(seq_index - k + seq_count, seq_count), 0, keepdims=False
-            )
-            for k in range(seq_count)
-        ],
-        axis=1,
-    )
-    share_wide = summed_share(ordered.reshape(grad_wide.shape))
-    share["z"] = share_wide[:, :Z]
-    share["phi"] = share_wide[:, Z : Z + D]
-    share["h"] = share_wide[:, Z + D :]
-    d_mixed = times_right(d_wide, wide_full) + times_plain(d_gampre, full["g"])
-
+    d_zphi = jnp.concatenate([d_zpre, d_phipre], axis=1)
+    grads = [as_half(times_left(mixed_low, d_zphi)), as_half(times_left(mixed_low, d_hpre))]
+    sum_wide = Flight(whole_sum, grads, clock)
+    clock = sum_v.advance(sum_wide.beside)
+    clock = sum_u.advance(clock)
+    clock = sum_up.advance(clock)
+    keep_up = Flight(kept_rows, [share_of("up", sum_up.finish())], clock)
+    clock = sum_g.advance(keep_up.beside)
+    clock = sum_wide.advance(clock)
+    d_zphi, clock = tied(d_zphi, clock)
+    d_mixed = (
+        times_right(d_zphi, zphi_full)
+        + times_right(d_hpre, full["h"])
+        + times_plain(d_gampre, full["g"])
+    )
+    d_mixed, clock = tied(d_mixed, clock)
+    clock = sum_v.advance(clock)
+    clock = sum_g.advance(clock)
+    clock = sum_wide.advance(clock)
+    keep_near = Flight(
+        kept_rows, [share_of("u", sum_u.finish()), share_of("g", sum_g.finish())], clock
+    )
+    clock = keep_down.advance(keep_near.beside)
+    clock = keep_up.advance(clock)
+    (block["down"],), (block["up"],) = keep_down.finish(), keep_up.finish()
+    column_one = Flight(
+        lambda x: column_rows(("down", "up"), x), [block["down"], block["up"]], clock
+    )
+    clock = sum_v.advance(column_one.beside)
+    keep_v = Flight(kept_rows, [share_of("v", sum_v.finish())], clock)
+    d_mixed, clock = tied(d_mixed, keep_v.beside)
     d_ema = d_mixed * silu_grad(mix_pre)
     d_ema_tiled = tiled(d_ema)
     state_shape = f32_shape(NE, SUBS, LANES)
@@ -432,7 +772,26 @@
         decay_tiled,
         start,
     )
+    first, clock = tied(first, clock)
+    clock = sum_wide.advance(clock)
+    clock = column_one.advance(clock)
     behind = carried(first, decay_all, False)
+    clock = keep_near.advance(clock)
+    block["u"], block["g"] = keep_near.finish()
+    clock = sum_wide.advance(clock)
+    share_wide = sum_wide.finish()
+    keep_wide = Flight(
+        kept_rows,
+        [
+            share_of("phi", share_wide[:, Z : Z + D]),
+            share_of("h", share_wide[:, Z + D :]),
+            share_of("z", share_wide[:, :Z]),
+        ],
+        clock,
+    )
+    clock = keep_v.advance(keep_wide.beside)
+    (block["v"],) = keep_v.finish()
+    behind, clock = tied(behind, clock)
     d_normed_ema = flat(
         local_call(
             ema_back_kernel,
@@ -445,6 +804,61 @@
             behind,
         )
     )
+    d_normed_ema, clock = tied(d_normed_ema, clock)
+    clock = column_one.advance(clock)
+    clock = keep_wide.advance(clock)
+    block["phi"], block["h"], block["z"] = keep_wide.finish()
+    column_two = Flight(lambda x: column_rows(("u", "g"), x), [block["u"], block["g"]], clock)
+    column_three = Flight(
+        lambda x: column_rows(("phi", "h", "z"), x),
+        [block["phi"], block["h"], block["z"]],
+        column_two.beside,
+    )
+    column_four = Flight(lambda x: column_rows(("v",), x), [block["v"]], column_three.beside)
+    columns_held = [item.finish() for item in (column_one, column_two, column_three, column_four)]
+    momentum = {name: block[name].astype(jnp.float32) for name in order}
+    which = jnp.zeros((), jnp.int32)
+    for index, names in enumerate(
+        (("down", "up"), ("u", "g"), ("phi", "h", "z"), ("v",))
+    ):
+        for name in names:
+            which = jnp.where(dp_index == SLOT[name], index, which)
+    gram = lax.switch(
+        which, [lambda *items, i=i: times_left(items[i], items[i]) for i in range(4)], *columns_held
+    )
+    factor_high, factor_low = orthogonal_factor(gram)
+    height = max(block[name].shape[0] for name in order)
+    item = chosen(order, [block[name] for name in order], height)
+    direction = as_half(times_plain(item, factor_high) + times_plain(item, factor_low))
+    tall, middle_rows, low_rows = (size // seq_count for size in (FF, V, D))
+    there = across(direction, 1)
+    even = own_bit(1) == 0
+    first_item, second_item = jnp.where(even, direction, there), jnp.where(even, there, direction)
+    packed = jnp.where(
+        dp_index < 4,
+        jnp.concatenate([first_item[:tall], second_item[:low_rows]], axis=0),
+        jnp.concatenate(
+            [
+                first_item[:middle_rows],
+                second_item[:middle_rows],
+                jnp.zeros((tall + low_rows - 2 * middle_rows, D), jnp.bfloat16),
+            ],
+            axis=0,
+        ),
+    )
+    packed = pick(packed.reshape(2, -1, D), 0, own_bit(1))
+    packed = lax.all_gather(packed, "dp", axis=0, tiled=True).reshape(-1, tall + low_rows, D)
+    updated = {}
+    for name in order:
+        master = masters[name]
+        chip, core = SLOT[name] // 2, SLOT[name] % 2
+        at = 0 if core == 0 else (tall if chip < 2 else middle_rows)
+        piece = packed[chip, at : at + master.shape[0], : master.shape[1]].astype(jnp.float32)
+        rate = MATRIX_RATE * math.sqrt(master.shape[0] * seq_count / FAN[name])
+        updated[name] = master - rate * piece
+
+    d_normed_ema, direction = tied(d_normed_ema, direction)
+    d_normed = d_normed_all[rows:] + d_normed_there.astype(jnp.float32)
     d_mix = flat(d_mix)
     d_decay = mix * flat(d_state + decay_tiled * behind * state_tail)
     d_eta = d_mix * inject_rate * beta
@@ -455,57 +869,6 @@
     d_omega = jnp.sum(d_ema * normed, axis=0)
     d_input_norm, d_gain_one = norm_back_one(d_normed + d_normed_ema + omega * d_ema)
     tokens_grad = tokens_grad + d_input_norm
-
-    share_low = {}
-    momentum = {}
-    for name in order:
-        share_low[name] = as_half(MOMENTUM * own_slice(moments[name]) + share[name])
-    block = {}
-    for name in ("down", "up", "u", "g", "phi", "h"):
-        block[name] = lax.all_gather(share_low[name], "dp", axis=0, tiled=True)
-        momentum[name] = block[name].astype(jnp.float32)
-
-    def chosen(names, height):
-        out = jnp.zeros((height, D), jnp.bfloat16)
-        for name in names:
-            item = block[name]
-            item = jnp.pad(item, ((0, height - item.shape[0]), (0, D - item.shape[1])))
-            out = jnp.where(dp_index == SLOT[name], item, out)
-        return out
-
-    def gram_of(names):
-        height = max(block[name].shape[0] for name in names)
-        own = chosen(names, height)
-        pieces = [own] + in_columns(own, [SLOT[name] for name in names])
-        return times_left(jnp.concatenate(pieces, axis=0), jnp.concatenate(pieces, axis=0))
-
-    gram = gram_of(("down", "up")) + gram_of(("u", "g", "phi", "h"))
-    late = jnp.concatenate([share_low["v"], share_low["z"].reshape(-1, D)], axis=0)
-    late = lax.all_gather(late, ("seq", "dp"), axis=0, tiled=False)
-    late = late.reshape(seq_count, dp_count, -1, D)
-    cut = share_low["v"].shape[0]
-    all_v = late[:, :, :cut].reshape(seq_count, -1, D)
-    all_z = late[:, :, cut:].reshape(seq_count, -1, Z)
-    block["v"] = lax.dynamic_index_in_dim(all_v, seq_index, 0, keepdims=False)
-    block["z"] = lax.dynamic_index_in_dim(all_z, seq_index, 0, keepdims=False)
-    for name in ("v", "z"):
-        momentum[name] = block[name].astype(jnp.float32)
-    all_v = all_v.reshape(-1, D)
-    all_z = all_z.reshape(-1, Z)
-    gram_v = times_left(all_v, all_v)
-    gram_z = jnp.pad(times_left(all_z, all_z), ((0, D - Z), (0, D - Z)))
-    gram = gram + jnp.where(dp_index == SLOT["v"], gram_v, 0.0)
-    gram = gram + jnp.where(dp_index == SLOT["z"], gram_z, 0.0)
-    factor = as_half(orthogonal_factor(gram))
-    height = max(block[name].shape[0] for name in order)
-    direction = as_half(times_plain(chosen(order, height), factor))
-    directions = lax.all_gather(direction, "dp", axis=0, tiled=False)
-    updated = {}
-    for name in order:
-        master = masters[name]
-        piece = directions[SLOT[name], : master.shape[0], : master.shape[1]].astype(jnp.float32)
-        rate = MATRIX_RATE * math.sqrt(master.shape[0] * seq_count / FAN[name])
-        updated[name] = master - rate * piece
 
     grad_channel = jnp.concatenate(
         [

time: 1350 us -> 978 us (0.72)
  waiting for transfers between devices: 655 us -> 284 us
  matrix products: 349 us -> 153 us
  starting transfers between devices: 101 us -> 184 us
  Pallas kernels: 35.2 us -> 118 us
  other arithmetic: 118 us -> 150 us
  blocking collectives: 19.2 us -> 0 us
  local copies, waits for them, and re-layouts: 42 us -> 60.7 us
    all_gather x12 -> x8, waiting for transfers between devices: 213 us -> 0.08 us  [the longest x5 0.06 us: kept_rows(): lax.all_gather(packed, 'dp', axis=0, tiled=False)]
    reduce_scatter x6 -> x2, waiting for transfers between devices: 209 us -> 46.8 us  [far_sum(): lax.psum_scatter(grad, 'dp', scatter_dimension=0, tiled=True)]
    dot_general x17 -> x0, matrix products: 126 us -> none  [times_high(): jnp.dot(left, right, precision=HIGH, preferred_element_type=jnp.float32)]
    pallas_call x0 -> x1, Pallas kernels: none -> 91.7 us  [orthogonal_factor(): pl.pallas_call(factor_kernel, out_shape=(jax.ShapeDtypeStruct(gram.shape,...]
    ppermute x10 -> x66, starting transfers between devices: 24.9 us -> 97.8 us  [the longest x38 45 us: across(): lax.ppermute(x, 'dp', [(i, i ^ bit) for i in range(lax.axis_size('dp'))])]
    dot_general x12 -> x10, matrix products: 105 us -> 49.7 us  [times_left(): lax.dot_general(left, right, (((0,), (0,)), ((), ())), preferred_element_...]
    add x1 -> x13, other arithmetic: 1 us -> 23.7 us  [the longest x12 23.6 us: column_rows(): rest.append(held[2 * k - 1] + held[2 * (seq_count - k)])]
    ppermute x10 -> x66, waiting for transfers between devices: 95.6 us -> 118 us  [the longest x38 82.4 us: across(): lax.ppermute(x, 'dp', [(i, i ^ bit) for i in range(lax.axis_size('dp'))])]
  transfers between devices with their start and end apart: 79 -> 127, of which waited for: 46 -> 41; matrix products, arithmetic and copies ran while one was open for 19% -> 29% of each run, Pallas kernels for 3% -> 3%
where the time goes in v2:
time: 978 us; the launch traced here: 969 us
  waiting for transfers between devices  284 us (29%)
  starting transfers between devices  184 us (19%)
  matrix products  153 us (16%)
  other arithmetic  150 us (15%)
  Pallas kernels  118 us (12%)
  local copies, waits for them, and re-layouts  60.7 us (6%)
  between operations  18.1 us (2%)
    ppermute x42, waiting for transfers between devices, turned(): lax.ppermute(x, 'seq', [(i, (i + distance) % count) for i in range(count)])  112 us
    pallas_call x1, Pallas kernels, orthogonal_factor(): pl.pallas_call(factor_kernel, out_shape=(jax.ShapeDtypeStruct(gram.shape,...  91.7 us
    ppermute x38, waiting for transfers between devices, across(): lax.ppermute(x, 'dp', [(i, i ^ bit) for i in range(lax.axis_size('dp'))])  82.4 us
    ppermute x42, starting transfers between devices, turned(): lax.ppermute(x, 'seq', [(i, (i + distance) % count) for i in range(count)])  65.3 us
    dot_general x12, matrix products, times_plain(): return jnp.dot(left, right, preferred_element_type=jnp.float32)  55.2 us
    dot_general x10, matrix products, times_left(): lax.dot_general(left, right, (((0,), (0,)), ((), ())), preferred_element_...  49.7 us
    dot_general x9, matrix products, times_right(): lax.dot_general(left, right, (((1,), (1,)), ((), ())), preferred_element_...  48.4 us
    reduce_scatter x2, waiting for transfers between devices, far_sum(): lax.psum_scatter(grad, 'dp', scatter_dimension=0, tiled=True)  46.8 us
  transfers between devices with their start and end apart: 127, of which 41 were waited for; matrix products, arithmetic and copies ran while one was open for 29% of the time, Pallas kernels for 3%

profile of v2, /device:TPU:0, one launch (start us, length us, event | category | flops | bytes accessed | tf_op | source)
XLA Modules:
  0.0 968.6 jit_solution(136583460846691122)
XLA Ops:
  15.6 11.4 %collective-permute-done.38 = bf16[256,1024]{1,0:T(8,128)(2,1)S(1)} collective-permute-done((bf16[256,1024]{1,0:T(8,128)(2,1)S(1)}, bf16[256,1024]{1,0:T(8,128)(2,1)S(1)}, u32[]{:S(2)}, u32[]{:S(2)}) %collective-permute-start.38) | collective-permute-done | bytes 524320 | tf_op jit(solution)/shard_map/ppermute | solution.py:64
  27.0 32.4 %collective-permute-done.37 = bf16[256,1024]{1,0:T(8,128)(2,1)S(1)} collective-permute-done((bf16[256,1024]{1,0:T(8,128)(2,1)S(1)}, bf16[256,1024]{1,0:T(8,128)(2,1)S(1)}, u32[]{:S(2)}, u32[]{:S(2)}) %collective-permute-start.37) | collective-permute-done | bytes 524320 | tf_op jit(solution)/shard_map/ppermute | solution.py:64
  142.5 6.8 collective-permute-start.34
  156.7 8.5 collective-permute-done.22
  165.2 10.9 %collective-permute-done.21 = bf16[2,4,32,1152]{3,2,0,1:T(8,128)(2,1)} collective-permute-done((bf16[2,4,32,1152]{3,2,0,1:T(8,128)(2,1)}, bf16[2,4,32,1152]{3,2,0,1:T(8,128)(2,1)}, u32[]{:S(2)}, u32[]{:S(2)}) %collective-permute-start.21) | collective-permute-done | bytes 589856 | tf_op jit(solution)/shard_map/ppermute | solution.py:87
  183.6 28.0 %collective-permute-done.31 = bf16[2,4,2,32,1024]{4,3,2,1,0:T(8,128)(2,1)S(1)} collective-permute-done((bf16[2,4,2,32,1024]{4,3,2,1,0:T(8,128)(2,1)S(1)}, bf16[2,4,2,32,1024]{4,3,2,1,0:T(8,128)(2,1)S(1)}, u32[]{:S(2)}, u32[]{:S(2)}) %collective-permute-start.31) | collective-permute-done | bytes 1048608 | tf_op jit(solution)/shard_map/ppermute | solution.py:87
  230.6 8.7 multiply_convert_fusion.3
  239.4 6.8 fusion.42
  247.0 9.9 %multiply_convert_fusion.6 = (bf16[512,2048]{1,0:T(8,128)(2,1)S(1)}, f32[512,2048]{1,0:T(8,128)}) fusion(f32[512,2048]{1,0:T(8,128)} %fusion.42, bf16[512,1024]{1,0:T(8,128)(2,1)S(1)} %copy-done.91, bf16[2048,1024]{1,0:T(8,128)(2,1)S(1)} %bitcast.514), kind=kOutput, calls=%fused_computation.22 | convolution fusion | flops 2153775104 | bytes 15728640 | tf_op jit(solution)/shard_map/dot_general | solution.py:40
  264.3 7.7 fusion.120
  275.4 7.0 convolution_convert_fusion.1
  282.4 11.6 %convolution_add_fusion = f32[512,1024]{1,0:T(8,128)} fusion(f32[512,1024]{1,0:T(8,128)S(1)} %get-tuple-element.468, bf16[4096,1024]{1,0:T(8,128)(2,1)} %bitcast.585, f32[512,4096]{1,0:T(8,128)} %copy-done.157), kind=kOutput, calls=%fused_computation.103 | convolution fusion | flops 4305977344 | bytes 20971520 | tf_op jit(solution)/shard_map/dot_general | solution.py:36
  294.1 9.9 %multiply_convert_fusion.1 = bf16[512,4096]{1,0:T(8,128)(2,1)S(1)} fusion(f32[512,4096]{1,0:T(8,128)} %copy-done.157, bf16[512,1024]{1,0:T(8,128)(2,1)} %fusion.24, bf16[4096,1024]{1,0:T(8,128)(2,1)} %bitcast.586), kind=kOutput, calls=%fused_computation.4 | convolution fusion | flops 4313841664 | bytes 22020096 | tf_op jit(solution)/shard_map/dot_general | solution.py:40
  306.0 7.4 convolution_convert_fusion
  313.4 10.1 %multiply_reduce_fusion = (f32[1024]{0:T(1024)}, f32[512]{0:T(512)S(1)}, f32[512,1024]{1,0:T(8,128)S(1)}) fusion(f32[512,1024]{1,0:T(8,128)S(1)} %get-tuple-element.468, f32[512]{0:T(512)S(1)} %fusion.112, f32[512]{0:T(512)S(1)} %broadcast_multiply_fusion, f32[1024]{0:T(1024)S(1)} %bitcast.580, bf16[512,4096]{1,0:T(8,128)(2,1)} %copy-done.163, ...), kind=kOutput, calls=%fused_computation.72 | convolution fusion | flops 4298635776 | bytes 16791552 | tf_op jit(solution)/shard_map/dot_general | solution.py:36
  364.7 13.4 %reduce-scatter.3.cloned.1.call-done = bf16[512,1024]{1,0:T(8,128)(2,1)} async-done(((bf16[4096,1024]{1,0:T(8,128)(2,1)}), bf16[512,1024]{1,0:T(8,128)(2,1)}) %reduce-scatter.3.cloned.1.call-update) | async-done | bytes 1048592 | tf_op jit(solution)/shard_map/reduce_scatter | solution.py:200
  381.0 7.6 convolution_convert_fusion.5
  407.2 11.1 %collective-permute-done.46 = bf16[128,1024]{1,0:T(8,128)(2,1)S(1)} collective-permute-done((bf16[128,1024]{1,0:T(8,128)(2,1)S(1)}, bf16[128,1024]{1,0:T(8,128)(2,1)S(1)}, u32[]{:S(2)}, u32[]{:S(2)}) %collective-permute-start.46) | collective-permute-done | bytes 262176 | tf_op jit(solution)/shard_map/ppermute | solution.py:64
  424.4 33.4 %reduce-scatter.5.cloned.1.call-done = bf16[512,1024]{1,0:T(8,128)(2,1)} async-done(((bf16[4096,1024]{1,0:T(8,128)(2,1)}), bf16[512,1024]{1,0:T(8,128)(2,1)}) %reduce-scatter.5.cloned.1.call-update) | async-done | bytes 1048592 | tf_op jit(solution)/shard_map/reduce_scatter | solution.py:200
  469.3 15.5 %collective-permute-done.56 = bf16[128,1024]{1,0:T(8,128)(2,1)S(1)} collective-permute-done((bf16[128,1024]{1,0:T(8,128)(2,1)S(1)}, bf16[128,1024]{1,0:T(8,128)(2,1)S(1)}, u32[]{:S(2)}, u32[]{:S(2)}) %collective-permute-start.56) | collective-permute-done | bytes 262176 | tf_op jit(solution)/shard_map/ppermute | solution.py:64
  537.9 9.8 %collective-permute-done.65 = bf16[64,1024]{1,0:T(8,128)(2,1)S(1)} collective-permute-done((bf16[64,1024]{1,0:T(8,128)(2,1)S(1)}, bf16[64,1024]{1,0:T(8,128)(2,1)S(1)}, u32[]{:S(2)}, u32[]{:S(2)}) %collective-permute-start.65) | collective-permute-done | bytes 131104 | tf_op jit(solution)/shard_map/ppermute | solution.py:64
  563.5 9.3 collective-permute-done.81
  588.7 8.1 collective-permute-done.71
  616.7 14.2 %collective-permute-done.83 = bf16[1024,1024]{1,0:T(8,128)(2,1)} collective-permute-done((bf16[1024,1024]{1,0:T(8,128)(2,1)S(1)}, bf16[1024,1024]{1,0:T(8,128)(2,1)}, u32[]{:S(2)}, u32[]{:S(2)}) %collective-permute-start.83) | collective-permute-done | bytes 2097184 | tf_op jit(solution)/shard_map/ppermute | solution.py:269
  651.7 13.3 %collective-permute-done.85 = bf16[1024,1024]{1,0:T(8,128)(2,1)} collective-permute-done((bf16[1024,1024]{1,0:T(8,128)(2,1)}, bf16[1024,1024]{1,0:T(8,128)(2,1)}, u32[]{:S(2)}, u32[]{:S(2)}) %collective-permute-start.85) | collective-permute-done | bytes 2097184 | tf_op jit(solution)/shard_map/ppermute | solution.py:269
  715.1 10.9 %conditional.1 = (f32[1024,1024]{1,0:T(8,128)}) conditional(s32[]{:T(128)} %clamp.3, bf16[4096,1024]{1,0:T(8,128)(2,1)S(1)} %pad_maximum_fusion, bf16[2048,1024]{1,0:T(8,128)(2,1)} %pad_maximum_fusion.4, bf16[1024,1024]{1,0:T(8,128)(2,1)S(1)} %pad_maximum_fusion.11, bf16[2048,1024]{1,0:T(8,128)(2,1)} %pad_maximum_fusion.5), branch_computations={%region_11.12_spmd, %region_12.13_spmd, %region_13.14_spmd, %regio... | conditional | flops 8589934592 | bytes 12582920 | solution.py:826
  715.1 10.4 %fusion.136 = f32[1024,1024]{1,0:T(8,128)} fusion(bf16[4096,1024]{1,0:T(8,128)(2,1)S(1)} %param), kind=kOutput, calls=%fused_computation.424 | convolution fusion | flops 8589934592 | bytes 12582912 | tf_op jit(solution)/shard_map/cond/branch_0_fun/dot_general | solution.py:46
  726.0 91.7 %shard_map.394 = (bf16[1024,1024]{1,0:T(8,128)(2,1)}, bf16[1024,1024]{1,0:T(8,128)(2,1)}) custom-call(f32[1024,1024]{1,0:T(8,128)} %get-tuple-element.617.gram_ref), custom_call_target="tpu_custom_call" | custom-call | flops 73014444032 | bytes 8388608 | tf_op jit(solution)/shard_map/pallas_call | solution.py:485
  824.1 6.9 collective-permute-start.107
  855.9 14.6 %shard_map.392 = (f32[16,8,128]{2,1,0:T(8,128)S(1)}, f32[16,8,128]{2,1,0:T(8,128)S(1)}, f32[16,8,128]{2,1,0:T(8,128)S(1)}, f32[16,8,128]{2,1,0:T(8,128)S(1)}) custom-call(f32[512,8,128]{2,1,0:T(8,128)S(1)} %bitcast.475, f32[512,8,128]{2,1,0:T(8,128)S(1)} %bitcast.476, f32[16,8,128]{2,1,0:T(8,128)S(1)} %bitcast.483, f32[16,8,128]{2,1,0:T(8,128)S(1)} %copy-done.7), custom_call_target="tpu_custom_call" | custom-call | flops 83886080 | bytes 4194304 | tf_op jit(solution)/shard_map/pallas_call | solution.py:370
  941.4 7.5 bitcast_subtract_fusion.1
  952.5 9.1 bitcast_subtract_fusion
  (814 shorter events, 497.0 us)
Async XLA Ops:
  7.2 257.1 %all-gather.18.cloned.1.call-start = ((), (), s32[]{:S(2)}) async-start(), calls=%async_computation.4 | async-start | bytes 9437184 | tf_op jit(solution)/shard_map/all_gather | solution.py:195
  14.6 44.8 %collective-permute-start.37 = (bf16[256,1024]{1,0:T(8,128)(2,1)S(1)}, bf16[256,1024]{1,0:T(8,128)(2,1)S(1)}, u32[]{:S(2)}, u32[]{:S(2)}) collective-permute-start(bf16[256,1024]{1,0:T(8,128)(2,1)S(1)} %get-tuple-element.548), channel_id=1, source_target_pairs={{0,2},{1,3},{2,0},{3,1},{4,6},{5,7},{6,4},{7,5},{8,10},{9,11},{10,... | collective-permute-start | bytes 1572872 | tf_op jit(solution)/shard_map/ppermute | solution.py:64
  14.6 44.8 %collective-permute-start.36 = (bf16[256,1024]{1,0:T(8,128)(2,1)S(1)}, bf16[256,1024]{1,0:T(8,128)(2,1)S(1)}, u32[]{:S(2)}, u32[]{:S(2)}) collective-permute-start(bf16[256,1024]{1,0:T(8,128)(2,1)S(1)} %get-tuple-element.548), channel_id=1, source_target_pairs={{0,1},{1,2},{2,3},{3,0},{4,5},{5,6},{6,7},{7,4},{8,9},{9,10},{10,1... | collective-permute-start | bytes 1572872 | tf_op jit(solution)/shard_map/ppermute | solution.py:64
  61.2 221.2 %all-gather.20.cloned.1.call-start = ((), (), s32[]{:S(2)}) async-start(), calls=%async_computation.5 | async-start | bytes 9437184 | tf_op jit(solution)/shard_map/all_gather | solution.py:195
  133.7 42.4 %collective-permute-start.21 = (bf16[2,4,32,1152]{3,2,0,1:T(8,128)(2,1)}, bf16[2,4,32,1152]{3,2,0,1:T(8,128)(2,1)}, u32[]{:S(2)}, u32[]{:S(2)}) collective-permute-start(bf16[2,4,32,1152]{3,2,0,1:T(8,128)(2,1)} %pad_maximum_fusion.18), channel_id=1, source_target_pairs={{0,8},{4,12},{8,0},{12,4},{16,24},{20,28},{24,16},{28,20},{1,9},{5... | collective-permute-start | bytes 1769480 | tf_op jit(solution)/shard_map/ppermute | solution.py:87
  142.2 236.0 %reduce-scatter.3.cloned.1.call-start = ((), (), s32[]{:S(2)}) async-start(), calls=%async_computation.2 | async-start | bytes 9437184 | tf_op jit(solution)/shard_map/reduce_scatter | solution.py:200
  142.5 39.5 %collective-permute-start.34 = (bf16[512,1024]{1,0:T(8,128)(2,1)S(1)}, bf16[512,1024]{1,0:T(8,128)(2,1)S(1)}, u32[]{:S(2)}, u32[]{:S(2)}) collective-permute-start(bf16[512,1024]{1,0:T(8,128)(2,1)S(1)} %get-tuple-element.521), channel_id=1, source_target_pairs={{0,1},{2,3},{4,5},{6,7},{8,9},{10,11},{12,13},{14,15},{16,17},{18,... | collective-permute-start | bytes 3145736 | tf_op jit(solution)/shard_map/ppermute | solution.py:563
  153.7 57.9 %collective-permute-start.31 = (bf16[2,4,2,32,1024]{4,3,2,1,0:T(8,128)(2,1)S(1)}, bf16[2,4,2,32,1024]{4,3,2,1,0:T(8,128)(2,1)S(1)}, u32[]{:S(2)}, u32[]{:S(2)}) collective-permute-start(bf16[2,4,2,32,1024]{4,3,2,1,0:T(8,128)(2,1)S(1)} %pad_maximum_fusion.16), channel_id=1, source_target_pairs={{0,8},{4,12},{8,0},{12,4},{16,24},{20,28},{24,16},{28,20},{1,9},{5... | collective-permute-start | bytes 3145736 | tf_op jit(solution)/shard_map/ppermute | solution.py:87
  155.2 56.4 %collective-permute-start.32 = (bf16[2,4,2,32,1024]{4,3,2,1,0:T(8,128)(2,1)S(1)}, bf16[2,4,2,32,1024]{4,3,2,1,0:T(8,128)(2,1)S(1)}, u32[]{:S(2)}, u32[]{:S(2)}) collective-permute-start(bf16[2,4,2,32,1024]{4,3,2,1,0:T(8,128)(2,1)S(1)} %pad_maximum_fusion.17), channel_id=1, source_target_pairs={{0,16},{4,20},{8,24},{12,28},{16,0},{20,4},{24,8},{28,12},{1,17},{... | collective-permute-start | bytes 3145736 | tf_op jit(solution)/shard_map/ppermute | solution.py:87
  177.5 36.3 %collective-permute-start.23 = (bf16[2,2,4,32,1152]{4,3,0,1,2:T(8,128)(2,1)S(1)}, bf16[2,2,4,32,1152]{4,3,0,1,2:T(8,128)(2,1)S(1)}, u32[]{:S(2)}, u32[]{:S(2)}) collective-permute-start(bf16[2,2,4,32,1152]{4,3,0,1,2:T(8,128)(2,1)S(1)} %pad_maximum_fusion.12), channel_id=1, source_target_pairs={{0,4},{4,0},{8,12},{12,8},{16,20},{20,16},{24,28},{28,24},{1,5},{5... | collective-permute-start | bytes 3538952 | tf_op jit(solution)/shard_map/ppermute | solution.py:87
  178.8 34.9 %collective-permute-start.24 = (bf16[2,2,4,32,1024]{4,3,1,0,2:T(8,128)(2,1)S(1)}, bf16[2,2,4,32,1024]{4,3,1,0,2:T(8,128)(2,1)S(1)}, u32[]{:S(2)}, u32[]{:S(2)}) collective-permute-start(bf16[2,2,4,32,1024]{4,3,1,0,2:T(8,128)(2,1)S(1)} %pad_maximum_fusion.14), channel_id=1, source_target_pairs={{0,4},{4,0},{8,12},{12,8},{16,20},{20,16},{24,28},{28,24},{1,5},{5... | collective-permute-start | bytes 3145736 | tf_op jit(solution)/shard_map/ppermute | solution.py:87
  182.0 44.9 %collective-permute-start.35 = (bf16[2,4,4,1,32,1024]{5,4,2,1,0,3:T(8,128)(2,1)S(1)}, bf16[2,4,4,1,32,1024]{5,4,2,1,0,3:T(8,128)(2,1)S(1)}, u32[]{:S(2)}, u32[]{:S(2)}) collective-permute-start(bf16[2,4,4,1,32,1024]{5,4,2,1,0,3:T(8,128)(2,1)S(1)} %get-tuple-element.513), channel_id=1, source_target_pairs={{0,4},{4,0},{8,12},{12,8},{16,20},{20,16},{24,28},{28,24},{1,5},{5... | collective-permute-start | bytes 6291464 | tf_op jit(solution)/shard_map/ppermute | solution.py:87
  213.7 32.5 %collective-permute-start.33 = (bf16[2,4,4,2,32,1024]{5,4,3,2,1,0:T(8,128)(2,1)S(1)}, bf16[2,4,4,2,32,1024]{5,4,3,2,1,0:T(8,128)(2,1)S(1)}, u32[]{:S(2)}, u32[]{:S(2)}) collective-permute-start(bf16[2,4,4,2,32,1024]{5,4,3,2,1,0:T(8,128)(2,1)S(1)} %get-tuple-element.496), channel_id=1, source_target_pairs={{0,4},{4,0},{8,12},{12,8},{16,20},{20,16},{24,28},{28,24},{1,5},{5... | collective-permute-start | bytes 12582920 | tf_op jit(solution)/shard_map/ppermute | solution.py:87
  294.0 163.8 %reduce-scatter.5.cloned.1.call-start = ((), (), s32[]{:S(2)}) async-start(), calls=%async_computation.3 | async-start | bytes 9437184 | tf_op jit(solution)/shard_map/reduce_scatter | solution.py:200
  325.9 272.7 %all-gather.22.cloned.1.call-start = ((), (), s32[]{:S(2)}) async-start(), calls=%async_computation.6 | async-start | bytes 2359296 | tf_op jit(solution)/shard_map/all_gather | solution.py:645
  347.7 30.4 %collective-permute-start.41 = (bf16[256,1024]{1,0:T(8,128)(2,1)}, bf16[256,1024]{1,0:T(8,128)(2,1)}, u32[]{:S(2)}, u32[]{:S(2)}) collective-permute-start(bf16[256,1024]{1,0:T(8,128)(2,1)} %get-tuple-element.493), channel_id=1, source_target_pairs={{0,8},{4,12},{8,0},{12,4},{16,24},{20,28},{24,16},{28,20},{1,9},{5... | collective-permute-start | bytes 1572872 | tf_op jit(solution)/shard_map/ppermute | solution.py:87
  420.3 178.4 %all-gather.24.cloned.1.call-start = ((), (), s32[]{:S(2)}) async-start(), calls=%async_computation.7 | async-start | bytes 2359296 | tf_op jit(solution)/shard_map/all_gather | solution.py:645
  423.1 45.6 %collective-permute-start.44 = (f32[512,128]{1,0:T(8,128)}, f32[512,128]{1,0:T(8,128)}, u32[]{:S(2)}, u32[]{:S(2)}) collective-permute-start(f32[512,128]{1,0:T(8,128)} %slice.573), channel_id=1, source_target_pairs={{1,0},{3,2},{5,4},{7,6},{9,8},{11,10},{13,12},{15,14},{17,16},{19,... | collective-permute-start | bytes 786440 | tf_op jit(solution)/shard_map/ppermute | solution.py:716
  486.9 117.5 %all-gather.28.cloned.1.call-start = ((), (), s32[]{:S(2)}) async-start(), calls=%async_computation.9 | async-start | bytes 1179648 | tf_op jit(solution)/shard_map/all_gather | solution.py:645
  552.4 55.4 %all-gather.32.cloned.1.call-start = ((), (), s32[]{:S(2)}) async-start(), calls=%async_computation.11 | async-start | bytes 1327104 | tf_op jit(solution)/shard_map/all_gather | solution.py:645
  575.3 64.3 %all-gather.26.cloned.1.call-start = ((), (), s32[]{:S(2)}) async-start(), calls=%async_computation.8 | async-start | bytes 2359296 | tf_op jit(solution)/shard_map/all_gather | solution.py:645
  598.5 341.4 %all-gather.30.cloned.1.call-start = ((), (), s32[]{:S(2)}) async-start(), calls=%async_computation.10 | async-start | bytes 11796480 | tf_op jit(solution)/shard_map/all_gather | solution.py:850
  600.5 30.5 %collective-permute-start.83 = (bf16[1024,1024]{1,0:T(8,128)(2,1)S(1)}, bf16[1024,1024]{1,0:T(8,128)(2,1)}, u32[]{:S(2)}, u32[]{:S(2)}) collective-permute-start(bf16[1024,1024]{1,0:T(8,128)(2,1)S(1)} %select_select_fusion.1), channel_id=1, source_target_pairs={{8,9},{9,10},{10,11},{0,1},{1,2},{2,3}} | collective-permute-start | bytes 6291464 | tf_op jit(solution)/shard_map/ppermute | solution.py:269
  603.1 30.5 %collective-permute-start.84 = (bf16[1024,1024]{1,0:T(8,128)(2,1)S(1)}, bf16[1024,1024]{1,0:T(8,128)(2,1)}, u32[]{:S(2)}, u32[]{:S(2)}) collective-permute-start(bf16[1024,1024]{1,0:T(8,128)(2,1)S(1)} %select_select_fusion.1), channel_id=1, source_target_pairs={{9,8},{10,9},{11,10},{1,0},{2,1},{3,2}} | collective-permute-start | bytes 6291464 | tf_op jit(solution)/shard_map/ppermute | solution.py:270
  615.1 29.3 %collective-permute-start.103 = (bf16[512,1024]{1,0:T(8,128)(2,1)}, bf16[512,1024]{1,0:T(8,128)(2,1)}, u32[]{:S(2)}, u32[]{:S(2)}) collective-permute-start(bf16[512,1024]{1,0:T(8,128)(2,1)} %collective-permute-done.102), channel_id=1, source_target_pairs={{29,28},{30,29},{31,30}} | collective-permute-start | bytes 3145736 | tf_op jit(solution)/shard_map/ppermute | solution.py:270
  633.6 31.3 %collective-permute-start.85 = (bf16[1024,1024]{1,0:T(8,128)(2,1)}, bf16[1024,1024]{1,0:T(8,128)(2,1)}, u32[]{:S(2)}, u32[]{:S(2)}) collective-permute-start(bf16[1024,1024]{1,0:T(8,128)(2,1)} %collective-permute-done.83), channel_id=1, source_target_pairs={{8,9},{9,10},{10,11},{0,1},{1,2},{2,3}} | collective-permute-start | bytes 6291464 | tf_op jit(solution)/shard_map/ppermute | solution.py:269
  636.8 33.9 %collective-permute-start.86 = (bf16[1024,1024]{1,0:T(8,128)(2,1)}, bf16[1024,1024]{1,0:T(8,128)(2,1)}, u32[]{:S(2)}, u32[]{:S(2)}) collective-permute-start(bf16[1024,1024]{1,0:T(8,128)(2,1)} %collective-permute-done.84), channel_id=1, source_target_pairs={{9,8},{10,9},{11,10},{1,0},{2,1},{3,2}} | collective-permute-start | bytes 6291464 | tf_op jit(solution)/shard_map/ppermute | solution.py:270
  646.7 30.0 %collective-permute-start.106 = (bf16[512,1024]{1,0:T(8,128)(2,1)}, bf16[512,1024]{1,0:T(8,128)(2,1)}, u32[]{:S(2)}, u32[]{:S(2)}) collective-permute-start(bf16[512,1024]{1,0:T(8,128)(2,1)} %collective-permute-done.105), channel_id=1, source_target_pairs={{28,29},{29,30},{30,31}} | collective-permute-start | bytes 3145736 | tf_op jit(solution)/shard_map/ppermute | solution.py:269
  648.4 30.0 %collective-permute-start.93 = (bf16[512,1024]{1,0:T(8,128)(2,1)}, bf16[512,1024]{1,0:T(8,128)(2,1)}, u32[]{:S(2)}, u32[]{:S(2)}) collective-permute-start(bf16[512,1024]{1,0:T(8,128)(2,1)} %collective-permute-done.89), channel_id=1, source_target_pairs={{24,25},{25,26},{26,27},{16,17},{17,18},{18,19}} | collective-permute-start | bytes 3145736 | tf_op jit(solution)/shard_map/ppermute | solution.py:269
  671.4 35.9 %collective-permute-start.88 = (bf16[1024,1024]{1,0:T(8,128)(2,1)}, bf16[1024,1024]{1,0:T(8,128)(2,1)}, u32[]{:S(2)}, u32[]{:S(2)}) collective-permute-start(bf16[1024,1024]{1,0:T(8,128)(2,1)} %collective-permute-done.85), channel_id=1, source_target_pairs={{8,9},{9,10},{10,11},{0,1},{1,2},{2,3}} | collective-permute-start | bytes 6291464 | tf_op jit(solution)/shard_map/ppermute | solution.py:269
  675.4 35.2 %collective-permute-start.87 = (bf16[1024,1024]{1,0:T(8,128)(2,1)}, bf16[1024,1024]{1,0:T(8,128)(2,1)}, u32[]{:S(2)}, u32[]{:S(2)}) collective-permute-start(bf16[1024,1024]{1,0:T(8,128)(2,1)} %collective-permute-done.86), channel_id=1, source_target_pairs={{9,8},{10,9},{11,10},{1,0},{2,1},{3,2}} | collective-permute-start | bytes 6291464 | tf_op jit(solution)/shard_map/ppermute | solution.py:270
  845.1 52.4 %collective-permute-start.43 = (bf16[512,1024]{1,0:T(8,128)(2,1)}, bf16[512,1024]{1,0:T(8,128)(2,1)}, u32[]{:S(2)}, u32[]{:S(2)}) collective-permute-start(bf16[512,1024]{1,0:T(8,128)(2,1)} %slice.867), channel_id=1, source_target_pairs={{1,0},{3,2},{5,4},{7,6},{9,8},{11,10},{13,12},{15,14},{17,16},{19,... | collective-permute-start | bytes 3145736 | tf_op jit(solution)/shard_map/ppermute | solution.py:718
  (262 other events, 3428.0 us)
Sparse Core Ops, SparseCore 0:
  61.3 60.3 all-gather.17
  142.3 80.6 all-gather.19
  294.1 83.9 reduce-scatter.2
  381.8 75.8 reduce-scatter.4
  459.5 31.4 all-gather.21
  492.8 35.3 all-gather.23
  552.5 21.7 all-gather.27
  576.8 24.0 all-gather.31
  603.4 27.8 all-gather.25
  839.9 68.4 all-gather.29

commit v3 on v2

--- a/solution.py
+++ b/solution.py
@@ -260,16 +260,11 @@
 
 def in_columns(block, slots):
     count = lax.axis_size("seq")
-    up = [(s * count + i, s * count + i + 1) for s in slots for i in range(count - 1)]
-    down = [(j, i) for i, j in up]
+    pairs = [(s * count + i, s * count + (i + 1) % count) for s in slots for i in range(count)]
     held = [block]
-    above = below = block
     for _ in range(count - 1):
-        below, above = yield [below, above], [
-            lax.ppermute(below, ("dp", "seq"), up),
-            lax.ppermute(above, ("dp", "seq"), down),
-        ]
-        held += [below, above]
+        (item,) = yield [held[-1]], [lax.ppermute(held[-1], ("dp", "seq"), pairs)]
+        held.append(item)
     return held
 
 
@@ -654,11 +649,7 @@
         height = max(item.shape[0] for item in blocks)
         own = chosen(names, blocks, height)
         held = yield from in_columns(own, [SLOT[name] for name in names])
-        mine = held[0]
-        rest = []
-        for k in range(1, seq_count):
-            rest.append(held[2 * k - 1] + held[2 * (seq_count - k)])
-        return jnp.concatenate([mine] + rest, axis=0)
+        return held
 
     def chosen(names, blocks, height):
         out = jnp.zeros((height, D), jnp.bfloat16)
@@ -823,8 +814,12 @@
     ):
         for name in names:
             which = jnp.where(dp_index == SLOT[name], index, which)
+    def gram_of(items):
+        whole = jnp.concatenate(items, axis=0)
+        return times_left(whole, whole)
+
     gram = lax.switch(
-        which, [lambda *items, i=i: times_left(items[i], items[i]) for i in range(4)], *columns_held
+        which, [lambda *items, i=i: gram_of(items[i]) for i in range(4)], *columns_held
     )
     factor_high, factor_low = orthogonal_factor(gram)
     height = max(block[name].shape[0] for name in order)

time: 978 us -> 973 us (level)
  waiting for transfers between devices: 284 us -> 336 us
  other arithmetic: 150 us -> 116 us
  starting transfers between devices: 184 us -> 156 us
    ppermute x38, waiting for transfers between devices: 82.4 us -> 107 us  [across(): lax.ppermute(x, 'dp', [(i, i ^ bit) for i in range(lax.axis_size('dp'))])]
    add x12 -> x0, other arithmetic: 23.6 us -> none  [column_rows(): rest.append(held[2 * k - 1] + held[2 * (seq_count - k)])]
    ppermute x24 -> x12, starting transfers between devices: 37.8 us -> 20.1 us  [in_columns(): item, = (yield ([held[-1]], [lax.ppermute(held[-1], ('dp', 'seq'), pairs)]))]
    ppermute x42, waiting for transfers between devices: 112 us -> 129 us  [turned(): lax.ppermute(x, 'seq', [(i, (i + distance) % count) for i in range(count)])]
    all_gather x5, waiting for transfers between devices: 0.06 us -> 11.4 us  [kept_rows(): lax.all_gather(packed, 'dp', axis=0, tiled=False)]
    ppermute x24 -> x12, waiting for transfers between devices: 35.3 us -> 28.7 us  [in_columns(): item, = (yield ([held[-1]], [lax.ppermute(held[-1], ('dp', 'seq'), pairs)]))]
    unnamed x340 -> x314, local copies, waits for them, and re-layouts: 25.4 us -> 24.1 us
  transfers between devices with their start and end apart: 127 -> 115, of which waited for: 41 -> 44; matrix products, arithmetic and copies ran while one was open for 29% -> 26% of each run, Pallas kernels for 3% -> 3%
where the time goes in v3:
time: 973 us; the launch traced here: 964 us
  waiting for transfers between devices  336 us (35%)
  matrix products  159 us (16%)
  starting transfers between devices  156 us (16%)
  Pallas kernels  118 us (12%)
  other arithmetic  116 us (12%)
  local copies, waits for them, and re-layouts  61.4 us (6%)
  between operations  17.7 us (2%)
    ppermute x42, waiting for transfers between devices, turned(): lax.ppermute(x, 'seq', [(i, (i + distance) % count) for i in range(count)])  129 us
    ppermute x38, waiting for transfers between devices, across(): lax.ppermute(x, 'dp', [(i, i ^ bit) for i in range(lax.axis_size('dp'))])  107 us
    pallas_call x1, Pallas kernels, orthogonal_factor(): pl.pallas_call(factor_kernel, out_shape=(jax.ShapeDtypeStruct(gram.shape,...  91.7 us
    ppermute x42, starting transfers between devices, turned(): lax.ppermute(x, 'seq', [(i, (i + distance) % count) for i in range(count)])  67 us
    dot_general x10, matrix products, times_left(): lax.dot_general(left, right, (((0,), (0,)), ((), ())), preferred_element_...  56.7 us
    dot_general x12, matrix products, times_plain(): return jnp.dot(left, right, preferred_element_type=jnp.float32)  53.9 us
    reduce_scatter x2, waiting for transfers between devices, far_sum(): lax.psum_scatter(grad, 'dp', scatter_dimension=0, tiled=True)  50.4 us
    dot_general x9, matrix products, times_right(): lax.dot_general(left, right, (((1,), (1,)), ((), ())), preferred_element_...  48 us
  transfers between devices with their start and end apart: 115, of which 44 were waited for; matrix products, arithmetic and copies ran while one was open for 26% of the time, Pallas kernels for 3%

profile of v3, /device:TPU:0, one launch (start us, length us, event | category | flops | bytes accessed | tf_op | source)
XLA Modules:
  0.0 963.8 jit_solution(13815039424153362291)
XLA Ops:
  15.6 11.4 %collective-permute-done.38 = bf16[256,1024]{1,0:T(8,128)(2,1)S(1)} collective-permute-done((bf16[256,1024]{1,0:T(8,128)(2,1)S(1)}, bf16[256,1024]{1,0:T(8,128)(2,1)S(1)}, u32[]{:S(2)}, u32[]{:S(2)}) %collective-permute-start.38) | collective-permute-done | bytes 524320 | tf_op jit(solution)/shard_map/ppermute | solution.py:64
  27.0 32.4 %collective-permute-done.37 = bf16[256,1024]{1,0:T(8,128)(2,1)S(1)} collective-permute-done((bf16[256,1024]{1,0:T(8,128)(2,1)S(1)}, bf16[256,1024]{1,0:T(8,128)(2,1)S(1)}, u32[]{:S(2)}, u32[]{:S(2)}) %collective-permute-start.37) | collective-permute-done | bytes 524320 | tf_op jit(solution)/shard_map/ppermute | solution.py:64
  156.7 8.5 collective-permute-done.22
  165.2 10.9 %collective-permute-done.21 = bf16[2,4,32,1152]{3,2,0,1:T(8,128)(2,1)} collective-permute-done((bf16[2,4,32,1152]{3,2,0,1:T(8,128)(2,1)}, bf16[2,4,32,1152]{3,2,0,1:T(8,128)(2,1)}, u32[]{:S(2)}, u32[]{:S(2)}) %collective-permute-start.21) | collective-permute-done | bytes 589856 | tf_op jit(solution)/shard_map/ppermute | solution.py:87
  183.6 28.0 %collective-permute-done.31 = bf16[2,4,2,32,1024]{4,3,2,1,0:T(8,128)(2,1)S(1)} collective-permute-done((bf16[2,4,2,32,1024]{4,3,2,1,0:T(8,128)(2,1)S(1)}, bf16[2,4,2,32,1024]{4,3,2,1,0:T(8,128)(2,1)S(1)}, u32[]{:S(2)}, u32[]{:S(2)}) %collective-permute-start.31) | collective-permute-done | bytes 1048608 | tf_op jit(solution)/shard_map/ppermute | solution.py:87
  230.6 8.4 multiply_convert_fusion.3
  246.6 9.9 %multiply_convert_fusion.6 = (bf16[512,2048]{1,0:T(8,128)(2,1)S(1)}, f32[512,2048]{1,0:T(8,128)}) fusion(f32[512,2048]{1,0:T(8,128)} %fusion.78, bf16[512,1024]{1,0:T(8,128)(2,1)S(1)} %copy-done.79, bf16[2048,1024]{1,0:T(8,128)(2,1)S(1)} %bitcast.506), kind=kOutput, calls=%fused_computation.55 | convolution fusion | flops 2153775104 | bytes 15728640 | tf_op jit(solution)/shard_map/dot_general | solution.py:40
  264.0 7.7 fusion.156
  275.0 7.0 convolution_convert_fusion.1
  282.0 11.6 %convolution_add_fusion = f32[512,1024]{1,0:T(8,128)} fusion(f32[512,1024]{1,0:T(8,128)S(1)} %get-tuple-element.504, bf16[4096,1024]{1,0:T(8,128)(2,1)} %bitcast.577, f32[512,4096]{1,0:T(8,128)} %copy-done.144), kind=kOutput, calls=%fused_computation.135 | convolution fusion | flops 4305977344 | bytes 20971520 | tf_op jit(solution)/shard_map/dot_general | solution.py:36
  293.7 9.8 %multiply_convert_fusion.1 = bf16[512,4096]{1,0:T(8,128)(2,1)S(1)} fusion(f32[512,4096]{1,0:T(8,128)} %copy-done.144, bf16[512,1024]{1,0:T(8,128)(2,1)} %fusion.60, bf16[4096,1024]{1,0:T(8,128)(2,1)} %bitcast.578), kind=kOutput, calls=%fused_computation.39 | convolution fusion | flops 4313841664 | bytes 22020096 | tf_op jit(solution)/shard_map/dot_general | solution.py:40
  305.6 7.4 convolution_convert_fusion
  313.0 10.1 %multiply_reduce_fusion = (f32[1024]{0:T(1024)}, f32[512]{0:T(512)S(1)}, f32[512,1024]{1,0:T(8,128)S(1)}) fusion(f32[512,1024]{1,0:T(8,128)S(1)} %get-tuple-element.504, f32[512]{0:T(512)S(1)} %fusion.148, f32[512]{0:T(512)S(1)} %broadcast_multiply_fusion, f32[1024]{0:T(1024)S(1)} %bitcast.572, bf16[512,4096]{1,0:T(8,128)(2,1)} %copy-done.150, ...), kind=kOutput, calls=%fused_computation.104 | convolution fusion | flops 4298635776 | bytes 16791552 | tf_op jit(solution)/shard_map/dot_general | solution.py:36
  357.7 6.9 multiply_convert_fusion
  364.5 12.8 %reduce-scatter.3.cloned.1.call-done = bf16[512,1024]{1,0:T(8,128)(2,1)} async-done(((bf16[4096,1024]{1,0:T(8,128)(2,1)}), bf16[512,1024]{1,0:T(8,128)(2,1)}) %reduce-scatter.3.cloned.1.call-update) | async-done | bytes 1048592 | tf_op jit(solution)/shard_map/reduce_scatter | solution.py:200
  380.1 7.6 convolution_convert_fusion.5
  406.4 11.0 %collective-permute-done.46 = bf16[128,1024]{1,0:T(8,128)(2,1)S(1)} collective-permute-done((bf16[128,1024]{1,0:T(8,128)(2,1)S(1)}, bf16[128,1024]{1,0:T(8,128)(2,1)S(1)}, u32[]{:S(2)}, u32[]{:S(2)}) %collective-permute-start.46) | collective-permute-done | bytes 262176 | tf_op jit(solution)/shard_map/ppermute | solution.py:64
  419.4 37.6 %reduce-scatter.5.cloned.1.call-done = bf16[512,1024]{1,0:T(8,128)(2,1)} async-done(((bf16[4096,1024]{1,0:T(8,128)(2,1)}), bf16[512,1024]{1,0:T(8,128)(2,1)}) %reduce-scatter.5.cloned.1.call-update) | async-done | bytes 1048592 | tf_op jit(solution)/shard_map/reduce_scatter | solution.py:200
  469.3 15.7 %collective-permute-done.56 = bf16[128,1024]{1,0:T(8,128)(2,1)} collective-permute-done((bf16[128,1024]{1,0:T(8,128)(2,1)}, bf16[128,1024]{1,0:T(8,128)(2,1)}, u32[]{:S(2)}, u32[]{:S(2)}) %collective-permute-start.56) | collective-permute-done | bytes 262176 | tf_op jit(solution)/shard_map/ppermute | solution.py:64
  515.0 8.1 collective-permute-done.60
  550.1 8.1 collective-permute-done.53
  566.0 7.1 collective-permute-done.71
  581.5 12.5 %collective-permute-done.74 = bf16[2,4,32,1024]{3,2,1,0:T(8,128)(2,1)} collective-permute-done((bf16[2,4,32,1024]{3,2,1,0:T(8,128)(2,1)}, bf16[2,4,32,1024]{3,2,1,0:T(8,128)(2,1)}, u32[]{:S(2)}, u32[]{:S(2)}) %collective-permute-start.74) | collective-permute-done | bytes 524320 | tf_op jit(solution)/shard_map/ppermute | solution.py:87
  615.0 22.3 %collective-permute-done.80 = bf16[32,2176]{1,0:T(8,128)(2,1)S(1)} collective-permute-done((bf16[32,2176]{1,0:T(8,128)(2,1)S(1)}, bf16[32,2176]{1,0:T(8,128)(2,1)S(1)}, u32[]{:S(2)}, u32[]{:S(2)}) %collective-permute-start.80) | collective-permute-done | bytes 139296 | tf_op jit(solution)/shard_map/ppermute | solution.py:64
  656.4 11.4 %all-gather.32.cloned.1.call-done = bf16[8,68,1024]{2,1,0:T(8,128)(2,1)} async-done(((bf16[1,68,1024]{2,1,0:T(8,128)(2,1)}), bf16[8,68,1024]{2,1,0:T(8,128)(2,1)}) %all-gather.32.cloned.1.call-update) | async-done | bytes 1114128 | tf_op jit(solution)/shard_map/all_gather | solution.py:640
  688.4 26.0 %collective-permute-done.85 = bf16[1024,1024]{1,0:T(8,128)(2,1)} collective-permute-done((bf16[1024,1024]{1,0:T(8,128)(2,1)}, bf16[1024,1024]{1,0:T(8,128)(2,1)}, u32[]{:S(2)}, u32[]{:S(2)}) %collective-permute-start.85) | collective-permute-done | bytes 2097184 | tf_op jit(solution)/shard_map/ppermute | solution.py:266
  714.4 17.2 %conditional.1 = (f32[1024,1024]{1,0:T(8,128)}) conditional(s32[]{:T(128)} %clamp.3, (bf16[1024,1024]{1,0:T(8,128)(2,1)}, bf16[1024,1024]{1,0:T(8,128)(2,1)}, bf16[1024,1024]{1,0:T(8,128)(2,1)}, bf16[1024,1024]{1,0:T(8,128)(2,1)}) %tuple.402, (bf16[512,1024]{1,0:T(8,128)(2,1)}, bf16[512,1024]{1,0:T(8,128)(2,1)}, ...), branch_computations={%region_11.12_spmd, %region_12.13_spmd, %region_13.14_spmd, %regio... | conditional | flops 8623489024 | bytes 12582920 | solution.py:821
  714.4 16.8 %fusion = f32[1024,1024]{1,0:T(8,128)} fusion(bf16[1024,1024]{1,0:T(8,128)(2,1)} %get-tuple-element.40, bf16[1024,1024]{1,0:T(8,128)(2,1)} %get-tuple-element.34, bf16[1024,1024]{1,0:T(8,128)(2,1)} %get-tuple-element.33, bf16[1024,1024]{1,0:T(8,128)(2,1)} %get-tuple-element.32), kind=kOutput, calls=%fused_computation | convolution fusion | flops 8623489024 | bytes 12582912 | tf_op jit(solution)/shard_map/cond/branch_0_fun/dot_general | solution.py:46
  731.6 91.7 %shard_map.394 = (bf16[1024,1024]{1,0:T(8,128)(2,1)}, bf16[1024,1024]{1,0:T(8,128)(2,1)}) custom-call(f32[1024,1024]{1,0:T(8,128)} %get-tuple-element.653.gram_ref), custom_call_target="tpu_custom_call" | custom-call | flops 73014444032 | bytes 8388608 | tf_op jit(solution)/shard_map/pallas_call | solution.py:480
  855.2 14.6 %shard_map.392 = (f32[16,8,128]{2,1,0:T(8,128)S(1)}, f32[16,8,128]{2,1,0:T(8,128)S(1)}, f32[16,8,128]{2,1,0:T(8,128)S(1)}, f32[16,8,128]{2,1,0:T(8,128)S(1)}) custom-call(f32[512,8,128]{2,1,0:T(8,128)S(1)} %bitcast.467, f32[512,8,128]{2,1,0:T(8,128)S(1)} %bitcast.468, f32[16,8,128]{2,1,0:T(8,128)S(1)} %bitcast.475, f32[16,8,128]{2,1,0:T(8,128)S(1)} %copy-done.7), custom_call_target="tpu_custom_call" | custom-call | flops 83886080 | bytes 4194304 | tf_op jit(solution)/shard_map/pallas_call | solution.py:365
  936.6 7.5 bitcast_subtract_fusion.1
  947.7 9.1 bitcast_subtract_fusion
  (748 shorter events, 455.8 us)
Async XLA Ops:
  7.2 256.8 %all-gather.18.cloned.1.call-start = ((), (), s32[]{:S(2)}) async-start(), calls=%async_computation.4 | async-start | bytes 9437184 | tf_op jit(solution)/shard_map/all_gather | solution.py:195
  14.6 44.8 %collective-permute-start.37 = (bf16[256,1024]{1,0:T(8,128)(2,1)S(1)}, bf16[256,1024]{1,0:T(8,128)(2,1)S(1)}, u32[]{:S(2)}, u32[]{:S(2)}) collective-permute-start(bf16[256,1024]{1,0:T(8,128)(2,1)S(1)} %get-tuple-element.584), channel_id=1, source_target_pairs={{0,2},{1,3},{2,0},{3,1},{4,6},{5,7},{6,4},{7,5},{8,10},{9,11},{10,... | collective-permute-start | bytes 1572872 | tf_op jit(solution)/shard_map/ppermute | solution.py:64
  14.6 44.8 %collective-permute-start.36 = (bf16[256,1024]{1,0:T(8,128)(2,1)S(1)}, bf16[256,1024]{1,0:T(8,128)(2,1)S(1)}, u32[]{:S(2)}, u32[]{:S(2)}) collective-permute-start(bf16[256,1024]{1,0:T(8,128)(2,1)S(1)} %get-tuple-element.584), channel_id=1, source_target_pairs={{0,1},{1,2},{2,3},{3,0},{4,5},{5,6},{6,7},{7,4},{8,9},{9,10},{10,1... | collective-permute-start | bytes 1572872 | tf_op jit(solution)/shard_map/ppermute | solution.py:64
  61.2 220.8 %all-gather.20.cloned.1.call-start = ((), (), s32[]{:S(2)}) async-start(), calls=%async_computation.5 | async-start | bytes 9437184 | tf_op jit(solution)/shard_map/all_gather | solution.py:195
  133.6 42.4 %collective-permute-start.21 = (bf16[2,4,32,1152]{3,2,0,1:T(8,128)(2,1)}, bf16[2,4,32,1152]{3,2,0,1:T(8,128)(2,1)}, u32[]{:S(2)}, u32[]{:S(2)}) collective-permute-start(bf16[2,4,32,1152]{3,2,0,1:T(8,128)(2,1)} %pad_maximum_fusion.14), channel_id=1, source_target_pairs={{0,8},{4,12},{8,0},{12,4},{16,24},{20,28},{24,16},{28,20},{1,9},{5... | collective-permute-start | bytes 1769480 | tf_op jit(solution)/shard_map/ppermute | solution.py:87
  142.2 235.2 %reduce-scatter.3.cloned.1.call-start = ((), (), s32[]{:S(2)}) async-start(), calls=%async_computation.2 | async-start | bytes 9437184 | tf_op jit(solution)/shard_map/reduce_scatter | solution.py:200
  142.4 39.5 %collective-permute-start.34 = (bf16[512,1024]{1,0:T(8,128)(2,1)S(1)}, bf16[512,1024]{1,0:T(8,128)(2,1)S(1)}, u32[]{:S(2)}, u32[]{:S(2)}) collective-permute-start(bf16[512,1024]{1,0:T(8,128)(2,1)S(1)} %get-tuple-element.557), channel_id=1, source_target_pairs={{0,1},{2,3},{4,5},{6,7},{8,9},{10,11},{12,13},{14,15},{16,17},{18,... | collective-permute-start | bytes 3145736 | tf_op jit(solution)/shard_map/ppermute | solution.py:558
  153.7 57.9 %collective-permute-start.31 = (bf16[2,4,2,32,1024]{4,3,2,1,0:T(8,128)(2,1)S(1)}, bf16[2,4,2,32,1024]{4,3,2,1,0:T(8,128)(2,1)S(1)}, u32[]{:S(2)}, u32[]{:S(2)}) collective-permute-start(bf16[2,4,2,32,1024]{4,3,2,1,0:T(8,128)(2,1)S(1)} %pad_maximum_fusion.12), channel_id=1, source_target_pairs={{0,8},{4,12},{8,0},{12,4},{16,24},{20,28},{24,16},{28,20},{1,9},{5... | collective-permute-start | bytes 3145736 | tf_op jit(solution)/shard_map/ppermute | solution.py:87
  155.2 56.4 %collective-permute-start.32 = (bf16[2,4,2,32,1024]{4,3,2,1,0:T(8,128)(2,1)S(1)}, bf16[2,4,2,32,1024]{4,3,2,1,0:T(8,128)(2,1)S(1)}, u32[]{:S(2)}, u32[]{:S(2)}) collective-permute-start(bf16[2,4,2,32,1024]{4,3,2,1,0:T(8,128)(2,1)S(1)} %pad_maximum_fusion.13), channel_id=1, source_target_pairs={{0,16},{4,20},{8,24},{12,28},{16,0},{20,4},{24,8},{28,12},{1,17},{... | collective-permute-start | bytes 3145736 | tf_op jit(solution)/shard_map/ppermute | solution.py:87
  177.4 36.3 %collective-permute-start.23 = (bf16[2,2,4,32,1152]{4,3,0,1,2:T(8,128)(2,1)S(1)}, bf16[2,2,4,32,1152]{4,3,0,1,2:T(8,128)(2,1)S(1)}, u32[]{:S(2)}, u32[]{:S(2)}) collective-permute-start(bf16[2,2,4,32,1152]{4,3,0,1,2:T(8,128)(2,1)S(1)} %pad_maximum_fusion.8), channel_id=1, source_target_pairs={{0,4},{4,0},{8,12},{12,8},{16,20},{20,16},{24,28},{28,24},{1,5},{5... | collective-permute-start | bytes 3538952 | tf_op jit(solution)/shard_map/ppermute | solution.py:87
  178.8 34.9 %collective-permute-start.24 = (bf16[2,2,4,32,1024]{4,3,1,0,2:T(8,128)(2,1)S(1)}, bf16[2,2,4,32,1024]{4,3,1,0,2:T(8,128)(2,1)S(1)}, u32[]{:S(2)}, u32[]{:S(2)}) collective-permute-start(bf16[2,2,4,32,1024]{4,3,1,0,2:T(8,128)(2,1)S(1)} %pad_maximum_fusion.10), channel_id=1, source_target_pairs={{0,4},{4,0},{8,12},{12,8},{16,20},{20,16},{24,28},{28,24},{1,5},{5... | collective-permute-start | bytes 3145736 | tf_op jit(solution)/shard_map/ppermute | solution.py:87
  181.9 44.9 %collective-permute-start.35 = (bf16[2,4,4,1,32,1024]{5,4,2,1,0,3:T(8,128)(2,1)S(1)}, bf16[2,4,4,1,32,1024]{5,4,2,1,0,3:T(8,128)(2,1)S(1)}, u32[]{:S(2)}, u32[]{:S(2)}) collective-permute-start(bf16[2,4,4,1,32,1024]{5,4,2,1,0,3:T(8,128)(2,1)S(1)} %get-tuple-element.549), channel_id=1, source_target_pairs={{0,4},{4,0},{8,12},{12,8},{16,20},{20,16},{24,28},{28,24},{1,5},{5... | collective-permute-start | bytes 6291464 | tf_op jit(solution)/shard_map/ppermute | solution.py:87
  213.6 32.2 %collective-permute-start.33 = (bf16[2,4,4,2,32,1024]{5,4,3,2,1,0:T(8,128)(2,1)S(1)}, bf16[2,4,4,2,32,1024]{5,4,3,2,1,0:T(8,128)(2,1)S(1)}, u32[]{:S(2)}, u32[]{:S(2)}) collective-permute-start(bf16[2,4,4,2,32,1024]{5,4,3,2,1,0:T(8,128)(2,1)S(1)} %get-tuple-element.532), channel_id=1, source_target_pairs={{0,4},{4,0},{8,12},{12,8},{16,20},{20,16},{24,28},{28,24},{1,5},{5... | collective-permute-start | bytes 12582920 | tf_op jit(solution)/shard_map/ppermute | solution.py:87
  293.7 163.3 %reduce-scatter.5.cloned.1.call-start = ((), (), s32[]{:S(2)}) async-start(), calls=%async_computation.3 | async-start | bytes 9437184 | tf_op jit(solution)/shard_map/reduce_scatter | solution.py:200
  325.5 278.7 %all-gather.22.cloned.1.call-start = ((), (), s32[]{:S(2)}) async-start(), calls=%async_computation.6 | async-start | bytes 2359296 | tf_op jit(solution)/shard_map/all_gather | solution.py:640
  347.1 30.2 %collective-permute-start.41 = (bf16[256,1024]{1,0:T(8,128)(2,1)S(1)}, bf16[256,1024]{1,0:T(8,128)(2,1)}, u32[]{:S(2)}, u32[]{:S(2)}) collective-permute-start(bf16[256,1024]{1,0:T(8,128)(2,1)S(1)} %get-tuple-element.529), channel_id=1, source_target_pairs={{0,8},{4,12},{8,0},{12,4},{16,24},{20,28},{24,16},{28,20},{1,9},{5... | collective-permute-start | bytes 1572872 | tf_op jit(solution)/shard_map/ppermute | solution.py:87
  349.2 28.1 %collective-permute-start.42 = (bf16[256,1024]{1,0:T(8,128)(2,1)S(1)}, bf16[256,1024]{1,0:T(8,128)(2,1)}, u32[]{:S(2)}, u32[]{:S(2)}) collective-permute-start(bf16[256,1024]{1,0:T(8,128)(2,1)S(1)} %get-tuple-element.528), channel_id=1, source_target_pairs={{0,16},{4,20},{8,24},{12,28},{16,0},{20,4},{24,8},{28,12},{1,17},{... | collective-permute-start | bytes 1572872 | tf_op jit(solution)/shard_map/ppermute | solution.py:87
  419.4 184.9 %all-gather.24.cloned.1.call-start = ((), (), s32[]{:S(2)}) async-start(), calls=%async_computation.7 | async-start | bytes 2359296 | tf_op jit(solution)/shard_map/all_gather | solution.py:640
  487.4 159.0 %all-gather.28.cloned.1.call-start = ((), (), s32[]{:S(2)}) async-start(), calls=%async_computation.9 | async-start | bytes 1179648 | tf_op jit(solution)/shard_map/all_gather | solution.py:640
  509.0 34.1 %collective-permute-start.69 = (bf16[64,1024]{1,0:T(8,128)(2,1)S(1)}, bf16[64,1024]{1,0:T(8,128)(2,1)S(1)}, u32[]{:S(2)}, u32[]{:S(2)}) collective-permute-start(bf16[64,1024]{1,0:T(8,128)(2,1)S(1)} %get-tuple-element.578), channel_id=1, source_target_pairs={{0,1},{1,2},{2,3},{3,0},{4,5},{5,6},{6,7},{7,4},{8,9},{9,10},{10,1... | collective-permute-start | bytes 393224 | tf_op jit(solution)/shard_map/ppermute | solution.py:64
  509.9 33.3 %collective-permute-start.68 = (bf16[64,1024]{1,0:T(8,128)(2,1)S(1)}, bf16[64,1024]{1,0:T(8,128)(2,1)S(1)}, u32[]{:S(2)}, u32[]{:S(2)}) collective-permute-start(bf16[64,1024]{1,0:T(8,128)(2,1)S(1)} %get-tuple-element.579), channel_id=1, source_target_pairs={{0,2},{1,3},{2,0},{3,1},{4,6},{5,7},{6,4},{7,5},{8,10},{9,11},{10,... | collective-permute-start | bytes 393224 | tf_op jit(solution)/shard_map/ppermute | solution.py:64
  512.0 31.2 %collective-permute-start.67 = (bf16[64,1024]{1,0:T(8,128)(2,1)S(1)}, bf16[64,1024]{1,0:T(8,128)(2,1)S(1)}, u32[]{:S(2)}, u32[]{:S(2)}) collective-permute-start(bf16[64,1024]{1,0:T(8,128)(2,1)S(1)} %get-tuple-element.577), channel_id=1, source_target_pairs={{0,3},{1,0},{2,1},{3,2},{4,7},{5,4},{6,5},{7,6},{8,11},{9,8},{10,9... | collective-permute-start | bytes 393224 | tf_op jit(solution)/shard_map/ppermute | solution.py:64
  539.1 34.0 %collective-permute-start.51 = (bf16[4,4,32,1152]{3,2,0,1:T(8,128)(2,1)}, bf16[4,4,32,1152]{3,2,0,1:T(8,128)(2,1)}, u32[]{:S(2)}, u32[]{:S(2)}) collective-permute-start(bf16[4,4,32,1152]{3,2,0,1:T(8,128)(2,1)} %get-tuple-element.537), channel_id=1, source_target_pairs={{0,4},{4,0},{8,12},{12,8},{16,20},{20,16},{24,28},{28,24},{1,5},{5... | collective-permute-start | bytes 3538952 | tf_op jit(solution)/shard_map/ppermute | solution.py:87
  545.1 104.0 %all-gather.26.cloned.1.call-start = ((), (), s32[]{:S(2)}) async-start(), calls=%async_computation.8 | async-start | bytes 2359296 | tf_op jit(solution)/shard_map/all_gather | solution.py:640
  581.4 86.4 %all-gather.32.cloned.1.call-start = ((), (), s32[]{:S(2)}) async-start(), calls=%async_computation.11 | async-start | bytes 1327104 | tf_op jit(solution)/shard_map/all_gather | solution.py:640
  606.1 38.3 %collective-permute-start.83 = (bf16[1024,1024]{1,0:T(8,128)(2,1)S(1)}, bf16[1024,1024]{1,0:T(8,128)(2,1)}, u32[]{:S(2)}, u32[]{:S(2)}) collective-permute-start(bf16[1024,1024]{1,0:T(8,128)(2,1)S(1)} %select_select_fusion.1), channel_id=1, source_target_pairs={{8,9},{9,10},{10,11},{11,8},{0,1},{1,2},{2,3},{3,0}} | collective-permute-start | bytes 6291464 | tf_op jit(solution)/shard_map/ppermute | solution.py:266
  609.2 28.1 %collective-permute-start.80 = (bf16[32,2176]{1,0:T(8,128)(2,1)S(1)}, bf16[32,2176]{1,0:T(8,128)(2,1)S(1)}, u32[]{:S(2)}, u32[]{:S(2)}) collective-permute-start(bf16[32,2176]{1,0:T(8,128)(2,1)S(1)} %get-tuple-element.572), channel_id=1, source_target_pairs={{0,3},{1,0},{2,1},{3,2},{4,7},{5,4},{6,5},{7,6},{8,11},{9,8},{10,9... | collective-permute-start | bytes 417800 | tf_op jit(solution)/shard_map/ppermute | solution.py:64
  613.0 28.8 %collective-permute-start.81 = (bf16[32,2176]{1,0:T(8,128)(2,1)S(1)}, bf16[32,2176]{1,0:T(8,128)(2,1)S(1)}, u32[]{:S(2)}, u32[]{:S(2)}) collective-permute-start(bf16[32,2176]{1,0:T(8,128)(2,1)S(1)} %get-tuple-element.573), channel_id=1, source_target_pairs={{0,2},{1,3},{2,0},{3,1},{4,6},{5,7},{6,4},{7,5},{8,10},{9,11},{10,... | collective-permute-start | bytes 417800 | tf_op jit(solution)/shard_map/ppermute | solution.py:64
  644.3 290.8 %all-gather.30.cloned.1.call-start = ((), (), s32[]{:S(2)}) async-start(), calls=%async_computation.10 | async-start | bytes 11796480 | tf_op jit(solution)/shard_map/all_gather | solution.py:845
  644.4 30.0 %collective-permute-start.84 = (bf16[1024,1024]{1,0:T(8,128)(2,1)}, bf16[1024,1024]{1,0:T(8,128)(2,1)}, u32[]{:S(2)}, u32[]{:S(2)}) collective-permute-start(bf16[1024,1024]{1,0:T(8,128)(2,1)} %collective-permute-done.83), channel_id=1, source_target_pairs={{8,9},{9,10},{10,11},{11,8},{0,1},{1,2},{2,3},{3,0}} | collective-permute-start | bytes 6291464 | tf_op jit(solution)/shard_map/ppermute | solution.py:266
  674.4 40.0 %collective-permute-start.85 = (bf16[1024,1024]{1,0:T(8,128)(2,1)}, bf16[1024,1024]{1,0:T(8,128)(2,1)}, u32[]{:S(2)}, u32[]{:S(2)}) collective-permute-start(bf16[1024,1024]{1,0:T(8,128)(2,1)} %collective-permute-done.84), channel_id=1, source_target_pairs={{8,9},{9,10},{10,11},{11,8},{0,1},{1,2},{2,3},{3,0}} | collective-permute-start | bytes 6291464 | tf_op jit(solution)/shard_map/ppermute | solution.py:266
  844.3 52.3 %collective-permute-start.43 = (bf16[512,1024]{1,0:T(8,128)(2,1)}, bf16[512,1024]{1,0:T(8,128)(2,1)}, u32[]{:S(2)}, u32[]{:S(2)}) collective-permute-start(bf16[512,1024]{1,0:T(8,128)(2,1)} %slice.867), channel_id=1, source_target_pairs={{1,0},{3,2},{5,4},{7,6},{9,8},{11,10},{13,12},{15,14},{17,16},{19,... | collective-permute-start | bytes 3145736 | tf_op jit(solution)/shard_map/ppermute | solution.py:709
  (237 other events, 2874.7 us)
Sparse Core Ops, SparseCore 0:
  61.3 60.4 all-gather.17
  142.3 80.6 all-gather.19
  293.8 83.5 reduce-scatter.2
  381.0 75.8 reduce-scatter.4
  458.7 27.8 all-gather.21
  488.4 34.8 all-gather.23
  545.2 23.3 all-gather.27
  581.5 29.5 all-gather.25
  644.4 23.3 all-gather.31
  839.1 61.1 all-gather.29

commit v4 on v3

--- a/solution.py
+++ b/solution.py
@@ -270,12 +270,11 @@
 
 def summed_small(x):
     count, mine, dp = lax.axis_size("seq"), lax.axis_index("seq"), lax.axis_size("dp")
-    share = x.shape[0] // count
-    held = x.reshape(count, share, x.shape[1])
-    total = lax.dynamic_index_in_dim(held, mine, 0, keepdims=False)
+    share = x.shape[1] // count
+    total = lax.dynamic_slice_in_dim(x, mine * share, share, 1)
     for k in range(1, count):
-        piece = lax.dynamic_index_in_dim(held, lax.rem(mine + k, count), 0, keepdims=False)
-        total = total + turned(piece, k)
+        there = lax.rem(mine + k, count)
+        total = total + turned(lax.dynamic_slice_in_dim(x, there * share, share, 1), k)
     step = 1
     while step < dp:
         total = total + lax.ppermute(total, "dp", [(i, i ^ step) for i in range(dp)])
@@ -865,29 +864,27 @@
     d_input_norm, d_gain_one = norm_back_one(d_normed + d_normed_ema + omega * d_ema)
     tokens_grad = tokens_grad + d_input_norm
 
-    grad_channel = jnp.concatenate(
-        [
-            d_gain_one[:, None],
-            d_gain_two[:, None],
-            d_omega[:, None],
-            d_alpha.T,
-            d_delta.T,
-            d_beta.T,
-            d_eta.T,
-        ],
-        axis=1,
-    )
-    grad_query = jnp.stack([d_scale_q, d_shift_q, d_scale_k], axis=1)
     query_rows = Z // seq_count
-    channel_rows = D // seq_count
-    grad_query = jnp.pad(
-        grad_query.reshape(seq_count, query_rows, 3),
-        ((0, 0), (0, channel_rows - query_rows), (0, 0)),
-    ).reshape(D, 3)
-    small_sum = summed_small(jnp.concatenate([grad_channel, grad_query], axis=1))
+    grad_query = jnp.stack([d_scale_q, d_shift_q, d_scale_k]).reshape(3, seq_count, query_rows)
+    grad_query = jnp.pad(grad_query, ((0, 0), (0, 0), (0, D // seq_count - query_rows)))
+    small_sum = summed_small(
+        jnp.concatenate(
+            [
+                d_gain_one[None],
+                d_gain_two[None],
+                d_omega[None],
+                d_alpha,
+                d_delta,
+                d_beta,
+                d_eta,
+                grad_query.reshape(3, D),
+            ],
+            axis=0,
+        )
+    )
     columns = channel_params.shape[1]
-    channel_renewed = MOMENTUM * channel_moment + small_sum[:, :columns]
-    query_renewed = MOMENTUM * query_moment + small_sum[:query_rows, columns:]
+    channel_renewed = MOMENTUM * channel_moment + small_sum[:columns].T
+    query_renewed = MOMENTUM * query_moment + small_sum[columns:, :query_rows].T
     squares = jnp.concatenate(
         [
             jnp.sum(channel_renewed * channel_renewed, axis=0),

time: 973 us -> 972 us (level)
  no operation moved by 1% of the time
where the time goes in v4:
time: 972 us; the launch traced here: 963 us
  waiting for transfers between devices  336 us (35%)
  matrix products  159 us (16%)
  starting transfers between devices  156 us (16%)
  Pallas kernels  118 us (12%)
  other arithmetic  116 us (12%)
  local copies, waits for them, and re-layouts  60 us (6%)
  between operations  17.8 us (2%)
    ppermute x42, waiting for transfers between devices, turned(): lax.ppermute(x, 'seq', [(i, (i + distance) % count) for i in range(count)])  129 us
    ppermute x38, waiting for transfers between devices, across(): lax.ppermute(x, 'dp', [(i, i ^ bit) for i in range(lax.axis_size('dp'))])  107 us
    pallas_call x1, Pallas kernels, orthogonal_factor(): pl.pallas_call(factor_kernel, out_shape=(jax.ShapeDtypeStruct(gram.shape,...  91.7 us
    ppermute x42, starting transfers between devices, turned(): lax.ppermute(x, 'seq', [(i, (i + distance) % count) for i in range(count)])  66.9 us
    dot_general x10, matrix products, times_left(): lax.dot_general(left, right, (((0,), (0,)), ((), ())), preferred_element_...  56.7 us
    dot_general x12, matrix products, times_plain(): return jnp.dot(left, right, preferred_element_type=jnp.float32)  53.9 us
    reduce_scatter x2, waiting for transfers between devices, far_sum(): lax.psum_scatter(grad, 'dp', scatter_dimension=0, tiled=True)  50.4 us
    dot_general x9, matrix products, times_right(): lax.dot_general(left, right, (((1,), (1,)), ((), ())), preferred_element_...  48 us
  transfers between devices with their start and end apart: 115, of which 44 were waited for; matrix products, arithmetic and copies ran while one was open for 26% of the time, Pallas kernels for 3%

profile of v4, /device:TPU:0, one launch (start us, length us, event | category | flops | bytes accessed | tf_op | source)
XLA Modules:
  0.0 963.0 jit_solution(2300422369762345597)
XLA Ops:
  15.6 11.4 %collective-permute-done.38 = bf16[256,1024]{1,0:T(8,128)(2,1)S(1)} collective-permute-done((bf16[256,1024]{1,0:T(8,128)(2,1)S(1)}, bf16[256,1024]{1,0:T(8,128)(2,1)S(1)}, u32[]{:S(2)}, u32[]{:S(2)}) %collective-permute-start.38) | collective-permute-done | bytes 524320 | tf_op jit(solution)/shard_map/ppermute | solution.py:64
  27.0 32.4 %collective-permute-done.37 = bf16[256,1024]{1,0:T(8,128)(2,1)S(1)} collective-permute-done((bf16[256,1024]{1,0:T(8,128)(2,1)S(1)}, bf16[256,1024]{1,0:T(8,128)(2,1)S(1)}, u32[]{:S(2)}, u32[]{:S(2)}) %collective-permute-start.37) | collective-permute-done | bytes 524320 | tf_op jit(solution)/shard_map/ppermute | solution.py:64
  156.7 8.5 collective-permute-done.22
  165.2 10.9 %collective-permute-done.21 = bf16[2,4,32,1152]{3,2,0,1:T(8,128)(2,1)} collective-permute-done((bf16[2,4,32,1152]{3,2,0,1:T(8,128)(2,1)}, bf16[2,4,32,1152]{3,2,0,1:T(8,128)(2,1)}, u32[]{:S(2)}, u32[]{:S(2)}) %collective-permute-start.21) | collective-permute-done | bytes 589856 | tf_op jit(solution)/shard_map/ppermute | solution.py:87
  183.6 28.0 %collective-permute-done.31 = bf16[2,4,2,32,1024]{4,3,2,1,0:T(8,128)(2,1)S(1)} collective-permute-done((bf16[2,4,2,32,1024]{4,3,2,1,0:T(8,128)(2,1)S(1)}, bf16[2,4,2,32,1024]{4,3,2,1,0:T(8,128)(2,1)S(1)}, u32[]{:S(2)}, u32[]{:S(2)}) %collective-permute-start.31) | collective-permute-done | bytes 1048608 | tf_op jit(solution)/shard_map/ppermute | solution.py:87
  230.6 8.4 multiply_convert_fusion.3
  246.6 9.9 %multiply_convert_fusion.6 = (bf16[512,2048]{1,0:T(8,128)(2,1)S(1)}, f32[512,2048]{1,0:T(8,128)}) fusion(f32[512,2048]{1,0:T(8,128)} %fusion.78, bf16[512,1024]{1,0:T(8,128)(2,1)S(1)} %copy-done.79, bf16[2048,1024]{1,0:T(8,128)(2,1)S(1)} %bitcast.491), kind=kOutput, calls=%fused_computation.55 | convolution fusion | flops 2153775104 | bytes 15728640 | tf_op jit(solution)/shard_map/dot_general | solution.py:40
  264.0 7.7 fusion.157
  275.0 7.0 convolution_convert_fusion.1
  282.0 11.6 %convolution_add_fusion = f32[512,1024]{1,0:T(8,128)} fusion(f32[512,1024]{1,0:T(8,128)S(1)} %get-tuple-element.504, bf16[4096,1024]{1,0:T(8,128)(2,1)} %bitcast.559, f32[512,4096]{1,0:T(8,128)} %copy-done.144), kind=kOutput, calls=%fused_computation.135 | convolution fusion | flops 4305977344 | bytes 20971520 | tf_op jit(solution)/shard_map/dot_general | solution.py:36
  293.7 9.8 %multiply_convert_fusion.1 = bf16[512,4096]{1,0:T(8,128)(2,1)S(1)} fusion(f32[512,4096]{1,0:T(8,128)} %copy-done.144, bf16[512,1024]{1,0:T(8,128)(2,1)} %fusion.60, bf16[4096,1024]{1,0:T(8,128)(2,1)} %bitcast.560), kind=kOutput, calls=%fused_computation.39 | convolution fusion | flops 4313841664 | bytes 22020096 | tf_op jit(solution)/shard_map/dot_general | solution.py:40
  305.6 7.4 convolution_convert_fusion
  313.0 10.1 %multiply_reduce_fusion = (f32[1024]{0:T(1024)}, f32[512]{0:T(512)S(1)}, f32[512,1024]{1,0:T(8,128)S(1)}) fusion(f32[512,1024]{1,0:T(8,128)S(1)} %get-tuple-element.504, f32[512]{0:T(512)S(1)} %fusion.149, f32[512]{0:T(512)S(1)} %broadcast_multiply_fusion, f32[1024]{0:T(1024)S(1)} %bitcast.554, bf16[512,4096]{1,0:T(8,128)(2,1)} %copy-done.150, ...), kind=kOutput, calls=%fused_computation.104 | convolution fusion | flops 4298635776 | bytes 16791552 | tf_op jit(solution)/shard_map/dot_general | solution.py:36
  357.6 6.9 multiply_convert_fusion
  364.5 12.8 %reduce-scatter.3.cloned.1.call-done = bf16[512,1024]{1,0:T(8,128)(2,1)} async-done(((bf16[4096,1024]{1,0:T(8,128)(2,1)}), bf16[512,1024]{1,0:T(8,128)(2,1)}) %reduce-scatter.3.cloned.1.call-update) | async-done | bytes 1048592 | tf_op jit(solution)/shard_map/reduce_scatter | solution.py:200
  380.1 7.6 convolution_convert_fusion.5
  406.4 10.9 %collective-permute-done.46 = bf16[128,1024]{1,0:T(8,128)(2,1)S(1)} collective-permute-done((bf16[128,1024]{1,0:T(8,128)(2,1)S(1)}, bf16[128,1024]{1,0:T(8,128)(2,1)S(1)}, u32[]{:S(2)}, u32[]{:S(2)}) %collective-permute-start.46) | collective-permute-done | bytes 262176 | tf_op jit(solution)/shard_map/ppermute | solution.py:64
  419.4 37.6 %reduce-scatter.5.cloned.1.call-done = bf16[512,1024]{1,0:T(8,128)(2,1)} async-done(((bf16[4096,1024]{1,0:T(8,128)(2,1)}), bf16[512,1024]{1,0:T(8,128)(2,1)}) %reduce-scatter.5.cloned.1.call-update) | async-done | bytes 1048592 | tf_op jit(solution)/shard_map/reduce_scatter | solution.py:200
  469.4 15.7 %collective-permute-done.56 = bf16[128,1024]{1,0:T(8,128)(2,1)} collective-permute-done((bf16[128,1024]{1,0:T(8,128)(2,1)}, bf16[128,1024]{1,0:T(8,128)(2,1)}, u32[]{:S(2)}, u32[]{:S(2)}) %collective-permute-start.56) | collective-permute-done | bytes 262176 | tf_op jit(solution)/shard_map/ppermute | solution.py:64
  515.0 8.1 collective-permute-done.60
  550.1 8.1 collective-permute-done.53
  566.0 7.1 collective-permute-done.71
  581.4 12.4 %collective-permute-done.74 = bf16[2,4,32,1024]{3,2,1,0:T(8,128)(2,1)} collective-permute-done((bf16[2,4,32,1024]{3,2,1,0:T(8,128)(2,1)}, bf16[2,4,32,1024]{3,2,1,0:T(8,128)(2,1)}, u32[]{:S(2)}, u32[]{:S(2)}) %collective-permute-start.74) | collective-permute-done | bytes 524320 | tf_op jit(solution)/shard_map/ppermute | solution.py:87
  614.9 22.4 %collective-permute-done.80 = bf16[32,2176]{1,0:T(8,128)(2,1)S(1)} collective-permute-done((bf16[32,2176]{1,0:T(8,128)(2,1)S(1)}, bf16[32,2176]{1,0:T(8,128)(2,1)S(1)}, u32[]{:S(2)}, u32[]{:S(2)}) %collective-permute-start.80) | collective-permute-done | bytes 139296 | tf_op jit(solution)/shard_map/ppermute | solution.py:64
  656.4 11.3 %all-gather.32.cloned.1.call-done = bf16[8,68,1024]{2,1,0:T(8,128)(2,1)} async-done(((bf16[1,68,1024]{2,1,0:T(8,128)(2,1)}), bf16[8,68,1024]{2,1,0:T(8,128)(2,1)}) %all-gather.32.cloned.1.call-update) | async-done | bytes 1114128 | tf_op jit(solution)/shard_map/all_gather | solution.py:639
  688.4 26.0 %collective-permute-done.85 = bf16[1024,1024]{1,0:T(8,128)(2,1)} collective-permute-done((bf16[1024,1024]{1,0:T(8,128)(2,1)}, bf16[1024,1024]{1,0:T(8,128)(2,1)}, u32[]{:S(2)}, u32[]{:S(2)}) %collective-permute-start.85) | collective-permute-done | bytes 2097184 | tf_op jit(solution)/shard_map/ppermute | solution.py:266
  714.3 17.2 %conditional.1 = (f32[1024,1024]{1,0:T(8,128)}) conditional(s32[]{:T(128)} %clamp.3, (bf16[1024,1024]{1,0:T(8,128)(2,1)}, bf16[1024,1024]{1,0:T(8,128)(2,1)}, bf16[1024,1024]{1,0:T(8,128)(2,1)}, bf16[1024,1024]{1,0:T(8,128)(2,1)}) %tuple.400, (bf16[512,1024]{1,0:T(8,128)(2,1)}, bf16[512,1024]{1,0:T(8,128)(2,1)}, ...), branch_computations={%region_11.12_spmd, %region_12.13_spmd, %region_13.14_spmd, %regio... | conditional | flops 8623489024 | bytes 12582920 | solution.py:820
  714.3 16.8 %fusion = f32[1024,1024]{1,0:T(8,128)} fusion(bf16[1024,1024]{1,0:T(8,128)(2,1)} %get-tuple-element.40, bf16[1024,1024]{1,0:T(8,128)(2,1)} %get-tuple-element.34, bf16[1024,1024]{1,0:T(8,128)(2,1)} %get-tuple-element.33, bf16[1024,1024]{1,0:T(8,128)(2,1)} %get-tuple-element.32), kind=kOutput, calls=%fused_computation | convolution fusion | flops 8623489024 | bytes 12582912 | tf_op jit(solution)/shard_map/cond/branch_0_fun/dot_general | solution.py:46
  731.5 91.7 %shard_map.394 = (bf16[1024,1024]{1,0:T(8,128)(2,1)}, bf16[1024,1024]{1,0:T(8,128)(2,1)}) custom-call(f32[1024,1024]{1,0:T(8,128)} %get-tuple-element.649.gram_ref), custom_call_target="tpu_custom_call" | custom-call | flops 73014444032 | bytes 8388608 | tf_op jit(solution)/shard_map/pallas_call | solution.py:479
  855.1 14.6 %shard_map.392 = (f32[16,8,128]{2,1,0:T(8,128)S(1)}, f32[16,8,128]{2,1,0:T(8,128)S(1)}, f32[16,8,128]{2,1,0:T(8,128)S(1)}, f32[16,8,128]{2,1,0:T(8,128)S(1)}) custom-call(f32[512,8,128]{2,1,0:T(8,128)S(1)} %bitcast.452, f32[512,8,128]{2,1,0:T(8,128)S(1)} %bitcast.453, f32[16,8,128]{2,1,0:T(8,128)S(1)} %bitcast.460, f32[16,8,128]{2,1,0:T(8,128)S(1)} %copy-done.7), custom_call_target="tpu_custom_call" | custom-call | flops 83886080 | bytes 4194304 | tf_op jit(solution)/shard_map/pallas_call | solution.py:364
  935.8 7.5 bitcast_subtract_fusion.1
  946.9 9.1 bitcast_subtract_fusion
  (745 shorter events, 455.0 us)
Async XLA Ops:
  7.2 256.8 %all-gather.18.cloned.1.call-start = ((), (), s32[]{:S(2)}) async-start(), calls=%async_computation.4 | async-start | bytes 9437184 | tf_op jit(solution)/shard_map/all_gather | solution.py:195
  14.6 44.8 %collective-permute-start.37 = (bf16[256,1024]{1,0:T(8,128)(2,1)S(1)}, bf16[256,1024]{1,0:T(8,128)(2,1)S(1)}, u32[]{:S(2)}, u32[]{:S(2)}) collective-permute-start(bf16[256,1024]{1,0:T(8,128)(2,1)S(1)} %get-tuple-element.584), channel_id=1, source_target_pairs={{0,2},{1,3},{2,0},{3,1},{4,6},{5,7},{6,4},{7,5},{8,10},{9,11},{10,... | collective-permute-start | bytes 1572872 | tf_op jit(solution)/shard_map/ppermute | solution.py:64
  14.6 44.8 %collective-permute-start.36 = (bf16[256,1024]{1,0:T(8,128)(2,1)S(1)}, bf16[256,1024]{1,0:T(8,128)(2,1)S(1)}, u32[]{:S(2)}, u32[]{:S(2)}) collective-permute-start(bf16[256,1024]{1,0:T(8,128)(2,1)S(1)} %get-tuple-element.584), channel_id=1, source_target_pairs={{0,1},{1,2},{2,3},{3,0},{4,5},{5,6},{6,7},{7,4},{8,9},{9,10},{10,1... | collective-permute-start | bytes 1572872 | tf_op jit(solution)/shard_map/ppermute | solution.py:64
  61.2 220.8 %all-gather.20.cloned.1.call-start = ((), (), s32[]{:S(2)}) async-start(), calls=%async_computation.5 | async-start | bytes 9437184 | tf_op jit(solution)/shard_map/all_gather | solution.py:195
  133.6 42.4 %collective-permute-start.21 = (bf16[2,4,32,1152]{3,2,0,1:T(8,128)(2,1)}, bf16[2,4,32,1152]{3,2,0,1:T(8,128)(2,1)}, u32[]{:S(2)}, u32[]{:S(2)}) collective-permute-start(bf16[2,4,32,1152]{3,2,0,1:T(8,128)(2,1)} %pad_maximum_fusion.14), channel_id=1, source_target_pairs={{0,8},{4,12},{8,0},{12,4},{16,24},{20,28},{24,16},{28,20},{1,9},{5... | collective-permute-start | bytes 1769480 | tf_op jit(solution)/shard_map/ppermute | solution.py:87
  142.2 235.2 %reduce-scatter.3.cloned.1.call-start = ((), (), s32[]{:S(2)}) async-start(), calls=%async_computation.2 | async-start | bytes 9437184 | tf_op jit(solution)/shard_map/reduce_scatter | solution.py:200
  142.4 39.5 %collective-permute-start.34 = (bf16[512,1024]{1,0:T(8,128)(2,1)S(1)}, bf16[512,1024]{1,0:T(8,128)(2,1)S(1)}, u32[]{:S(2)}, u32[]{:S(2)}) collective-permute-start(bf16[512,1024]{1,0:T(8,128)(2,1)S(1)} %get-tuple-element.557), channel_id=1, source_target_pairs={{0,1},{2,3},{4,5},{6,7},{8,9},{10,11},{12,13},{14,15},{16,17},{18,... | collective-permute-start | bytes 3145736 | tf_op jit(solution)/shard_map/ppermute | solution.py:557
  153.7 57.9 %collective-permute-start.31 = (bf16[2,4,2,32,1024]{4,3,2,1,0:T(8,128)(2,1)S(1)}, bf16[2,4,2,32,1024]{4,3,2,1,0:T(8,128)(2,1)S(1)}, u32[]{:S(2)}, u32[]{:S(2)}) collective-permute-start(bf16[2,4,2,32,1024]{4,3,2,1,0:T(8,128)(2,1)S(1)} %pad_maximum_fusion.12), channel_id=1, source_target_pairs={{0,8},{4,12},{8,0},{12,4},{16,24},{20,28},{24,16},{28,20},{1,9},{5... | collective-permute-start | bytes 3145736 | tf_op jit(solution)/shard_map/ppermute | solution.py:87
  155.2 56.4 %collective-permute-start.32 = (bf16[2,4,2,32,1024]{4,3,2,1,0:T(8,128)(2,1)S(1)}, bf16[2,4,2,32,1024]{4,3,2,1,0:T(8,128)(2,1)S(1)}, u32[]{:S(2)}, u32[]{:S(2)}) collective-permute-start(bf16[2,4,2,32,1024]{4,3,2,1,0:T(8,128)(2,1)S(1)} %pad_maximum_fusion.13), channel_id=1, source_target_pairs={{0,16},{4,20},{8,24},{12,28},{16,0},{20,4},{24,8},{28,12},{1,17},{... | collective-permute-start | bytes 3145736 | tf_op jit(solution)/shard_map/ppermute | solution.py:87
  177.4 36.3 %collective-permute-start.23 = (bf16[2,2,4,32,1152]{4,3,0,1,2:T(8,128)(2,1)S(1)}, bf16[2,2,4,32,1152]{4,3,0,1,2:T(8,128)(2,1)S(1)}, u32[]{:S(2)}, u32[]{:S(2)}) collective-permute-start(bf16[2,2,4,32,1152]{4,3,0,1,2:T(8,128)(2,1)S(1)} %pad_maximum_fusion.8), channel_id=1, source_target_pairs={{0,4},{4,0},{8,12},{12,8},{16,20},{20,16},{24,28},{28,24},{1,5},{5... | collective-permute-start | bytes 3538952 | tf_op jit(solution)/shard_map/ppermute | solution.py:87
  178.8 34.9 %collective-permute-start.24 = (bf16[2,2,4,32,1024]{4,3,1,0,2:T(8,128)(2,1)S(1)}, bf16[2,2,4,32,1024]{4,3,1,0,2:T(8,128)(2,1)S(1)}, u32[]{:S(2)}, u32[]{:S(2)}) collective-permute-start(bf16[2,2,4,32,1024]{4,3,1,0,2:T(8,128)(2,1)S(1)} %pad_maximum_fusion.10), channel_id=1, source_target_pairs={{0,4},{4,0},{8,12},{12,8},{16,20},{20,16},{24,28},{28,24},{1,5},{5... | collective-permute-start | bytes 3145736 | tf_op jit(solution)/shard_map/ppermute | solution.py:87
  181.9 44.9 %collective-permute-start.35 = (bf16[2,4,4,1,32,1024]{5,4,2,1,0,3:T(8,128)(2,1)S(1)}, bf16[2,4,4,1,32,1024]{5,4,2,1,0,3:T(8,128)(2,1)S(1)}, u32[]{:S(2)}, u32[]{:S(2)}) collective-permute-start(bf16[2,4,4,1,32,1024]{5,4,2,1,0,3:T(8,128)(2,1)S(1)} %get-tuple-element.549), channel_id=1, source_target_pairs={{0,4},{4,0},{8,12},{12,8},{16,20},{20,16},{24,28},{28,24},{1,5},{5... | collective-permute-start | bytes 6291464 | tf_op jit(solution)/shard_map/ppermute | solution.py:87
  213.6 32.2 %collective-permute-start.33 = (bf16[2,4,4,2,32,1024]{5,4,3,2,1,0:T(8,128)(2,1)S(1)}, bf16[2,4,4,2,32,1024]{5,4,3,2,1,0:T(8,128)(2,1)S(1)}, u32[]{:S(2)}, u32[]{:S(2)}) collective-permute-start(bf16[2,4,4,2,32,1024]{5,4,3,2,1,0:T(8,128)(2,1)S(1)} %get-tuple-element.532), channel_id=1, source_target_pairs={{0,4},{4,0},{8,12},{12,8},{16,20},{20,16},{24,28},{28,24},{1,5},{5... | collective-permute-start | bytes 12582920 | tf_op jit(solution)/shard_map/ppermute | solution.py:87
  293.7 163.3 %reduce-scatter.5.cloned.1.call-start = ((), (), s32[]{:S(2)}) async-start(), calls=%async_computation.3 | async-start | bytes 9437184 | tf_op jit(solution)/shard_map/reduce_scatter | solution.py:200
  325.5 278.7 %all-gather.22.cloned.1.call-start = ((), (), s32[]{:S(2)}) async-start(), calls=%async_computation.6 | async-start | bytes 2359296 | tf_op jit(solution)/shard_map/all_gather | solution.py:639
  347.1 30.2 %collective-permute-start.41 = (bf16[256,1024]{1,0:T(8,128)(2,1)S(1)}, bf16[256,1024]{1,0:T(8,128)(2,1)}, u32[]{:S(2)}, u32[]{:S(2)}) collective-permute-start(bf16[256,1024]{1,0:T(8,128)(2,1)S(1)} %get-tuple-element.529), channel_id=1, source_target_pairs={{0,8},{4,12},{8,0},{12,4},{16,24},{20,28},{24,16},{28,20},{1,9},{5... | collective-permute-start | bytes 1572872 | tf_op jit(solution)/shard_map/ppermute | solution.py:87
  349.2 28.1 %collective-permute-start.42 = (bf16[256,1024]{1,0:T(8,128)(2,1)S(1)}, bf16[256,1024]{1,0:T(8,128)(2,1)}, u32[]{:S(2)}, u32[]{:S(2)}) collective-permute-start(bf16[256,1024]{1,0:T(8,128)(2,1)S(1)} %get-tuple-element.528), channel_id=1, source_target_pairs={{0,16},{4,20},{8,24},{12,28},{16,0},{20,4},{24,8},{28,12},{1,17},{... | collective-permute-start | bytes 1572872 | tf_op jit(solution)/shard_map/ppermute | solution.py:87
  419.3 184.9 %all-gather.24.cloned.1.call-start = ((), (), s32[]{:S(2)}) async-start(), calls=%async_computation.7 | async-start | bytes 2359296 | tf_op jit(solution)/shard_map/all_gather | solution.py:639
  487.4 158.9 %all-gather.28.cloned.1.call-start = ((), (), s32[]{:S(2)}) async-start(), calls=%async_computation.9 | async-start | bytes 1179648 | tf_op jit(solution)/shard_map/all_gather | solution.py:639
  508.9 34.1 %collective-permute-start.69 = (bf16[64,1024]{1,0:T(8,128)(2,1)S(1)}, bf16[64,1024]{1,0:T(8,128)(2,1)S(1)}, u32[]{:S(2)}, u32[]{:S(2)}) collective-permute-start(bf16[64,1024]{1,0:T(8,128)(2,1)S(1)} %get-tuple-element.578), channel_id=1, source_target_pairs={{0,1},{1,2},{2,3},{3,0},{4,5},{5,6},{6,7},{7,4},{8,9},{9,10},{10,1... | collective-permute-start | bytes 393224 | tf_op jit(solution)/shard_map/ppermute | solution.py:64
  509.8 33.2 %collective-permute-start.68 = (bf16[64,1024]{1,0:T(8,128)(2,1)S(1)}, bf16[64,1024]{1,0:T(8,128)(2,1)S(1)}, u32[]{:S(2)}, u32[]{:S(2)}) collective-permute-start(bf16[64,1024]{1,0:T(8,128)(2,1)S(1)} %get-tuple-element.579), channel_id=1, source_target_pairs={{0,2},{1,3},{2,0},{3,1},{4,6},{5,7},{6,4},{7,5},{8,10},{9,11},{10,... | collective-permute-start | bytes 393224 | tf_op jit(solution)/shard_map/ppermute | solution.py:64
  511.9 31.1 %collective-permute-start.67 = (bf16[64,1024]{1,0:T(8,128)(2,1)S(1)}, bf16[64,1024]{1,0:T(8,128)(2,1)S(1)}, u32[]{:S(2)}, u32[]{:S(2)}) collective-permute-start(bf16[64,1024]{1,0:T(8,128)(2,1)S(1)} %get-tuple-element.577), channel_id=1, source_target_pairs={{0,3},{1,0},{2,1},{3,2},{4,7},{5,4},{6,5},{7,6},{8,11},{9,8},{10,9... | collective-permute-start | bytes 393224 | tf_op jit(solution)/shard_map/ppermute | solution.py:64
  539.1 34.0 %collective-permute-start.51 = (bf16[4,4,32,1152]{3,2,0,1:T(8,128)(2,1)}, bf16[4,4,32,1152]{3,2,0,1:T(8,128)(2,1)}, u32[]{:S(2)}, u32[]{:S(2)}) collective-permute-start(bf16[4,4,32,1152]{3,2,0,1:T(8,128)(2,1)} %get-tuple-element.537), channel_id=1, source_target_pairs={{0,4},{4,0},{8,12},{12,8},{16,20},{20,16},{24,28},{28,24},{1,5},{5... | collective-permute-start | bytes 3538952 | tf_op jit(solution)/shard_map/ppermute | solution.py:87
  545.0 104.0 %all-gather.26.cloned.1.call-start = ((), (), s32[]{:S(2)}) async-start(), calls=%async_computation.8 | async-start | bytes 2359296 | tf_op jit(solution)/shard_map/all_gather | solution.py:639
  581.4 86.3 %all-gather.32.cloned.1.call-start = ((), (), s32[]{:S(2)}) async-start(), calls=%async_computation.11 | async-start | bytes 1327104 | tf_op jit(solution)/shard_map/all_gather | solution.py:639
  606.1 38.3 %collective-permute-start.83 = (bf16[1024,1024]{1,0:T(8,128)(2,1)S(1)}, bf16[1024,1024]{1,0:T(8,128)(2,1)}, u32[]{:S(2)}, u32[]{:S(2)}) collective-permute-start(bf16[1024,1024]{1,0:T(8,128)(2,1)S(1)} %select_select_fusion.1), channel_id=1, source_target_pairs={{8,9},{9,10},{10,11},{11,8},{0,1},{1,2},{2,3},{3,0}} | collective-permute-start | bytes 6291464 | tf_op jit(solution)/shard_map/ppermute | solution.py:266
  609.1 28.1 %collective-permute-start.80 = (bf16[32,2176]{1,0:T(8,128)(2,1)S(1)}, bf16[32,2176]{1,0:T(8,128)(2,1)S(1)}, u32[]{:S(2)}, u32[]{:S(2)}) collective-permute-start(bf16[32,2176]{1,0:T(8,128)(2,1)S(1)} %get-tuple-element.572), channel_id=1, source_target_pairs={{0,3},{1,0},{2,1},{3,2},{4,7},{5,4},{6,5},{7,6},{8,11},{9,8},{10,9... | collective-permute-start | bytes 417800 | tf_op jit(solution)/shard_map/ppermute | solution.py:64
  613.0 28.8 %collective-permute-start.81 = (bf16[32,2176]{1,0:T(8,128)(2,1)S(1)}, bf16[32,2176]{1,0:T(8,128)(2,1)S(1)}, u32[]{:S(2)}, u32[]{:S(2)}) collective-permute-start(bf16[32,2176]{1,0:T(8,128)(2,1)S(1)} %get-tuple-element.573), channel_id=1, source_target_pairs={{0,2},{1,3},{2,0},{3,1},{4,6},{5,7},{6,4},{7,5},{8,10},{9,11},{10,... | collective-permute-start | bytes 417800 | tf_op jit(solution)/shard_map/ppermute | solution.py:64
  644.3 290.0 %all-gather.30.cloned.1.call-start = ((), (), s32[]{:S(2)}) async-start(), calls=%async_computation.10 | async-start | bytes 11796480 | tf_op jit(solution)/shard_map/all_gather | solution.py:844
  644.4 30.0 %collective-permute-start.84 = (bf16[1024,1024]{1,0:T(8,128)(2,1)}, bf16[1024,1024]{1,0:T(8,128)(2,1)}, u32[]{:S(2)}, u32[]{:S(2)}) collective-permute-start(bf16[1024,1024]{1,0:T(8,128)(2,1)} %collective-permute-done.83), channel_id=1, source_target_pairs={{8,9},{9,10},{10,11},{11,8},{0,1},{1,2},{2,3},{3,0}} | collective-permute-start | bytes 6291464 | tf_op jit(solution)/shard_map/ppermute | solution.py:266
  674.4 40.0 %collective-permute-start.85 = (bf16[1024,1024]{1,0:T(8,128)(2,1)}, bf16[1024,1024]{1,0:T(8,128)(2,1)}, u32[]{:S(2)}, u32[]{:S(2)}) collective-permute-start(bf16[1024,1024]{1,0:T(8,128)(2,1)} %collective-permute-done.84), channel_id=1, source_target_pairs={{8,9},{9,10},{10,11},{11,8},{0,1},{1,2},{2,3},{3,0}} | collective-permute-start | bytes 6291464 | tf_op jit(solution)/shard_map/ppermute | solution.py:266
  844.2 51.7 %collective-permute-start.43 = (bf16[512,1024]{1,0:T(8,128)(2,1)}, bf16[512,1024]{1,0:T(8,128)(2,1)}, u32[]{:S(2)}, u32[]{:S(2)}) collective-permute-start(bf16[512,1024]{1,0:T(8,128)(2,1)} %slice.871), channel_id=1, source_target_pairs={{1,0},{3,2},{5,4},{7,6},{9,8},{11,10},{13,12},{15,14},{17,16},{19,... | collective-permute-start | bytes 3145736 | tf_op jit(solution)/shard_map/ppermute | solution.py:708
  (237 other events, 2874.3 us)
Sparse Core Ops, SparseCore 0:
  61.3 60.4 all-gather.17
  142.3 80.6 all-gather.19
  293.8 83.5 reduce-scatter.2
  381.0 75.8 reduce-scatter.4
  458.7 27.8 all-gather.21
  488.4 34.8 all-gather.23
  545.1 23.4 all-gather.27
  581.5 29.5 all-gather.25
  644.4 23.2 all-gather.31
  839.0 61.1 all-gather.29
